TPU v7x, 512 devices: a whole 4x4x16 slice. The times are simulated.
512 devices in a mesh: slab: 64 (over x, z_hi, y, core), off: 8 (over z_lo).
Axes of the slice: x: 4, y: 4, z: 16 (z_hi: 2, z_lo: 8; z = z_hi * 8 + z_lo), core: 2. Of those that a mesh axis runs over, the one named last changes fastest.
Arguments:
- bead_data: bfloat16 [524288, 2, 128], P(('slab', 'off')), may hold values from -6 to 6
- bead_cell: int32 [524288], P(('slab', 'off')), may hold values from 0 to 65535, as said below
- m2l_ops: bfloat16 [128, 128, 128], P('off'), may hold values from -0.0625 to 0.0625
- offsets: int32 [128, 3], P('off'), may hold values from -3 to 2, as said below
Outputs:
- bead_field: float32 [524288], P(('slab', 'off'))
Inputs may be any that keep to these rules, and one draw needn't show every extreme that they name: `bead_cell`: each device's 1024 beads come in 64 blocks of 16; block s lies in slab s, and is made of 8 runs of 2 beads, run r lying in cells s * 1024 + r * 128 to s * 1024 + (r + 1) * 128 - 1. Distinct offsets whose three components lie in -3 to 2 and are not all in -1 to 1.
All inputs are finite; a program needn't handle non-finite values.
Results may differ from a plain program's by a relative error of at most 0.0029.
Values may be sent and summed in bfloat16 or wider, within the bound.
No kernel may reach another device: no remote copies, remote signals or barrier semaphores. Data moves between devices by JAX's collectives and lax.ppermute only.
A program may use at most 64 MiB of HBM per device.

v0:
```python
import jax
import jax.numpy as jnp
from jax import lax
from jax.sharding import PartitionSpec as P

GX = 8
GY = 32
CZS = 4


def padded_2(cells, sides, width):
    for axis, dim in sides:
        count = lax.axis_size(axis)
        ends = count - 1
        head = lax.slice_in_dim(cells, 0, width, axis=dim)
        tail = lax.slice_in_dim(cells, cells.shape[dim] - width, cells.shape[dim], axis=dim)
        cells = jnp.concatenate(
            [
                lax.ppermute(tail, axis, [(i, (i + 1) % count) for i in range(ends)]),
                cells,
                lax.ppermute(head, axis, [((i + 1) % count, i) for i in range(ends)]),
            ],
            axis=dim,
        )
    return cells


def translate_all(multipole, m2l_ops, offsets):
    cells_dev = CZS * GX * GY
    width = multipole.shape[3]
    rimmed = padded_2(multipole, (("slab", 0),), 3)
    padded = jnp.pad(rimmed, ((0, 0), (3, 3), (3, 3), (0, 0)))
    zero = jnp.zeros((), jnp.int32)

    def translate(total, item):
        matrix, shift = item
        starts = (shift[0] + 3, shift[1] + 3, shift[2] + 3, zero)
        window = lax.dynamic_slice(padded, starts, (CZS, GX, GY, width)).reshape(cells_dev, width)
        return (total + jnp.dot(window, matrix, preferred_element_type=jnp.float32), None)

    own_local, _ = lax.scan(
        translate, jnp.zeros((cells_dev, width), jnp.float32), (m2l_ops, offsets)
    )
    return own_local


def body(bead_data, bead_cell, m2l_ops, offsets):
    arrived, cells = (
        lax.all_to_all(bead_data, "slab", split_axis=0, concat_axis=0, tiled=True),
        lax.all_to_all(bead_cell, "slab", split_axis=0, concat_axis=0, tiled=True),
    )
    cells_dev = CZS * GX * GY
    width = bead_data.shape[2]
    local_cell = cells - lax.axis_index("slab") * cells_dev
    moments = arrived[:, 0, :].astype(jnp.float32)
    partial_value = jax.ops.segment_sum(moments, local_cell, num_segments=cells_dev)
    summed = lax.psum(partial_value, "off")
    multipole = summed.astype(jnp.bfloat16).reshape(CZS, GX, GY, width)
    own_local = translate_all(multipole, m2l_ops, offsets)
    local = lax.psum(own_local, "off")
    picked = local[local_cell]
    basis = arrived[:, 1, :].astype(jnp.float32)
    field = jnp.sum(picked * basis, axis=1) * width ** (-0.5)
    return lax.all_to_all(field, "slab", split_axis=0, concat_axis=0, tiled=True)


def solution(mesh):
    in_specs = (
        P(("slab", "off"), None, None),
        P(("slab", "off")),
        P("off", None, None),
        P("off", None),
    )
    out_specs = P(("slab", "off"))
    return jax.shard_map(body, mesh=mesh, in_specs=in_specs, out_specs=out_specs, check_vma=False)
```

profile of v0, /device:TPU:1, one launch (start us, length us, event | category | flops | bytes accessed | tf_op | source)
XLA Modules:
  0.0 429.9 jit_solution(4062004109152879285)
XLA Ops:
  7.3 38.5 %all_to_all.23 = s32[64,16,1]{1,2,0:T(1,128)S(1)} all-to-all(s32[64,16,1]{1,2,0:T(1,128)S(1)} %bitcast.51), channel_id=1, replica_groups=mesh['slab'=64,'off'=8] {'slab'}, dimensions={0} | all-to-all | bytes 8192 | tf_op jit(solution)/shard_map/all_to_all | solution.py:50
  45.8 4.7 %all-to-all-start.1 = ((bf16[1024,2,128]{2,1,0:T(2,128)(2,1)}), bf16[1024,2,128]{2,1,0:T(2,128)(2,1)S(1)}, u32[]{:S(2)}, u32[]{:S(2)}) async-start(bf16[1024,2,128]{2,1,0:T(2,128)(2,1)} %param.6), calls=%async_computation.1 | async-start | bytes 1048576 | tf_op jit(solution)/shard_map/all_to_all | solution.py:49
  51.9 20.3 %all-to-all-done.1 = bf16[1024,2,128]{2,1,0:T(2,128)(2,1)S(1)} async-done(((bf16[1024,2,128]{2,1,0:T(2,128)(2,1)}), bf16[1024,2,128]{2,1,0:T(2,128)(2,1)S(1)}, u32[]{:S(2)}, u32[]{:S(2)}) %all-to-all-start.1) | async-done | bytes 524320 | tf_op jit(solution)/shard_map/all_to_all | solution.py:49
  73.0 6.1 %scatter_custom_fusion = f32[1024,128]{1,0:T(8,128)S(1)} fusion(s32[1024]{0:T(1024)S(1)} %reshape.87, f32[1024,128]{1,0:T(8,128)S(1)} %bitcast.46, f32[]{:T(128)} %constant.59.clone.1), kind=kCustom, calls=%fused_computation.24 | custom fusion | flops 131072 | bytes 524292 | tf_op jit(solution)/shard_map/scatter-add | solution.py:56
  79.1 68.6 %all-reduce.5 = bf16[1024,128]{1,0:T(8,128)(2,1)S(1)} all-reduce(f32[1024,128]{1,0:T(8,128)S(1)} %scatter_custom_fusion), channel_id=1, replica_groups=mesh['slab'=64,'off'=8] {'off'}, use_global_device_ids=true, to_apply=%region_1.0 | all-reduce | flops 131072 | bytes 786432 | tf_op jit(solution)/shard_map/psum | solution.py:57
  147.7 9.4 %collective-permute-start = (bf16[3,8,32,128]{3,2,1,0:T(8,128)(2,1)S(1)}, bf16[3,8,32,128]{3,2,1,0:T(8,128)(2,1)S(1)}, u32[]{:S(2)}, u32[]{:S(2)}) collective-permute-start(bf16[3,8,32,128]{3,2,1,0:T(8,128)(2,1)S(1)} %bitcast.48), channel_id=1, source_target_pairs={{0,8},{8,16},{16,24},{24,32},{32,40},{40,48},{48,56},{56,64},{64,7... | collective-permute-start | bytes 589832 | tf_op jit(solution)/shard_map/ppermute | solution.py:19
  157.1 1.9 collective-permute-start.1
  159.7 4.4 %collective-permute-done.1 = bf16[3,8,32,128]{3,2,1,0:T(8,128)(2,1)S(1)} collective-permute-done((bf16[3,8,32,128]{3,2,1,0:T(8,128)(2,1)S(1)}, bf16[3,8,32,128]{3,2,1,0:T(8,128)(2,1)S(1)}, u32[]{:S(2)}, u32[]{:S(2)}) %collective-permute-start.1) | collective-permute-done | bytes 196640 | tf_op jit(solution)/shard_map/ppermute | solution.py:21
  164.5 90.3 %while.13 = (s32[]{:T(128)}, f32[1024,128]{1,0:T(8,128)S(1)}, s32[16,3]{0,1:T(4,128)S(1)}, bf16[10,14,38,128]{3,2,1,0:T(8,128)(2,1)S(1)}, bf16[16,128,128]{2,1,0...) while((s32[]{:T(128)}, f32[1024,128]{1,0:T(8,128)S(1)}, ...), condition=%wide.region_3.4_spmd.clone, body=%wide.region_2.3_spmd.clone.sunk | while | flops 33816592 | bytes 1868609 | solution.py:41
  169.1 1.0 convolution_add_fusion.2
  174.8 1.0 convolution_add_fusion.2
  180.4 1.0 convolution_add_fusion.2
  186.1 1.0 convolution_add_fusion.2
  191.7 1.0 convolution_add_fusion.2
  197.4 1.0 convolution_add_fusion.2
  208.7 1.0 convolution_add_fusion.2
  214.3 1.0 convolution_add_fusion.2
  220.0 1.0 convolution_add_fusion.2
  231.2 1.0 convolution_add_fusion.2
  242.5 1.0 convolution_add_fusion.2
  253.8 1.0 convolution_add_fusion.2
  255.8 128.6 %all-reduce.4.cloned.1.call-done = f32[1024,128]{1,0:T(8,128)} async-done(((f32[1024,128]{1,0:T(8,128)}), f32[1024,128]{1,0:T(8,128)}) %all-reduce.4.cloned.1.call-update) | async-done | bytes 524304 | tf_op jit(solution)/shard_map/psum | solution.py:60
  384.4 3.8 gather_fusion
  388.6 32.5 %all_to_all.24 = f32[64,16,1]{1,2,0:T(1,128)S(1)} all-to-all(f32[64,16,1]{1,2,0:T(1,128)S(1)} %bitcast.50), channel_id=1, replica_groups=mesh['slab'=64,'off'=8] {'slab'}, dimensions={0} | all-to-all | bytes 8192 | tf_op jit(solution)/shard_map/all_to_all | solution.py:64
  (76 shorter events, 24.0 us)
Async XLA Ops:
  45.8 26.4 %all-to-all-start.1 = ((bf16[1024,2,128]{2,1,0:T(2,128)(2,1)}), bf16[1024,2,128]{2,1,0:T(2,128)(2,1)S(1)}, u32[]{:S(2)}, u32[]{:S(2)}) async-start(bf16[1024,2,128]{2,1,0:T(2,128)(2,1)} %param.6), calls=%async_computation.1 | async-start | bytes 1048576 | tf_op jit(solution)/shard_map/all_to_all | solution.py:49
  50.6 333.9 %all-reduce.4.cloned.1.call-start = ((), (), s32[]{:S(2)}) async-start(), calls=%async_computation.3 | async-start | bytes 1048576 | tf_op jit(solution)/shard_map/psum | solution.py:60
  147.7 16.8 %copy-start.1 = (s32[16,3]{0,1:T(4,128)S(1)}, s32[16,3]{0,1:T(4,128)}, u32[]{:S(2)}) copy-start(s32[16,3]{0,1:T(4,128)} %param.9) | copy-start | bytes 580
  147.7 12.0 %collective-permute-start = (bf16[3,8,32,128]{3,2,1,0:T(8,128)(2,1)S(1)}, bf16[3,8,32,128]{3,2,1,0:T(8,128)(2,1)S(1)}, u32[]{:S(2)}, u32[]{:S(2)}) collective-permute-start(bf16[3,8,32,128]{3,2,1,0:T(8,128)(2,1)S(1)} %bitcast.48), channel_id=1, source_target_pairs={{0,8},{8,16},{16,24},{24,32},{32,40},{40,48},{48,56},{56,64},{64,7... | collective-permute-start | bytes 589832 | tf_op jit(solution)/shard_map/ppermute | solution.py:19
  157.1 7.0 %collective-permute-start.1 = (bf16[3,8,32,128]{3,2,1,0:T(8,128)(2,1)S(1)}, bf16[3,8,32,128]{3,2,1,0:T(8,128)(2,1)S(1)}, u32[]{:S(2)}, u32[]{:S(2)}) collective-permute-start(bf16[3,8,32,128]{3,2,1,0:T(8,128)(2,1)S(1)} %bitcast.47), channel_id=1, source_target_pairs={{8,0},{16,8},{24,16},{32,24},{40,32},{48,40},{56,48},{64,56},{72,6... | collective-permute-start | bytes 589832 | tf_op jit(solution)/shard_map/ppermute | solution.py:21
  254.9 0.8 copy-start
Sparse Core Ops, SparseCore 0:
  255.8 128.5 all-reduce.3
where the time goes:
time: 432 us; the launch traced here: 430 us
  waiting for transfers between devices  154 us (36%)
  blocking collectives  140 us (32%)
  loops' own time  61 us (14%)
  local copies, waits for them, and re-layouts  20.2 us (5%)
  matrix products  16.5 us (4%)
  starting transfers between devices  16.1 us (4%)
  between operations  13.5 us (3%)
  other arithmetic  8.96 us (2%)
    psum x1, waiting for transfers between devices, body(): local = lax.psum(own_local, 'off')  129 us
    psum x1, blocking collectives, body(): summed = lax.psum(partial_value, 'off')  68.6 us
    another operation x1, loops' own time, translate_all(): lax.scan(translate, jnp.zeros((cells_dev, width), jnp.float32), (m2l_ops,...  61 us
    all_to_all x1, blocking collectives, body(): lax.all_to_all(bead_cell, 'slab', split_axis=0, concat_axis=0, tiled=True)  38.5 us
    all_to_all x1, blocking collectives, body(): lax.all_to_all(field, 'slab', split_axis=0, concat_axis=0, tiled=True)  32.5 us
    all_to_all x1, waiting for transfers between devices, body(): lax.all_to_all(bead_data, 'slab', split_axis=0, concat_axis=0, tiled=True)  20.3 us
    dot_general x16, matrix products, translate(): jnp.dot(window, matrix, preferred_element_type=jnp.float32)  16.5 us
    slice x16, local copies, waits for them, and re-layouts, translate(): starts = (shift[0] + 3, shift[1] + 3, shift[2] + 3, zero)  9.67 us
  transfers between devices with their start and end apart: 4, of which 4 were waited for; matrix products, arithmetic and copies ran while one was open for 0% of the time, Pallas kernels for 0%

commit v1 on v0

v1 whole, which is shorter than its diff:
```python
import functools

import jax
import jax.numpy as jnp
import numpy as np
from jax import lax
from jax.experimental import pallas as pl
from jax.experimental.pallas import tpu as pltpu
from jax.sharding import Mesh, PartitionSpec as P

GX = 8
GY = 32
CZS = 4
RUN = 128
BF = jnp.bfloat16
F32 = jnp.float32

OWNERS = ("zh", "zl", "x", "y", "c")
SLABS = ("x", "zh", "zl")
GROUP = ("y", "c")
VMEM = pl.BlockSpec(memory_space=pltpu.VMEM)
SMEM = pl.BlockSpec(memory_space=pltpu.SMEM)


def one_hot(ids):
    lanes = lax.broadcasted_iota(jnp.int32, ids.shape, 1).astype(F32)
    return (ids.astype(F32) == lanes).astype(F32).astype(BF)


def sum_kernel(ids_ref, moments_ref, out_ref):
    cells = lax.dot_general(
        one_hot(ids_ref[...]),
        moments_ref[...],
        (((0,), (0,)), ((), ())),
        preferred_element_type=F32,
    ).astype(BF)
    for peer in range(out_ref.shape[0]):
        out_ref[peer] = cells


def m2l_kernel(offsets_ref, ops_ref, own_ref, low_ref, high_ref, out_ref, rows, shifted):
    shifted[:, :, 0:3] = jnp.zeros((6, 9, 3, GY, 128), BF)
    shifted[:, :, 11:13] = jnp.zeros((6, 9, 2, GY, 128), BF)
    rows[:, 0:8, :] = jnp.zeros((GX, 8, 128), F32)
    rows[:, 40:48, :] = jnp.zeros((GX, 8, 128), F32)
    for plane in range(9):
        ref, at = (low_ref, plane) if plane < 3 else (own_ref, plane - 3) if plane < 7 else (high_ref, plane - 7)
        rows[:, 8:40, :] = ref[at * 256 : (at + 1) * 256, :].astype(F32).reshape(GX, GY, 128)
        for dy in range(6):
            shifted[dy, plane, 3:11] = rows[:, 5 + dy : 37 + dy, :].astype(BF)
    ops = ops_ref[...].reshape(16 * 128, 128)
    for z in range(CZS):
        windows = []
        for k in range(16):
            dz, dx, dy = offsets_ref[k, 0], offsets_ref[k, 1], offsets_ref[k, 2]
            window = shifted[dy + 3, dz + (3 + z), pl.ds(dx + 3, GX)]
            windows.append(window.reshape(GX * GY, 128))
        total = jnp.dot(jnp.concatenate(windows, axis=1), ops, preferred_element_type=F32)
        out_ref[z * 256 : (z + 1) * 256, :] = total.astype(BF)


def field_kernel(ids_ref, basis_ref, parts_ref, out_ref):
    local = parts_ref[0].astype(F32)
    for peer in range(1, parts_ref.shape[0]):
        local = local + parts_ref[peer].astype(F32)
    high = local.astype(BF)
    low = (local - high.astype(F32)).astype(BF)
    pick = one_hot(ids_ref[...])
    picked = jnp.dot(pick, high, preferred_element_type=F32)
    picked = picked + jnp.dot(pick, low, preferred_element_type=F32)
    product = picked * basis_ref[...].astype(F32)
    out_ref[...] = jnp.sum(product.reshape(8, 128, 128), axis=2) * (128 ** -0.5)


def ops_moves():
    moves = []
    for z in range(16):
        for a in range(8):
            d = (a - z) % 8
            d = d - 8 if d > 4 else d
            moves.append((spot((z + d) % 16, (a + z) % 8), spot(z, a)))
    return moves


def spot(z, a):
    return (z // 8 * 8 + a) * 8 + z % 8


def slab_spot(s):
    return s % 4 * 16 + s // 4


def call(kernel, out_shape, in_specs, scratch=(), flops=0, size=0):
    return pl.pallas_call(
        kernel,
        out_shape=out_shape,
        in_specs=in_specs,
        out_specs=VMEM,
        scratch_shapes=list(scratch),
        compiler_params=pltpu.CompilerParams(vmem_limit_bytes=40 * 1024 * 1024),
        cost_estimate=pl.CostEstimate(flops=flops, bytes_accessed=size, transcendentals=0),
    )


def body(bead_data, bead_cell, m2l_ops, offsets):
    place = ("zh", "y", "c", "zl")
    ops = lax.ppermute(m2l_ops, place, ops_moves())
    shifts = lax.ppermute(offsets, place, ops_moves())

    inside = jnp.bitwise_and(bead_cell, RUN - 1).astype(BF).reshape(512, 1, 2, 1)
    inside = jnp.broadcast_to(inside, (512, 1, 2, 128))
    sent = jnp.concatenate([bead_data.reshape(512, 2, 2, 128), inside], axis=1)
    got = lax.all_to_all(sent.reshape(1536, 2, 128), OWNERS, split_axis=0, concat_axis=0, tiled=True)
    got = got.reshape(512, 3, 2, 128)
    moments = got[:, :2, 0].reshape(1024, 128)
    basis = got[:, :2, 1].reshape(1024, 128)
    ids = got[:, 2].reshape(1024, 128)

    cells = call(sum_kernel, jax.ShapeDtypeStruct((8, 128, 128), BF), [VMEM, VMEM])(ids, moments)
    slab = lax.all_to_all(cells, GROUP, split_axis=0, concat_axis=0, tiled=True).reshape(1024, 128)
    low = lax.ppermute(slab[256:], SLABS, [(slab_spot(i), slab_spot(i + 1)) for i in range(63)])
    high = lax.ppermute(slab[:512], SLABS, [(slab_spot(i + 1), slab_spot(i)) for i in range(63)])
    parts = call(
        m2l_kernel,
        jax.ShapeDtypeStruct((1024, 128), BF),
        [SMEM, VMEM, VMEM, VMEM, VMEM],
        [pltpu.VMEM((GX, 48, 128), F32), pltpu.VMEM((6, 9, 13, GY, 128), BF)],
    )(shifts, ops, slab, low, high)
    parts = lax.all_to_all(parts.reshape(8, 128, 128), GROUP, split_axis=0, concat_axis=0, tiled=True)
    field = call(field_kernel, jax.ShapeDtypeStruct((8, 128), F32), [VMEM, VMEM, VMEM])(ids, basis, parts)
    field = lax.all_to_all(field.reshape(512, 2), OWNERS, split_axis=0, concat_axis=0, tiled=True)
    return field.reshape(1024)


def solution(mesh):
    fine = Mesh(mesh.devices.reshape(4, 2, 4, 2, 8), ("x", "zh", "y", "c", "zl"))
    every = ("x", "zh", "y", "c", "zl")
    in_specs = (P(every, None, None), P(every), P("zl", None, None), P("zl", None))
    return jax.shard_map(body, mesh=fine, in_specs=in_specs, out_specs=P(every), check_vma=False)
```

time: 432 us -> 168 us (0.39)
  waiting for transfers between devices: 154 us -> 58.4 us
  blocking collectives: 140 us -> 50.3 us
  loops' own time: 61 us -> 0 us
  starting transfers between devices: 16.1 us -> 46.8 us
  matrix products: 16.5 us -> 0 us
  local copies, waits for them, and re-layouts: 20.2 us -> 3.72 us
  between operations: 13.5 us -> 0.16 us
  other arithmetic: 8.96 us -> 4 us
    psum x1 -> x0, waiting for transfers between devices: 129 us -> none  [body(): local = lax.psum(own_local, 'off')]
    psum x1 -> x0, blocking collectives: 68.6 us -> none  [body(): summed = lax.psum(partial_value, 'off')]
    another operation x1 -> x0, loops' own time: 61 us -> none  [translate_all(): lax.scan(translate, jnp.zeros((cells_dev, width), jnp.float32), (m2l_ops,...]
    all_to_all x1 -> x2, waiting for transfers between devices: 20.3 us -> 57.6 us  [the longest x1 51.3 us: body(): lax.all_to_all(sent.reshape(1536, 2, 128), OWNERS, split_axis=0, concat_a...]
    all_to_all x1 -> x2, starting transfers between devices: 4.72 us -> 31 us  [the longest x1 24.3 us: body(): lax.all_to_all(sent.reshape(1536, 2, 128), OWNERS, split_axis=0, concat_a...]
    all_to_all x2, blocking collectives: 71 us -> 50.3 us  [the longest x1 39.3 us: body(): lax.all_to_all(field.reshape(512, 2), OWNERS, split_axis=0, concat_axis=0...]
    dot_general x16 -> x0, matrix products: 16.5 us -> none  [translate(): jnp.dot(window, matrix, preferred_element_type=jnp.float32)]
    slice x17 -> x4, local copies, waits for them, and re-layouts: 9.7 us -> 0.93 us  [the longest x1 0.73 us: body(): moments = got[:, :2, 0].reshape(1024, 128)]
  transfers between devices with their start and end apart: 4 -> 6, of which waited for: 4 -> 3; matrix products, arithmetic and copies ran while one was open for 0% -> 1% of each run, Pallas kernels for 0% -> 0%
where the time goes in v1:
time: 168 us; the launch traced here: 167 us
  waiting for transfers between devices  58.4 us (35%)
  blocking collectives  50.3 us (30%)
  starting transfers between devices  46.8 us (28%)
  other arithmetic  4 us (2%)
  Pallas kernels  3.97 us (2%)
  local copies, waits for them, and re-layouts  3.72 us (2%)
    all_to_all x1, waiting for transfers between devices, body(): lax.all_to_all(sent.reshape(1536, 2, 128), OWNERS, split_axis=0, concat_a...  51.3 us
    all_to_all x1, blocking collectives, body(): lax.all_to_all(field.reshape(512, 2), OWNERS, split_axis=0, concat_axis=0...  39.3 us
    all_to_all x1, starting transfers between devices, body(): lax.all_to_all(sent.reshape(1536, 2, 128), OWNERS, split_axis=0, concat_a...  24.3 us
    all_to_all x1, blocking collectives, body(): lax.all_to_all(cells, GROUP, split_axis=0, concat_axis=0, tiled=True)  11 us
    ppermute x1, starting transfers between devices, body(): shifts = lax.ppermute(offsets, place, ops_moves())  8.65 us
    all_to_all x1, starting transfers between devices, body(): lax.all_to_all(parts.reshape(8, 128, 128), GROUP, split_axis=0, concat_ax...  6.72 us
    all_to_all x1, waiting for transfers between devices, body(): lax.all_to_all(parts.reshape(8, 128, 128), GROUP, split_axis=0, concat_ax...  6.32 us
    ppermute x1, starting transfers between devices, body(): ops = lax.ppermute(m2l_ops, place, ops_moves())  3.66 us
  transfers between devices with their start and end apart: 6, of which 3 were waited for; matrix products, arithmetic and copies ran while one was open for 1% of the time, Pallas kernels for 0%

profile of v1, /device:TPU:1, one launch (start us, length us, event | category | flops | bytes accessed | tf_op | source)
XLA Modules:
  0.0 167.3 jit_solution(1574804848319692097)
XLA Ops:
  0.0 0.7 and_convert_fusion
  0.8 0.3 broadcast_in_dim.7
  1.0 0.6 broadcast_in_dim.8
  1.6 2.0 %pad_maximum_fusion = bf16[512,3,2,128]{3,2,1,0:T(2,128)(2,1)} fusion(bf16[512,1,2,128]{3,2,1,0:T(2,128)(2,1)S(1)} %broadcast_in_dim.8, bf16[512,2,2,128]{3,2,1,0:T(2,128)(2,1)S(1)} %bitcast.19), kind=kLoop, calls=%fused_computation | loop fusion | flops 393216 | bytes 1572864 | tf_op jit(solution)/shard_map/concatenate | solution.py:112
  3.6 24.3 %all-to-all-start = ((bf16[1536,2,128]{2,1,0:T(2,128)(2,1)}), bf16[1536,2,128]{2,1,0:T(2,128)(2,1)S(1)}, u32[]{:S(2)}, u32[]{:S(2)}) async-start(bf16[1536,2,128]{2,1,0:T(2,128)(2,1)} %bitcast.1), calls=%async_computation | async-start | bytes 1572864 | tf_op jit(solution)/shard_map/all_to_all | solution.py:113
  27.9 3.7 %collective-permute-start.1 = (bf16[16,128,128]{2,1,0:T(8,128)(2,1)S(1)}, bf16[16,128,128]{2,1,0:T(8,128)(2,1)S(1)}, u32[]{:S(2)}, u32[]{:S(2)}) collective-permute-start(bf16[16,128,128]{2,1,0:T(8,128)(2,1)S(1)} %copy-done.2), channel_id=1, source_target_pairs={{0,0},{9,8},{18,16},{27,24},{36,32},{109,40},{118,48},{127,56},{8,... | collective-permute-start | bytes 1572872 | tf_op jit(solution)/shard_map/ppermute | solution.py:107
  31.6 51.3 %all-to-all-done = bf16[1536,2,128]{2,1,0:T(2,128)(2,1)S(1)} async-done(((bf16[1536,2,128]{2,1,0:T(2,128)(2,1)}), bf16[1536,2,128]{2,1,0:T(2,128)(2,1)S(1)}, u32[]{:S(2)}, u32[]{:S(2)}) %all-to-all-start) | async-done | bytes 786464 | tf_op jit(solution)/shard_map/all_to_all | solution.py:113
  82.9 0.7 fusion
  83.6 0.2 slice.28
  84.0 0.3 shard_map.46
  84.3 11.0 %all_to_all.24 = bf16[8,128,128]{2,1,0:T(8,128)(2,1)S(1)} all-to-all(bf16[8,128,128]{2,1,0:T(8,128)(2,1)S(1)} %shard_map.46), channel_id=1, replica_groups=mesh['x'=4,'zh'=2,'y'=4,'c'=2,'zl'=8] {'y','c'}, dimensions={0} | all-to-all | bytes 524288 | tf_op jit(solution)/shard_map/all_to_all | solution.py:120
  95.3 2.2 %collective-permute-start.2 = (bf16[768,128]{1,0:T(8,128)(2,1)S(1)}, bf16[768,128]{1,0:T(8,128)(2,1)S(1)}, u32[]{:S(2)}, u32[]{:S(2)}) collective-permute-start(bf16[768,128]{1,0:T(8,128)(2,1)S(1)} %bitcast.20), channel_id=1, source_target_pairs={{0,128},{128,256},{256,384},{384,1},{1,129},{129,257},{257,385},{3... | collective-permute-start | bytes 589832 | tf_op jit(solution)/shard_map/ppermute | solution.py:121
  97.5 1.3 collective-permute-start.3
  98.9 8.6 %collective-permute-start = (s32[16,3]{1,0:T(8,128)S(1)}, s32[16,3]{1,0:T(8,128)S(1)}, u32[]{:S(2)}, u32[]{:S(2)}) collective-permute-start(s32[16,3]{1,0:T(8,128)S(1)} %copy.10), channel_id=1, source_target_pairs={{0,0},{9,8},{18,16},{27,24},{36,32},{109,40},{118,48},{127,56},{8,... | collective-permute-start | bytes 584 | tf_op jit(solution)/shard_map/ppermute | solution.py:108
  107.5 0.8 collective-permute-done.offsets_ref
  108.3 3.3 %shard_map.47 = bf16[1024,128]{1,0:T(8,128)(2,1)} custom-call(s32[16,3]{1,0:T(8,128)S(1)} %collective-permute-done.offsets_ref, bf16[16,128,128]{2,1,0:T(8,128)(2,1)S(1)} %collective-permute-done.1.ops_ref, bf16[1024,128]{1,0:T(8,128)(2,1)S(1)} %bitcast.11, bf16[768,128]{1,0:T(8,128)(2,1)S(1)} %collective-permute-done.2.low_ref, ...), custom_call_target="tpu_custom_call" | custom-call | tf_op jit(solution)/shard_map/pallas_call | solution.py:123
  111.6 6.7 %all-to-all-start.2 = ((bf16[8,128,128]{2,1,0:T(8,128)(2,1)}), bf16[8,128,128]{2,1,0:T(8,128)(2,1)S(1)}, u32[]{:S(2)}, u32[]{:S(2)}) async-start(bf16[8,128,128]{2,1,0:T(8,128)(2,1)} %bitcast.7), calls=%async_computation.2 | async-start | bytes 524288 | tf_op jit(solution)/shard_map/all_to_all | solution.py:129
  118.5 6.3 %all-to-all-done.2.parts_ref = bf16[8,128,128]{2,1,0:T(8,128)(2,1)S(1)} async-done(((bf16[8,128,128]{2,1,0:T(8,128)(2,1)}), bf16[8,128,128]{2,1,0:T(8,128)(2,1)S(1)}, u32[]{:S(2)}, u32[]{:S(2)}) %all-to-all-start.2) | async-done | bytes 262176 | tf_op jit(solution)/shard_map/all_to_all | solution.py:129
  124.9 0.4 shard_map.48
  125.2 0.2 all_to_all.18
  125.5 39.3 %all_to_all.25 = f32[512,1,2]{2,1,0:T(1,128)S(1)} all-to-all(f32[512,1,2]{2,1,0:T(1,128)S(1)} %bitcast.18), channel_id=1, replica_groups=mesh['x'=4,'zh'=2,'y'=4,'c'=2,'zl'=8] {'zh','zl','x','y','c'}, dimensions={0} | all-to-all | bytes 8192 | tf_op jit(solution)/shard_map/all_to_all | solution.py:131
  164.7 0.5 broadcast.4
  165.2 1.3 reduce.3
  166.5 0.8 reshape.34
  (14 shorter events, 0.5 us)
Async XLA Ops:
  0.0 1.6 copy-start
  3.6 24.3 %copy-start.2 = (bf16[16,128,128]{2,1,0:T(8,128)(2,1)S(1)}, bf16[16,128,128]{2,1,0:T(8,128)(2,1)}, u32[]{:S(2)}) copy-start(bf16[16,128,128]{2,1,0:T(8,128)(2,1)} %param.6) | copy-start | bytes 1572868
  3.6 79.3 %all-to-all-start = ((bf16[1536,2,128]{2,1,0:T(2,128)(2,1)}), bf16[1536,2,128]{2,1,0:T(2,128)(2,1)S(1)}, u32[]{:S(2)}, u32[]{:S(2)}) async-start(bf16[1536,2,128]{2,1,0:T(2,128)(2,1)} %bitcast.1), calls=%async_computation | async-start | bytes 1572864 | tf_op jit(solution)/shard_map/all_to_all | solution.py:113
  27.9 80.4 %collective-permute-start.1 = (bf16[16,128,128]{2,1,0:T(8,128)(2,1)S(1)}, bf16[16,128,128]{2,1,0:T(8,128)(2,1)S(1)}, u32[]{:S(2)}, u32[]{:S(2)}) collective-permute-start(bf16[16,128,128]{2,1,0:T(8,128)(2,1)S(1)} %copy-done.2), channel_id=1, source_target_pairs={{0,0},{9,8},{18,16},{27,24},{36,32},{109,40},{118,48},{127,56},{8,... | collective-permute-start | bytes 1572872 | tf_op jit(solution)/shard_map/ppermute | solution.py:107
  95.3 13.0 %collective-permute-start.2 = (bf16[768,128]{1,0:T(8,128)(2,1)S(1)}, bf16[768,128]{1,0:T(8,128)(2,1)S(1)}, u32[]{:S(2)}, u32[]{:S(2)}) collective-permute-start(bf16[768,128]{1,0:T(8,128)(2,1)S(1)} %bitcast.20), channel_id=1, source_target_pairs={{0,128},{128,256},{256,384},{384,1},{1,129},{129,257},{257,385},{3... | collective-permute-start | bytes 589832 | tf_op jit(solution)/shard_map/ppermute | solution.py:121
  97.5 1.3 copy-start.1
  97.5 10.8 %collective-permute-start.3 = (bf16[512,128]{1,0:T(8,128)(2,1)S(1)}, bf16[512,128]{1,0:T(8,128)(2,1)S(1)}, u32[]{:S(2)}, u32[]{:S(2)}) collective-permute-start(bf16[512,128]{1,0:T(8,128)(2,1)S(1)} %bitcast.21), channel_id=1, source_target_pairs={{128,0},{256,128},{384,256},{1,384},{129,1},{257,129},{385,257},{2... | collective-permute-start | bytes 393224 | tf_op jit(solution)/shard_map/ppermute | solution.py:122
  98.9 9.4 %collective-permute-start = (s32[16,3]{1,0:T(8,128)S(1)}, s32[16,3]{1,0:T(8,128)S(1)}, u32[]{:S(2)}, u32[]{:S(2)}) collective-permute-start(s32[16,3]{1,0:T(8,128)S(1)} %copy.10), channel_id=1, source_target_pairs={{0,0},{9,8},{18,16},{27,24},{36,32},{109,40},{118,48},{127,56},{8,... | collective-permute-start | bytes 584 | tf_op jit(solution)/shard_map/ppermute | solution.py:108
  111.6 13.2 %all-to-all-start.2 = ((bf16[8,128,128]{2,1,0:T(8,128)(2,1)}), bf16[8,128,128]{2,1,0:T(8,128)(2,1)S(1)}, u32[]{:S(2)}, u32[]{:S(2)}) async-start(bf16[8,128,128]{2,1,0:T(8,128)(2,1)} %bitcast.7), calls=%async_computation.2 | async-start | bytes 524288 | tf_op jit(solution)/shard_map/all_to_all | solution.py:129

commit v2 on v1

v2 whole, which is shorter than its diff:
```python
import functools

import jax
import jax.numpy as jnp
import numpy as np
from jax import lax
from jax.experimental import pallas as pl
from jax.experimental.pallas import tpu as pltpu
from jax.sharding import Mesh, PartitionSpec as P

GX = 8
GY = 32
CZS = 4
RUN = 128
BF = jnp.bfloat16
F32 = jnp.float32

COLUMN = ("zh", "zl")
LAYER = ("x", "y", "c")
SLABS = ("x", "zh", "zl")
GROUP = ("y", "c")
VMEM = pl.BlockSpec(memory_space=pltpu.VMEM)
SMEM = pl.BlockSpec(memory_space=pltpu.SMEM)


def iota(shape, dim):
    return lax.broadcasted_iota(jnp.int32, shape, dim)


def mask(where):
    return jnp.where(where, 1.0, 0.0)


def dot(a, b, dims=((1,), (0,)), precision=None):
    return lax.dot_general(a, b, (dims, ((), ())), precision=precision, preferred_element_type=F32)


def pack_kernel(offsets_ref, beads_ref, cells_ref, out_ref):
    for z in range(16):
        out_ref[z, 0:64] = beads_ref[64 * z : 64 * z + 64]
    inside = jnp.bitwise_and(cells_ref[...], RUN - 1).astype(F32)
    lane = iota((1, 128), 1)
    shifts = jnp.zeros((1, 128), F32)
    for k in range(16):
        for j in range(3):
            shifts = jnp.where(lane == 3 * k + j, offsets_ref[k, j].astype(F32), shifts)
    rows = []
    for z in range(16):
        rows += [inside[z // 2 : z // 2 + 1], shifts]
    out_ref[:, 64] = jnp.concatenate(rows, axis=0).astype(BF).reshape(16, 2, 128)


def regroup_kernel(place_ref, got_ref, out_ref, offsets_ref):
    core, half, shard = place_ref[0], place_ref[1], place_ref[2]
    for z in range(16):
        out_ref[:, 2 * z : 2 * z + 2] = got_ref[z, 0:64].reshape(32, 2, 2, 128)
    extra = got_ref[:, 64].reshape(32, 128)
    row, lane = iota((32, 128), 0), iota((32, 128), 1)
    take_row, take_lane = iota((64, 128), 0), iota((64, 128), 1)
    ids = jnp.zeros((64, 128), F32)
    for i in range(2):
        put = mask((row % 2 == 0) & (lane // 2 - 32 * core == row + i))
        take = mask((take_row % 2 == 0) & (take_lane == 64 * half + take_row + i))
        moved = dot(extra, put.astype(BF), ((0,), (0,)))
        ids = ids + dot(take.astype(BF), moved.astype(BF))
    out_ref[:, 32] = ids.astype(BF).reshape(32, 2, 128)
    out_ref[:, 33:40] = jnp.zeros((32, 7, 2, 128), BF)
    own = jnp.sum(mask(row == 2 * shard + 1) * extra.astype(F32), axis=0, keepdims=True)
    offsets_ref[...] = jnp.broadcast_to(own, (8, 128)).astype(jnp.int32)


def rows_of(got_ref, pair):
    at = 160 * pair
    return jnp.concatenate([got_ref[at : at + 64, :], got_ref[at + 80 : at + 144, :]], axis=0)


def sum_kernel(got_ref, cells_ref, ids_ref):
    cell, lane = iota((128, 128), 0), iota((128, 128), 1)
    even = lane % 2 == 0
    total = jnp.zeros((128, 128), F32)
    for pair in range(16):
        at = 160 * pair
        ids = got_ref[at + 64 : at + 80, :].astype(F32) + got_ref[at + 144 : at + 160, :].astype(F32)
        ids = ids[0:1]
        ids_ref[pair : pair + 1, :] = ids
        hot = mask((ids.astype(jnp.int32) == cell) & even).astype(BF)
        total = total + dot(hot, rows_of(got_ref, pair))
    cells = total.astype(BF)
    for peer in range(cells_ref.shape[0]):
        cells_ref[peer] = cells


def m2l_kernel(offsets_ref, ops_ref, own_ref, low_ref, high_ref, out_ref, rows, shifted):
    shifted[:, :, 0:3] = jnp.zeros((6, 9, 3, GY, 128), BF)
    shifted[:, :, 11:13] = jnp.zeros((6, 9, 2, GY, 128), BF)
    rows[:, 0:8, :] = jnp.zeros((GX, 8, 128), F32)
    rows[:, 40:48, :] = jnp.zeros((GX, 8, 128), F32)
    for plane in range(9):
        ref, at = (low_ref, plane) if plane < 3 else (own_ref, plane - 3) if plane < 7 else (high_ref, plane - 7)
        rows[:, 8:40, :] = ref[at * 256 : (at + 1) * 256, :].astype(F32).reshape(GX, GY, 128)
        for dy in range(6):
            shifted[dy, plane, 3:11] = rows[:, 5 + dy : 37 + dy, :].astype(BF)
    ops = ops_ref[...].reshape(16 * 128, 128)
    for z in range(CZS):
        windows = []
        for k in range(16):
            dz, dx, dy = offsets_ref[0, 3 * k], offsets_ref[0, 3 * k + 1], offsets_ref[0, 3 * k + 2]
            window = shifted[dy + 3, dz + (3 + z), pl.ds(dx + 3, GX)]
            windows.append(window.reshape(GX * GY, 128))
        total = jnp.dot(jnp.concatenate(windows, axis=1), ops, preferred_element_type=F32)
        out_ref[z * 256 : (z + 1) * 256, :] = total.astype(BF)


def field_kernel(ids_ref, got_ref, parts_ref, out_ref):
    local = parts_ref[0].astype(F32)
    for peer in range(1, parts_ref.shape[0]):
        local = local + parts_ref[peer].astype(F32)
    high = local.astype(BF)
    low = (local - high.astype(F32)).astype(BF)
    split = jnp.concatenate([high, low], axis=0)
    cell, lane = iota((128, 128), 0), iota((128, 128), 1)
    odd = lane % 2 == 1
    for pair in range(16):
        every = dot(split, rows_of(got_ref, pair), ((1,), (1,)))
        every = every[0:128] + every[128:256]
        hot = (ids_ref[pair : pair + 1, :].astype(jnp.int32) == cell) & odd
        field = jnp.sum(jnp.where(hot, every, 0.0), axis=0, keepdims=True) * (128 ** -0.5)
        out_ref[2 * pair : 2 * pair + 1, :] = field
        out_ref[2 * pair + 1 : 2 * pair + 2, :] = field


def return_kernel(place_ref, got_ref, out_ref):
    core, half = place_ref[0], place_ref[1]
    exact = lax.Precision.HIGHEST
    z, lane = iota((16, 128), 0), iota((16, 128), 1)
    owner, column = iota((32, 128), 0), iota((32, 128), 1)
    total = jnp.zeros((16, 128), F32)
    for i in range(2):
        take = mask(lane == 64 * core + 4 * z + 2 * i + 1)
        put = mask(column == 64 * half + 2 * owner + i)
        total = total + dot(dot(take, got_ref[...], ((1,), (1,)), exact), put, precision=exact)
    out_ref[...] = total


def join_kernel(got_ref, out_ref):
    for k in range(8):
        out_ref[k : k + 1, :] = got_ref[2 * k : 2 * k + 1, :] + got_ref[2 * k + 1 : 2 * k + 2, :]


def ops_moves():
    moves = []
    for z in range(16):
        for a in range(8):
            d = (a - z) % 8
            d = d - 8 if d > 4 else d
            moves.append((spot((z + d) % 16, (a + z) % 8), spot(z, a)))
    return moves


def spot(z, a):
    return (z // 8 * 8 + a) * 8 + z % 8


def slab_spot(s):
    return s % 4 * 16 + s // 4


def call(kernel, out_shape, in_specs, scratch=()):
    many = isinstance(out_shape, list)
    return pl.pallas_call(
        kernel,
        out_shape=out_shape,
        in_specs=in_specs,
        out_specs=[VMEM] * len(out_shape) if many else VMEM,
        scratch_shapes=list(scratch),
        compiler_params=pltpu.CompilerParams(vmem_limit_bytes=40 * 1024 * 1024),
    )


def shape(*size, kind=BF):
    return jax.ShapeDtypeStruct(size, kind)


def exchange(array, axes):
    return lax.all_to_all(array, axes, split_axis=0, concat_axis=0, tiled=True)


def body(bead_data, bead_cell, m2l_ops, offsets):
    core = lax.axis_index("c")
    place = jnp.stack([core, lax.axis_index("zl") % 2, lax.axis_index("y") * 2 + core])

    sent = call(pack_kernel, shape(16, 65, 2, 128), [SMEM, VMEM, VMEM])(
        offsets, bead_data, bead_cell.reshape(8, 128)
    )
    got = exchange(sent.reshape(1040, 2, 128), COLUMN)
    m2l_ops, got = lax.optimization_barrier((m2l_ops, got))
    ops = lax.ppermute(m2l_ops, ("zh", "y", "c", "zl"), ops_moves())
    sent, shifts = call(
        regroup_kernel, [shape(32, 40, 2, 128), shape(8, 128, kind=jnp.int32)], [SMEM, VMEM]
    )(place, got.reshape(16, 65, 2, 128))
    rows = exchange(sent.reshape(1280, 2, 128), LAYER).reshape(2560, 128)

    cells, ids = call(sum_kernel, [shape(8, 128, 128), shape(16, 128, kind=F32)], [VMEM])(rows)
    slab = exchange(cells, GROUP).reshape(1024, 128)
    low = lax.ppermute(slab[256:], SLABS, [(slab_spot(i), slab_spot(i + 1)) for i in range(63)])
    high = lax.ppermute(slab[:512], SLABS, [(slab_spot(i + 1), slab_spot(i)) for i in range(63)])
    parts = call(
        m2l_kernel,
        shape(1024, 128),
        [SMEM, VMEM, VMEM, VMEM, VMEM],
        [pltpu.VMEM((GX, 48, 128), F32), pltpu.VMEM((6, 9, 13, GY, 128), BF)],
    )(shifts, ops, slab, low, high)
    parts = exchange(parts.reshape(8, 128, 128), GROUP)
    field = call(field_kernel, shape(32, 128, kind=F32), [VMEM, VMEM, VMEM])(ids, rows, parts)
    field = exchange(field, LAYER)
    field = call(return_kernel, shape(16, 128, kind=F32), [SMEM, VMEM])(place, field)
    field = exchange(field, COLUMN)
    return call(join_kernel, shape(8, 128, kind=F32), [VMEM])(field).reshape(1024)


def solution(mesh):
    fine = Mesh(mesh.devices.reshape(4, 2, 4, 2, 8), ("x", "zh", "y", "c", "zl"))
    every = ("x", "zh", "y", "c", "zl")
    in_specs = (P(every, None, None), P(every), P("zl", None, None), P("zl", None))
    return jax.shard_map(body, mesh=fine, in_specs=in_specs, out_specs=P(every), check_vma=False)
```

time: 168 us -> 146 us (0.87)
  waiting for transfers between devices: 58.4 us -> 37.3 us
  blocking collectives: 50.3 us -> 60.9 us
  starting transfers between devices: 46.8 us -> 36.7 us
  Pallas kernels: 3.97 us -> 8.1 us
  other arithmetic: 4 us -> 0.08 us
  local copies, waits for them, and re-layouts: 3.72 us -> 1.84 us
    all_to_all x2, waiting for transfers between devices: 57.6 us -> 32.9 us  [exchange(): return lax.all_to_all(array, axes, split_axis=0, concat_axis=0, tiled=True)]
    all_to_all x2 -> x4, blocking collectives: 50.3 us -> 60.9 us  [exchange(): return lax.all_to_all(array, axes, split_axis=0, concat_axis=0, tiled=True)]
    ppermute x2 -> x1, starting transfers between devices: 12.3 us -> 3.05 us  [body(): ops = lax.ppermute(m2l_ops, ('zh', 'y', 'c', 'zl'), ops_moves())]
    ppermute x1, waiting for transfers between devices: 0.01 us -> 4.4 us  [body(): lax.ppermute(slab[:512], SLABS, [(slab_spot(i + 1), slab_spot(i)) for i i...]
    pallas_call x3 -> x7, Pallas kernels: 3.97 us -> 8.1 us  [the longest x1 2.55 us: body(): call(m2l_kernel, shape(1024, 128), [SMEM, VMEM, VMEM, VMEM, VMEM], [pltpu...]
    concatenate x1 -> x0, other arithmetic: 1.96 us -> none  [body(): sent = jnp.concatenate([bead_data.reshape(512, 2, 2, 128), inside], axis=1)]
  transfers between devices with their start and end apart: 6 -> 5, of which waited for: 3 -> 3; matrix products, arithmetic and copies ran while one was open for 1% -> 0% of each run, Pallas kernels for 0% -> 0%
where the time goes in v2:
time: 146 us; the launch traced here: 145 us
  blocking collectives  60.9 us (42%)
  waiting for transfers between devices  37.3 us (26%)
  starting transfers between devices  36.7 us (25%)
  Pallas kernels  8.1 us (6%)
  local copies, waits for them, and re-layouts  1.84 us (1%)
    all_to_all x4, blocking collectives, exchange(): return lax.all_to_all(array, axes, split_axis=0, concat_axis=0, tiled=True)  60.9 us
    all_to_all x2, waiting for transfers between devices, exchange(): return lax.all_to_all(array, axes, split_axis=0, concat_axis=0, tiled=True)  32.9 us
    all_to_all x2, starting transfers between devices, exchange(): return lax.all_to_all(array, axes, split_axis=0, concat_axis=0, tiled=True)  30.1 us
    ppermute x1, waiting for transfers between devices, body(): lax.ppermute(slab[:512], SLABS, [(slab_spot(i + 1), slab_spot(i)) for i i...  4.4 us
    ppermute x1, starting transfers between devices, body(): ops = lax.ppermute(m2l_ops, ('zh', 'y', 'c', 'zl'), ops_moves())  3.05 us
  transfers between devices with their start and end apart: 5, of which 3 were waited for; matrix products, arithmetic and copies ran while one was open for 0% of the time, Pallas kernels for 0%

profile of v2, /device:TPU:1, one launch (start us, length us, event | category | flops | bytes accessed | tf_op | source)
XLA Modules:
  0.0 145.1 jit_solution(17430248406228764237)
XLA Ops:
  0.0 0.8 copy.6.offsets_ref
  0.8 1.0 copy-done
  1.8 1.5 %shard_map.46 = bf16[16,65,2,128]{3,2,1,0:T(2,128)(2,1)} custom-call(s32[16,3]{1,0:T(8,128)S(1)} %copy.6.offsets_ref, bf16[1024,2,128]{2,1,0:T(2,128)(2,1)S(1)} %copy-done, s32[8,128]{1,0:T(8,128)S(1)} %bitcast.30), custom_call_target="tpu_custom_call" | custom-call | tf_op jit(solution)/shard_map/pallas_call | solution.py:192
  3.3 15.7 %all-to-all-start = ((bf16[1040,2,128]{2,1,0:T(2,128)(2,1)}), bf16[1040,2,128]{2,1,0:T(2,128)(2,1)S(1)}, u32[]{:S(2)}, u32[]{:S(2)}) async-start(bf16[1040,2,128]{2,1,0:T(2,128)(2,1)} %bitcast.4), calls=%async_computation | async-start | bytes 1064960 | tf_op jit(solution)/shard_map/all_to_all | solution.py:185
  19.1 0.1 pad_add_fusion.place_ref
  19.2 23.0 %all-to-all-done = bf16[1040,2,128]{2,1,0:T(2,128)(2,1)S(1)} async-done(((bf16[1040,2,128]{2,1,0:T(2,128)(2,1)}), bf16[1040,2,128]{2,1,0:T(2,128)(2,1)S(1)}, u32[]{:S(2)}, u32[]{:S(2)}) %all-to-all-start) | async-done | bytes 532512 | tf_op jit(solution)/shard_map/all_to_all | solution.py:185
  42.2 1.8 %shard_map.47 = (bf16[32,40,2,128]{3,2,1,0:T(2,128)(2,1)}, s32[8,128]{1,0:T(8,128)S(1)}) custom-call(s32[3]{0:T(128)S(1)} %pad_add_fusion.place_ref, bf16[16,65,2,128]{3,2,1,0:T(2,128)(2,1)S(1)} %bitcast.24), custom_call_target="tpu_custom_call" | custom-call | tf_op jit(solution)/shard_map/pallas_call | solution.py:198
  44.0 14.4 %all-to-all-start.1 = ((bf16[1280,2,128]{2,1,0:T(2,128)(2,1)}), bf16[1280,2,128]{2,1,0:T(2,128)(2,1)S(1)}, u32[]{:S(2)}, u32[]{:S(2)}) async-start(bf16[1280,2,128]{2,1,0:T(2,128)(2,1)} %bitcast.6), calls=%async_computation.1 | async-start | bytes 1310720 | tf_op jit(solution)/shard_map/all_to_all | solution.py:185
  58.4 3.1 %collective-permute-start = (bf16[16,128,128]{2,1,0:T(8,128)(2,1)S(1)}, bf16[16,128,128]{2,1,0:T(8,128)(2,1)S(1)}, u32[]{:S(2)}, u32[]{:S(2)}) collective-permute-start(bf16[16,128,128]{2,1,0:T(8,128)(2,1)S(1)} %copy-done.2), channel_id=1, source_target_pairs={{0,0},{9,8},{18,16},{27,24},{36,32},{109,40},{118,48},{127,56},{8,... | collective-permute-start | bytes 1572872 | tf_op jit(solution)/shard_map/ppermute | solution.py:197
  61.4 9.9 %all-to-all-done.1 = bf16[1280,2,128]{2,1,0:T(2,128)(2,1)S(1)} async-done(((bf16[1280,2,128]{2,1,0:T(2,128)(2,1)}), bf16[1280,2,128]{2,1,0:T(2,128)(2,1)S(1)}, u32[]{:S(2)}, u32[]{:S(2)}) %all-to-all-start.1) | async-done | bytes 655392 | tf_op jit(solution)/shard_map/all_to_all | solution.py:185
  71.3 0.3 shard_map.48
  71.6 9.3 %all_to_all.42 = bf16[8,128,128]{2,1,0:T(8,128)(2,1)S(1)} all-to-all(bf16[8,128,128]{2,1,0:T(8,128)(2,1)S(1)} %get-tuple-element.16), channel_id=1, replica_groups=mesh['x'=4,'zh'=2,'y'=4,'c'=2,'zl'=8] {'y','c'}, dimensions={0} | all-to-all | bytes 524288 | tf_op jit(solution)/shard_map/all_to_all | solution.py:185
  80.9 2.3 %collective-permute-start.1 = (bf16[768,128]{1,0:T(8,128)(2,1)S(1)}, bf16[768,128]{1,0:T(8,128)(2,1)S(1)}, u32[]{:S(2)}, u32[]{:S(2)}) collective-permute-start(bf16[768,128]{1,0:T(8,128)(2,1)S(1)} %bitcast.31), channel_id=1, source_target_pairs={{0,128},{128,256},{256,384},{384,1},{1,129},{129,257},{257,385},{3... | collective-permute-start | bytes 589832 | tf_op jit(solution)/shard_map/ppermute | solution.py:205
  83.2 1.3 collective-permute-start.2
  84.5 0.0 collective-permute-done.ops_ref
  84.5 4.4 %collective-permute-done.2.high_ref = bf16[512,128]{1,0:T(8,128)(2,1)S(1)} collective-permute-done((bf16[512,128]{1,0:T(8,128)(2,1)S(1)}, bf16[512,128]{1,0:T(8,128)(2,1)S(1)}, u32[]{:S(2)}, u32[]{:S(2)}) %collective-permute-start.2) | collective-permute-done | bytes 131104 | tf_op jit(solution)/shard_map/ppermute | solution.py:206
  88.9 0.0 collective-permute-done.1.low_ref
  88.9 2.6 %shard_map.49 = bf16[1024,128]{1,0:T(8,128)(2,1)S(1)} custom-call(s32[8,128]{1,0:T(8,128)S(1)} %get-tuple-element.14.offsets_ref, bf16[16,128,128]{2,1,0:T(8,128)(2,1)S(1)} %collective-permute-done.ops_ref, bf16[1024,128]{1,0:T(8,128)(2,1)S(1)} %bitcast.23, bf16[768,128]{1,0:T(8,128)(2,1)S(1)} %collective-permute-done.1.low_ref, ...), custom_call_target="tpu_custom_call" | custom-call | tf_op jit(solution)/shard_map/pallas_call | solution.py:207
  91.4 11.4 %all_to_all.43.parts_ref = bf16[8,128,128]{2,1,0:T(8,128)(2,1)S(1)} all-to-all(bf16[8,128,128]{2,1,0:T(8,128)(2,1)S(1)} %bitcast.25), channel_id=1, replica_groups=mesh['x'=4,'zh'=2,'y'=4,'c'=2,'zl'=8] {'y','c'}, dimensions={0} | all-to-all | bytes 524288 | tf_op jit(solution)/shard_map/all_to_all | solution.py:185
  102.8 0.4 shard_map.50
  103.3 16.8 %all_to_all.44 = f32[32,1,128]{2,1,0:T(1,128)S(1)} all-to-all(f32[32,1,128]{2,1,0:T(1,128)S(1)} %bitcast.26), channel_id=1, replica_groups=mesh['x'=4,'zh'=2,'y'=4,'c'=2,'zl'=8] {'x','y','c'}, dimensions={0} | all-to-all | bytes 32768 | tf_op jit(solution)/shard_map/all_to_all | solution.py:185
  120.1 0.9 shard_map.51
  121.0 23.5 %all_to_all.45 = f32[16,1,128]{2,1,0:T(1,128)S(1)} all-to-all(f32[16,1,128]{2,1,0:T(1,128)S(1)} %bitcast.28), channel_id=1, replica_groups=mesh['x'=4,'zh'=2,'y'=4,'c'=2,'zl'=8] {'zh','zl'}, dimensions={0} | all-to-all | bytes 16384 | tf_op jit(solution)/shard_map/all_to_all | solution.py:185
  144.5 0.6 shard_map.52
  (7 shorter events, 0.0 us)
Async XLA Ops:
  0.0 0.8 copy-start.1
  0.8 1.0 copy-start
  3.3 38.9 %all-to-all-start = ((bf16[1040,2,128]{2,1,0:T(2,128)(2,1)}), bf16[1040,2,128]{2,1,0:T(2,128)(2,1)S(1)}, u32[]{:S(2)}, u32[]{:S(2)}) async-start(bf16[1040,2,128]{2,1,0:T(2,128)(2,1)} %bitcast.4), calls=%async_computation | async-start | bytes 1064960 | tf_op jit(solution)/shard_map/all_to_all | solution.py:185
  44.0 14.4 %copy-start.2 = (bf16[16,128,128]{2,1,0:T(8,128)(2,1)S(1)}, bf16[16,128,128]{2,1,0:T(8,128)(2,1)}, u32[]{:S(2)}) copy-start(bf16[16,128,128]{2,1,0:T(8,128)(2,1)} %param.6) | copy-start | bytes 1572868
  44.0 27.3 %all-to-all-start.1 = ((bf16[1280,2,128]{2,1,0:T(2,128)(2,1)}), bf16[1280,2,128]{2,1,0:T(2,128)(2,1)S(1)}, u32[]{:S(2)}, u32[]{:S(2)}) async-start(bf16[1280,2,128]{2,1,0:T(2,128)(2,1)} %bitcast.6), calls=%async_computation.1 | async-start | bytes 1310720 | tf_op jit(solution)/shard_map/all_to_all | solution.py:185
  58.4 26.1 %collective-permute-start = (bf16[16,128,128]{2,1,0:T(8,128)(2,1)S(1)}, bf16[16,128,128]{2,1,0:T(8,128)(2,1)S(1)}, u32[]{:S(2)}, u32[]{:S(2)}) collective-permute-start(bf16[16,128,128]{2,1,0:T(8,128)(2,1)S(1)} %copy-done.2), channel_id=1, source_target_pairs={{0,0},{9,8},{18,16},{27,24},{36,32},{109,40},{118,48},{127,56},{8,... | collective-permute-start | bytes 1572872 | tf_op jit(solution)/shard_map/ppermute | solution.py:197
  80.9 8.0 %collective-permute-start.1 = (bf16[768,128]{1,0:T(8,128)(2,1)S(1)}, bf16[768,128]{1,0:T(8,128)(2,1)S(1)}, u32[]{:S(2)}, u32[]{:S(2)}) collective-permute-start(bf16[768,128]{1,0:T(8,128)(2,1)S(1)} %bitcast.31), channel_id=1, source_target_pairs={{0,128},{128,256},{256,384},{384,1},{1,129},{129,257},{257,385},{3... | collective-permute-start | bytes 589832 | tf_op jit(solution)/shard_map/ppermute | solution.py:205
  83.2 5.7 %collective-permute-start.2 = (bf16[512,128]{1,0:T(8,128)(2,1)S(1)}, bf16[512,128]{1,0:T(8,128)(2,1)S(1)}, u32[]{:S(2)}, u32[]{:S(2)}) collective-permute-start(bf16[512,128]{1,0:T(8,128)(2,1)S(1)} %bitcast.32), channel_id=1, source_target_pairs={{128,0},{256,128},{384,256},{1,384},{129,1},{257,129},{385,257},{2... | collective-permute-start | bytes 393224 | tf_op jit(solution)/shard_map/ppermute | solution.py:206

commit v3 on v2

v3 whole, which is shorter than its diff:
```python
import functools

import jax
import jax.numpy as jnp
import numpy as np
from jax import lax
from jax.experimental import pallas as pl
from jax.experimental.pallas import tpu as pltpu
from jax.sharding import Mesh, PartitionSpec as P

GX = 8
GY = 32
CZS = 4
RUN = 128
BF = jnp.bfloat16
F32 = jnp.float32

COLUMN = ("zh", "zl")
LAYER = ("x", "y", "c")
SLABS = ("x", "zh", "zl")
GROUP = ("y", "c")
VMEM = pl.BlockSpec(memory_space=pltpu.VMEM)
SMEM = pl.BlockSpec(memory_space=pltpu.SMEM)


def iota(shape, dim):
    return lax.broadcasted_iota(jnp.int32, shape, dim)


def mask(where):
    return jnp.where(where, 1.0, 0.0)


def dot(a, b, dims=((1,), (0,)), precision=None):
    return lax.dot_general(a, b, (dims, ((), ())), precision=precision, preferred_element_type=F32)


def pack_kernel(offsets_ref, rows_ref, cells_ref, moments_ref):
    to, at = iota((64, 128), 0), iota((64, 128), 1)
    part = mask(at == 2 * to).astype(BF)
    for z in range(16):
        moments_ref[z, 0:32] = dot(part, rows_ref[128 * z : 128 * z + 128, :]).astype(BF).reshape(32, 2, 128)
    inside = jnp.bitwise_and(cells_ref[...], RUN - 1).astype(F32)
    lane = iota((1, 128), 1)
    shifts = jnp.zeros((1, 128), F32)
    for k in range(16):
        for j in range(3):
            shifts = jnp.where(lane == 3 * k + j, offsets_ref[j, k].astype(F32), shifts)
    rows = []
    for z in range(16):
        rows += [inside[z // 2 : z // 2 + 1], shifts]
    moments_ref[:, 32] = jnp.concatenate(rows, axis=0).astype(BF).reshape(16, 2, 128)


def regroup_kernel(place_ref, got_ref, out_ref, offsets_ref):
    quarter, half, shard = place_ref[0], place_ref[1], place_ref[2]
    for z in range(16):
        out_ref[:, z] = got_ref[z, 0:32]
    extra = got_ref[:, 32].reshape(32, 128)
    row, lane = iota((32, 128), 0), iota((32, 128), 1)
    take_row, take_lane = iota((64, 128), 0), iota((64, 128), 1)
    ids = jnp.zeros((64, 128), F32)
    for i in range(2):
        put = mask((row % 2 == 0) & (lane - 32 * quarter == row + i))
        take = mask((take_row % 2 == 0) & (take_lane == 64 * half + take_row + i))
        moved = dot(extra, put.astype(BF), ((0,), (0,)))
        ids = ids + dot(take.astype(BF), moved.astype(BF))
    out_ref[:, 16] = ids.astype(BF).reshape(32, 2, 128)
    out_ref[:, 17:24] = jnp.zeros((32, 7, 2, 128), BF)
    own = jnp.sum(mask(row == 2 * shard + 1) * extra.astype(F32), axis=0, keepdims=True)
    offsets_ref[...] = jnp.broadcast_to(own, (8, 128)).astype(jnp.int32)


def sum_kernel(got_ref, cells_ref, ids_ref):
    cell = iota((128, 128), 0)
    total = jnp.zeros((128, 128), F32)
    for four in range(8):
        blocks = [got_ref[4 * four + j] for j in range(4)]
        ids = sum(block[32:48].astype(F32) for block in blocks)[0:1]
        ids_ref[four : four + 1, :] = ids
        hot = mask(ids.astype(jnp.int32) == cell).astype(BF)
        total = total + dot(hot, jnp.concatenate([block[0:32] for block in blocks], axis=0))
    cells = total.astype(BF)
    for peer in range(cells_ref.shape[0]):
        cells_ref[peer] = cells


def m2l_kernel(offsets_ref, ops_ref, own_ref, low_ref, high_ref, out_ref, rows, shifted):
    shifted[:, :, 0:3] = jnp.zeros((6, 9, 3, GY, 128), BF)
    shifted[:, :, 11:13] = jnp.zeros((6, 9, 2, GY, 128), BF)
    rows[:, 0:8, :] = jnp.zeros((GX, 8, 128), F32)
    rows[:, 40:48, :] = jnp.zeros((GX, 8, 128), F32)
    for plane in range(9):
        ref, at = (low_ref, plane) if plane < 3 else (own_ref, plane - 3) if plane < 7 else (high_ref, plane - 7)
        rows[:, 8:40, :] = ref[at * 256 : (at + 1) * 256, :].astype(F32).reshape(GX, GY, 128)
        for dy in range(6):
            shifted[dy, plane, 3:11] = rows[:, 5 + dy : 37 + dy, :].astype(BF)
    ops = ops_ref[...].reshape(16 * 128, 128)
    for z in range(CZS):
        windows = []
        for k in range(16):
            dz, dx, dy = offsets_ref[0, 3 * k], offsets_ref[0, 3 * k + 1], offsets_ref[0, 3 * k + 2]
            window = shifted[dy + 3, dz + (3 + z), pl.ds(dx + 3, GX)]
            windows.append(window.reshape(GX * GY, 128))
        total = jnp.dot(jnp.concatenate(windows, axis=1), ops, preferred_element_type=F32)
        out_ref[z * 256 : (z + 1) * 256, :] = total.astype(BF)


def pick_kernel(ids_ref, parts_ref, out_ref):
    local = parts_ref[0].astype(F32)
    for peer in range(1, parts_ref.shape[0]):
        local = local + parts_ref[peer].astype(F32)
    local = local.astype(BF)
    cell = iota((128, 128), 0)
    for four in range(8):
        hot = mask(ids_ref[four : four + 1, :].astype(jnp.int32) == cell).astype(BF)
        out_ref[128 * four : 128 * four + 128, :] = dot(hot, local, ((0,), (0,))).astype(BF)


def return_kernel(got_ref, out_ref):
    for z in range(16):
        out_ref[z] = got_ref[:, z]


def field_kernel(rows_ref, picked_ref, out_ref):
    to, at = iota((128, 256), 0), iota((128, 256), 1)
    part = mask(at == 2 * to + 1).astype(BF)
    ones = jnp.ones((8, 128), BF)
    for k in range(8):
        basis = dot(part, rows_ref[256 * k : 256 * k + 256, :])
        product = basis * picked_ref[128 * k : 128 * k + 128, :].astype(F32)
        high = product.astype(BF)
        low = (product - high.astype(F32)).astype(BF)
        field = dot(ones, high, ((1,), (1,))) + dot(ones, low, ((1,), (1,)))
        out_ref[k : k + 1, :] = field[0:1] * (128 ** -0.5)


def ops_moves():
    moves = []
    for z in range(16):
        for a in range(8):
            d = (a - z) % 8
            d = d - 8 if d > 4 else d
            moves.append((spot((z + d) % 16, (a + z) % 8), spot(z, a)))
    return moves


def spot(z, a):
    return (z // 8 * 8 + a) * 8 + z % 8


def slab_spot(s):
    return s % 4 * 16 + s // 4


def call(kernel, out_shape, in_specs, scratch=()):
    many = isinstance(out_shape, list)
    return pl.pallas_call(
        kernel,
        out_shape=out_shape,
        in_specs=in_specs,
        out_specs=[VMEM] * len(out_shape) if many else VMEM,
        scratch_shapes=list(scratch),
        compiler_params=pltpu.CompilerParams(vmem_limit_bytes=40 * 1024 * 1024),
    )


def shape(*size, kind=BF):
    return jax.ShapeDtypeStruct(size, kind)


def exchange(array, axes):
    return lax.all_to_all(array, axes, split_axis=0, concat_axis=0, tiled=True)


def body(bead_data, bead_cell, m2l_ops, offsets):
    shard = lax.axis_index("y") * 2 + lax.axis_index("c")
    place = jnp.stack([shard % 4, lax.axis_index("zl") % 2, shard])

    rows = bead_data.reshape(2048, 128)
    moments = call(pack_kernel, shape(16, 33, 2, 128), [SMEM, VMEM, VMEM])(
        offsets.T, rows, bead_cell.reshape(8, 128)
    )
    moments = exchange(moments.reshape(528, 2, 128), COLUMN)
    m2l_ops, moments = lax.optimization_barrier((m2l_ops, moments))
    moments, shifts = call(
        regroup_kernel, [shape(32, 24, 2, 128), shape(8, 128, kind=jnp.int32)], [SMEM, VMEM]
    )(place, moments.reshape(16, 33, 2, 128))
    moments = exchange(moments.reshape(768, 2, 128), LAYER).reshape(32, 48, 128)
    ops = lax.ppermute(m2l_ops, ("zh", "y", "c", "zl"), ops_moves())
    cells, ids = call(sum_kernel, [shape(8, 128, 128), shape(8, 128, kind=F32)], [VMEM])(moments)
    slab = exchange(cells, GROUP).reshape(1024, 128)
    low = lax.ppermute(slab[256:], SLABS, [(slab_spot(i), slab_spot(i + 1)) for i in range(63)])
    high = lax.ppermute(slab[:512], SLABS, [(slab_spot(i + 1), slab_spot(i)) for i in range(63)])
    parts = call(
        m2l_kernel,
        shape(1024, 128),
        [SMEM, VMEM, VMEM, VMEM, VMEM],
        [pltpu.VMEM((GX, 48, 128), F32), pltpu.VMEM((6, 9, 13, GY, 128), BF)],
    )(shifts, ops, slab, low, high)
    parts = exchange(parts.reshape(8, 128, 128), GROUP)
    picked = call(pick_kernel, shape(1024, 128), [VMEM, VMEM])(ids, parts)
    picked = exchange(picked.reshape(512, 2, 128), LAYER)
    picked = call(return_kernel, shape(16, 32, 2, 128), [VMEM])(picked.reshape(32, 16, 2, 128))
    picked = exchange(picked.reshape(512, 2, 128), COLUMN).reshape(1024, 128)
    return call(field_kernel, shape(8, 128, kind=F32), [VMEM, VMEM])(rows, picked).reshape(1024)


def solution(mesh):
    fine = Mesh(mesh.devices.reshape(4, 2, 4, 2, 8), ("x", "zh", "y", "c", "zl"))
    every = ("x", "zh", "y", "c", "zl")
    in_specs = (P(every, None, None), P(every), P("zl", None, None), P("zl", None))
    return jax.shard_map(body, mesh=fine, in_specs=in_specs, out_specs=P(every), check_vma=False)
```

time: 146 us -> 140 us (0.959)
  the two profiles are of different devices: /device:TPU:1 before, /device:TPU:32 now
where the time goes in v3:
time: 140 us; the launch traced here: 139 us
  blocking collectives  67.5 us (48%)
  starting transfers between devices  36.4 us (26%)
  waiting for transfers between devices  24.4 us (17%)
  Pallas kernels  8.12 us (6%)
  local copies, waits for them, and re-layouts  2.44 us (2%)
    all_to_all x4, blocking collectives, exchange(): return lax.all_to_all(array, axes, split_axis=0, concat_axis=0, tiled=True)  67.5 us
    all_to_all x2, starting transfers between devices, exchange(): return lax.all_to_all(array, axes, split_axis=0, concat_axis=0, tiled=True)  22.5 us
    all_to_all x2, waiting for transfers between devices, exchange(): return lax.all_to_all(array, axes, split_axis=0, concat_axis=0, tiled=True)  21.9 us
    ppermute x1, starting transfers between devices, body(): ops = lax.ppermute(m2l_ops, ('zh', 'y', 'c', 'zl'), ops_moves())  5.91 us
    ppermute x1, starting transfers between devices, body(): lax.ppermute(slab[:512], SLABS, [(slab_spot(i + 1), slab_spot(i)) for i i...  5.43 us
  transfers between devices with their start and end apart: 5, of which 3 were waited for; matrix products, arithmetic and copies ran while one was open for 0% of the time, Pallas kernels for 0%

profile of v3, /device:TPU:32, one launch (start us, length us, event | category | flops | bytes accessed | tf_op | source)
XLA Modules:
  0.0 139.1 jit_solution(17003633007298555544)
XLA Ops:
  0.0 0.7 copy-done.2
  0.7 1.0 copy-done
  1.7 0.7 copy-done.3
  2.4 1.6 %shard_map.46 = bf16[16,33,2,128]{3,2,1,0:T(2,128)(2,1)} custom-call(s32[3,16]{1,0:T(4,128)S(1)} %bitcast.30, bf16[2048,128]{1,0:T(8,128)(2,1)S(1)} %bitcast.20, s32[8,128]{1,0:T(8,128)S(1)} %bitcast.29), custom_call_target="tpu_custom_call" | custom-call | tf_op jit(solution)/shard_map/pallas_call | solution.py:181
  4.0 15.2 %all-to-all-start = ((bf16[528,2,128]{2,1,0:T(2,128)(2,1)}), bf16[528,2,128]{2,1,0:T(2,128)(2,1)S(1)}, u32[]{:S(2)}, u32[]{:S(2)}) async-start(bf16[528,2,128]{2,1,0:T(2,128)(2,1)} %bitcast.6), calls=%async_computation | async-start | bytes 540672 | tf_op jit(solution)/shard_map/all_to_all | solution.py:173
  19.2 0.1 pad_add_fusion.place_ref
  19.3 17.9 %all-to-all-done = bf16[528,2,128]{2,1,0:T(2,128)(2,1)S(1)} async-done(((bf16[528,2,128]{2,1,0:T(2,128)(2,1)}), bf16[528,2,128]{2,1,0:T(2,128)(2,1)S(1)}, u32[]{:S(2)}, u32[]{:S(2)}) %all-to-all-start) | async-done | bytes 270368 | tf_op jit(solution)/shard_map/all_to_all | solution.py:173
  37.2 1.7 %shard_map.47 = (bf16[32,24,2,128]{3,2,1,0:T(2,128)(2,1)}, s32[8,128]{1,0:T(8,128)S(1)}) custom-call(s32[3]{0:T(128)S(1)} %pad_add_fusion.place_ref, bf16[16,33,2,128]{3,2,1,0:T(2,128)(2,1)S(1)} %bitcast.23), custom_call_target="tpu_custom_call" | custom-call | tf_op jit(solution)/shard_map/pallas_call | solution.py:186
  38.9 7.3 %all-to-all-start.1 = ((bf16[768,2,128]{2,1,0:T(2,128)(2,1)}), bf16[768,2,128]{2,1,0:T(2,128)(2,1)S(1)}, u32[]{:S(2)}, u32[]{:S(2)}) async-start(bf16[768,2,128]{2,1,0:T(2,128)(2,1)} %bitcast.8), calls=%async_computation.1 | async-start | bytes 786432 | tf_op jit(solution)/shard_map/all_to_all | solution.py:173
  46.2 5.9 %collective-permute-start = (bf16[16,128,128]{2,1,0:T(8,128)(2,1)S(1)}, bf16[16,128,128]{2,1,0:T(8,128)(2,1)S(1)}, u32[]{:S(2)}, u32[]{:S(2)}) collective-permute-start(bf16[16,128,128]{2,1,0:T(8,128)(2,1)S(1)} %copy-done.4), channel_id=1, source_target_pairs={{0,0},{9,8},{18,16},{27,24},{36,32},{109,40},{118,48},{127,56},{8,... | collective-permute-start | bytes 1572872 | tf_op jit(solution)/shard_map/ppermute | solution.py:190
  52.2 4.0 %all-to-all-done.1 = bf16[768,2,128]{2,1,0:T(2,128)(2,1)S(1)} async-done(((bf16[768,2,128]{2,1,0:T(2,128)(2,1)}), bf16[768,2,128]{2,1,0:T(2,128)(2,1)S(1)}, u32[]{:S(2)}, u32[]{:S(2)}) %all-to-all-start.1) | async-done | bytes 393248 | tf_op jit(solution)/shard_map/all_to_all | solution.py:173
  56.2 0.2 shard_map.48
  56.4 10.2 %all_to_all.30 = bf16[8,128,128]{2,1,0:T(8,128)(2,1)S(1)} all-to-all(bf16[8,128,128]{2,1,0:T(8,128)(2,1)S(1)} %get-tuple-element.16), channel_id=1, replica_groups=mesh['x'=4,'zh'=2,'y'=4,'c'=2,'zl'=8] {'y','c'}, dimensions={0} | all-to-all | bytes 524288 | tf_op jit(solution)/shard_map/all_to_all | solution.py:173
  66.7 2.5 %collective-permute-start.1 = (bf16[768,128]{1,0:T(8,128)(2,1)S(1)}, bf16[768,128]{1,0:T(8,128)(2,1)S(1)}, u32[]{:S(2)}, u32[]{:S(2)}) collective-permute-start(bf16[768,128]{1,0:T(8,128)(2,1)S(1)} %bitcast.31), channel_id=1, source_target_pairs={{0,128},{128,256},{256,384},{384,1},{1,129},{129,257},{257,385},{3... | collective-permute-start | bytes 589832 | tf_op jit(solution)/shard_map/ppermute | solution.py:193
  69.2 5.4 %collective-permute-start.2 = (bf16[512,128]{1,0:T(8,128)(2,1)S(1)}, bf16[512,128]{1,0:T(8,128)(2,1)S(1)}, u32[]{:S(2)}, u32[]{:S(2)}) collective-permute-start(bf16[512,128]{1,0:T(8,128)(2,1)S(1)} %bitcast.32), channel_id=1, source_target_pairs={{128,0},{256,128},{384,256},{1,384},{129,1},{257,129},{385,257},{2... | collective-permute-start | bytes 393224 | tf_op jit(solution)/shard_map/ppermute | solution.py:194
  74.7 0.0 collective-permute-done.ops_ref
  74.7 2.5 %collective-permute-done.2.high_ref = bf16[512,128]{1,0:T(8,128)(2,1)S(1)} collective-permute-done((bf16[512,128]{1,0:T(8,128)(2,1)S(1)}, bf16[512,128]{1,0:T(8,128)(2,1)S(1)}, u32[]{:S(2)}, u32[]{:S(2)}) %collective-permute-start.2) | collective-permute-done | bytes 131104 | tf_op jit(solution)/shard_map/ppermute | solution.py:194
  77.2 2.6 %shard_map.49 = bf16[1024,128]{1,0:T(8,128)(2,1)S(1)} custom-call(s32[8,128]{1,0:T(8,128)S(1)} %get-tuple-element.14.offsets_ref, bf16[16,128,128]{2,1,0:T(8,128)(2,1)S(1)} %collective-permute-done.ops_ref, bf16[1024,128]{1,0:T(8,128)(2,1)S(1)} %bitcast.19, bf16[768,128]{1,0:T(8,128)(2,1)S(1)} %collective-permute-done.1.low_ref, ...), custom_call_target="tpu_custom_call" | custom-call | tf_op jit(solution)/shard_map/pallas_call | solution.py:195
  79.7 12.0 %all_to_all.31.parts_ref = bf16[8,128,128]{2,1,0:T(8,128)(2,1)S(1)} all-to-all(bf16[8,128,128]{2,1,0:T(8,128)(2,1)S(1)} %bitcast.28), channel_id=1, replica_groups=mesh['x'=4,'zh'=2,'y'=4,'c'=2,'zl'=8] {'y','c'}, dimensions={0} | all-to-all | bytes 524288 | tf_op jit(solution)/shard_map/all_to_all | solution.py:173
  91.7 0.3 shard_map.50
  92.0 20.0 %all_to_all.32 = bf16[512,2,128]{2,1,0:T(2,128)(2,1)S(1)} all-to-all(bf16[512,2,128]{2,1,0:T(2,128)(2,1)S(1)} %bitcast.25), channel_id=1, replica_groups=mesh['x'=4,'zh'=2,'y'=4,'c'=2,'zl'=8] {'x','y','c'}, dimensions={0} | all-to-all | bytes 524288 | tf_op jit(solution)/shard_map/all_to_all | solution.py:173
  112.0 0.2 shard_map.51
  112.2 25.3 %all_to_all.33 = bf16[512,2,128]{2,1,0:T(2,128)(2,1)S(1)} all-to-all(bf16[512,2,128]{2,1,0:T(2,128)(2,1)S(1)} %bitcast.27), channel_id=1, replica_groups=mesh['x'=4,'zh'=2,'y'=4,'c'=2,'zl'=8] {'zh','zl'}, dimensions={0} | all-to-all | bytes 524288 | tf_op jit(solution)/shard_map/all_to_all | solution.py:173
  137.5 1.6 %shard_map.52 = f32[8,128]{1,0:T(8,128)} custom-call(bf16[2048,128]{1,0:T(8,128)(2,1)S(1)} %bitcast.21, bf16[1024,128]{1,0:T(8,128)(2,1)S(1)} %bitcast.24), custom_call_target="tpu_custom_call" | custom-call | tf_op jit(solution)/shard_map/pallas_call | solution.py:206
  (10 shorter events, 0.0 us)
Async XLA Ops:
  0.0 0.7 copy-start.2
  0.7 1.0 copy-start
  1.7 0.7 copy-start.3
  4.0 33.2 %all-to-all-start = ((bf16[528,2,128]{2,1,0:T(2,128)(2,1)}), bf16[528,2,128]{2,1,0:T(2,128)(2,1)S(1)}, u32[]{:S(2)}, u32[]{:S(2)}) async-start(bf16[528,2,128]{2,1,0:T(2,128)(2,1)} %bitcast.6), calls=%async_computation | async-start | bytes 540672 | tf_op jit(solution)/shard_map/all_to_all | solution.py:173
  37.2 9.0 %copy-start.4 = (bf16[16,128,128]{2,1,0:T(8,128)(2,1)S(1)}, bf16[16,128,128]{2,1,0:T(8,128)(2,1)}, u32[]{:S(2)}) copy-start(bf16[16,128,128]{2,1,0:T(8,128)(2,1)} %param.6) | copy-start | bytes 1572868
  38.9 17.3 %all-to-all-start.1 = ((bf16[768,2,128]{2,1,0:T(2,128)(2,1)}), bf16[768,2,128]{2,1,0:T(2,128)(2,1)S(1)}, u32[]{:S(2)}, u32[]{:S(2)}) async-start(bf16[768,2,128]{2,1,0:T(2,128)(2,1)} %bitcast.8), calls=%async_computation.1 | async-start | bytes 786432 | tf_op jit(solution)/shard_map/all_to_all | solution.py:173
  46.2 28.4 %collective-permute-start = (bf16[16,128,128]{2,1,0:T(8,128)(2,1)S(1)}, bf16[16,128,128]{2,1,0:T(8,128)(2,1)S(1)}, u32[]{:S(2)}, u32[]{:S(2)}) collective-permute-start(bf16[16,128,128]{2,1,0:T(8,128)(2,1)S(1)} %copy-done.4), channel_id=1, source_target_pairs={{0,0},{9,8},{18,16},{27,24},{36,32},{109,40},{118,48},{127,56},{8,... | collective-permute-start | bytes 1572872 | tf_op jit(solution)/shard_map/ppermute | solution.py:190
  66.7 10.5 %collective-permute-start.1 = (bf16[768,128]{1,0:T(8,128)(2,1)S(1)}, bf16[768,128]{1,0:T(8,128)(2,1)S(1)}, u32[]{:S(2)}, u32[]{:S(2)}) collective-permute-start(bf16[768,128]{1,0:T(8,128)(2,1)S(1)} %bitcast.31), channel_id=1, source_target_pairs={{0,128},{128,256},{256,384},{384,1},{1,129},{129,257},{257,385},{3... | collective-permute-start | bytes 589832 | tf_op jit(solution)/shard_map/ppermute | solution.py:193
  69.2 7.9 %collective-permute-start.2 = (bf16[512,128]{1,0:T(8,128)(2,1)S(1)}, bf16[512,128]{1,0:T(8,128)(2,1)S(1)}, u32[]{:S(2)}, u32[]{:S(2)}) collective-permute-start(bf16[512,128]{1,0:T(8,128)(2,1)S(1)} %bitcast.32), channel_id=1, source_target_pairs={{128,0},{256,128},{384,256},{1,384},{129,1},{257,129},{385,257},{2... | collective-permute-start | bytes 393224 | tf_op jit(solution)/shard_map/ppermute | solution.py:194
  112.0 25.5 %copy-start.1 = (bf16[1024,2,128]{2,1,0:T(2,128)(2,1)S(1)}, bf16[1024,2,128]{2,1,0:T(2,128)(2,1)}, u32[]{:S(2)}) copy-start(bf16[1024,2,128]{2,1,0:T(2,128)(2,1)} %param.4) | copy-start | bytes 1572868

commit v4 on v3

--- a/solution.py
+++ b/solution.py
@@ -135,14 +135,11 @@
         out_ref[k : k + 1, :] = field[0:1] * (128 ** -0.5)
 
 
+REACH = (0, 4, 1, -1, 2, -2, 3, -3)
+
+
 def ops_moves():
-    moves = []
-    for z in range(16):
-        for a in range(8):
-            d = (a - z) % 8
-            d = d - 8 if d > 4 else d
-            moves.append((spot((z + d) % 16, (a + z) % 8), spot(z, a)))
-    return moves
+    return [(spot((z + REACH[a]) % 16, a), spot(z, a)) for z in range(16) for a in range(8)]
 
 
 def spot(z, a):
@@ -174,8 +171,10 @@
 
 
 def body(bead_data, bead_cell, m2l_ops, offsets):
-    shard = lax.axis_index("y") * 2 + lax.axis_index("c")
-    place = jnp.stack([shard % 4, lax.axis_index("zl") % 2, shard])
+    peer = lax.axis_index("y") * 2 + lax.axis_index("c")
+    layer = lax.axis_index("zl")
+    shard = (layer + 8 + jnp.array(REACH, jnp.int32)[peer]) % 8
+    place = jnp.stack([peer % 4, layer % 2, shard])
 
     rows = bead_data.reshape(2048, 128)
     moments = call(pack_kernel, shape(16, 33, 2, 128), [SMEM, VMEM, VMEM])(

time: 140 us -> 134 us (0.957)
  blocking collectives: 67.5 us -> 61.7 us
  starting transfers between devices: 36.4 us -> 31.2 us
  waiting for transfers between devices: 24.4 us -> 28.4 us
    all_to_all x4, blocking collectives: 67.5 us -> 61.7 us  [exchange(): return lax.all_to_all(array, axes, split_axis=0, concat_axis=0, tiled=True)]
    ppermute x1, starting transfers between devices: 5.91 us -> 0.69 us  [body(): ops = lax.ppermute(m2l_ops, ('zh', 'y', 'c', 'zl'), ops_moves())]
    all_to_all x2, waiting for transfers between devices: 21.9 us -> 25.2 us  [exchange(): return lax.all_to_all(array, axes, split_axis=0, concat_axis=0, tiled=True)]
    unnamed x10 -> x12, local copies, waits for them, and re-layouts: 2.42 us -> 3.06 us
  transfers between devices with their start and end apart: 5 -> 5, of which waited for: 3 -> 3; matrix products, arithmetic and copies ran while one was open for 0% -> 1% of each run, Pallas kernels for 0% -> 0%
where the time goes in v4:
time: 134 us
  blocking collectives  61.7 us (46%)
  starting transfers between devices  31.2 us (23%)
  waiting for transfers between devices  28.4 us (21%)
  Pallas kernels  8.11 us (6%)
  local copies, waits for them, and re-layouts  3.67 us (3%)
    all_to_all x4, blocking collectives, exchange(): return lax.all_to_all(array, axes, split_axis=0, concat_axis=0, tiled=True)  61.7 us
    all_to_all x2, waiting for transfers between devices, exchange(): return lax.all_to_all(array, axes, split_axis=0, concat_axis=0, tiled=True)  25.2 us
    all_to_all x2, starting transfers between devices, exchange(): return lax.all_to_all(array, axes, split_axis=0, concat_axis=0, tiled=True)  22.5 us
    ppermute x1, starting transfers between devices, body(): lax.ppermute(slab[:512], SLABS, [(slab_spot(i + 1), slab_spot(i)) for i i...  5.43 us
    ppermute x1, waiting for transfers between devices, body(): lax.ppermute(slab[:512], SLABS, [(slab_spot(i + 1), slab_spot(i)) for i i...  3.21 us
    unnamed x12, local copies, waits for them, and re-layouts  3.06 us
  transfers between devices with their start and end apart: 5, of which 3 were waited for; matrix products, arithmetic and copies ran while one was open for 1% of the time, Pallas kernels for 0%

profile of v4, /device:TPU:32, one launch (start us, length us, event | category | flops | bytes accessed | tf_op | source)
XLA Modules:
  0.0 133.9 jit_solution(2818277080240925893)
XLA Ops:
  0.0 0.7 copy-done.2
  0.7 1.0 copy-done
  1.7 0.7 copy-done.3
  2.4 1.6 %shard_map.55 = bf16[16,33,2,128]{3,2,1,0:T(2,128)(2,1)} custom-call(s32[3,16]{1,0:T(4,128)S(1)} %bitcast.31, bf16[2048,128]{1,0:T(8,128)(2,1)S(1)} %bitcast.21, s32[8,128]{1,0:T(8,128)S(1)} %bitcast.30), custom_call_target="tpu_custom_call" | custom-call | tf_op jit(solution)/shard_map/pallas_call | solution.py:180
  4.0 15.2 %all-to-all-start = ((bf16[528,2,128]{2,1,0:T(2,128)(2,1)}), bf16[528,2,128]{2,1,0:T(2,128)(2,1)S(1)}, u32[]{:S(2)}, u32[]{:S(2)}) async-start(bf16[528,2,128]{2,1,0:T(2,128)(2,1)} %bitcast.7), calls=%async_computation | async-start | bytes 540672 | tf_op jit(solution)/shard_map/all_to_all | solution.py:170
  19.2 0.6 copy-done.5
  19.9 0.6 dynamic_slice.3
  21.2 16.0 %all-to-all-done = bf16[528,2,128]{2,1,0:T(2,128)(2,1)S(1)} async-done(((bf16[528,2,128]{2,1,0:T(2,128)(2,1)}), bf16[528,2,128]{2,1,0:T(2,128)(2,1)S(1)}, u32[]{:S(2)}, u32[]{:S(2)}) %all-to-all-start) | async-done | bytes 270368 | tf_op jit(solution)/shard_map/all_to_all | solution.py:170
  37.2 1.7 %shard_map.56 = (bf16[32,24,2,128]{3,2,1,0:T(2,128)(2,1)}, s32[8,128]{1,0:T(8,128)S(1)}) custom-call(s32[3]{0:T(128)S(1)} %pad_add_fusion.place_ref, bf16[16,33,2,128]{3,2,1,0:T(2,128)(2,1)S(1)} %bitcast.24), custom_call_target="tpu_custom_call" | custom-call | tf_op jit(solution)/shard_map/pallas_call | solution.py:185
  38.9 7.3 %all-to-all-start.1 = ((bf16[768,2,128]{2,1,0:T(2,128)(2,1)}), bf16[768,2,128]{2,1,0:T(2,128)(2,1)S(1)}, u32[]{:S(2)}, u32[]{:S(2)}) async-start(bf16[768,2,128]{2,1,0:T(2,128)(2,1)} %bitcast.9), calls=%async_computation.1 | async-start | bytes 786432 | tf_op jit(solution)/shard_map/all_to_all | solution.py:170
  46.2 0.7 collective-permute-start
  46.9 9.2 %all-to-all-done.1 = bf16[768,2,128]{2,1,0:T(2,128)(2,1)S(1)} async-done(((bf16[768,2,128]{2,1,0:T(2,128)(2,1)}), bf16[768,2,128]{2,1,0:T(2,128)(2,1)S(1)}, u32[]{:S(2)}, u32[]{:S(2)}) %all-to-all-start.1) | async-done | bytes 393248 | tf_op jit(solution)/shard_map/all_to_all | solution.py:170
  56.2 0.2 shard_map.57
  56.4 10.2 %all_to_all.30 = bf16[8,128,128]{2,1,0:T(8,128)(2,1)S(1)} all-to-all(bf16[8,128,128]{2,1,0:T(8,128)(2,1)S(1)} %get-tuple-element.16), channel_id=1, replica_groups=mesh['x'=4,'zh'=2,'y'=4,'c'=2,'zl'=8] {'y','c'}, dimensions={0} | all-to-all | bytes 524288 | tf_op jit(solution)/shard_map/all_to_all | solution.py:170
  66.7 2.5 %collective-permute-start.1 = (bf16[768,128]{1,0:T(8,128)(2,1)S(1)}, bf16[768,128]{1,0:T(8,128)(2,1)S(1)}, u32[]{:S(2)}, u32[]{:S(2)}) collective-permute-start(bf16[768,128]{1,0:T(8,128)(2,1)S(1)} %bitcast.32), channel_id=1, source_target_pairs={{0,128},{128,256},{256,384},{384,1},{1,129},{129,257},{257,385},{3... | collective-permute-start | bytes 589832 | tf_op jit(solution)/shard_map/ppermute | solution.py:192
  69.2 5.4 %collective-permute-start.2 = (bf16[512,128]{1,0:T(8,128)(2,1)S(1)}, bf16[512,128]{1,0:T(8,128)(2,1)S(1)}, u32[]{:S(2)}, u32[]{:S(2)}) collective-permute-start(bf16[512,128]{1,0:T(8,128)(2,1)S(1)} %bitcast.33), channel_id=1, source_target_pairs={{128,0},{256,128},{384,256},{1,384},{129,1},{257,129},{385,257},{2... | collective-permute-start | bytes 393224 | tf_op jit(solution)/shard_map/ppermute | solution.py:193
  74.7 3.2 %collective-permute-done.2.high_ref = bf16[512,128]{1,0:T(8,128)(2,1)S(1)} collective-permute-done((bf16[512,128]{1,0:T(8,128)(2,1)S(1)}, bf16[512,128]{1,0:T(8,128)(2,1)S(1)}, u32[]{:S(2)}, u32[]{:S(2)}) %collective-permute-start.2) | collective-permute-done | bytes 131104 | tf_op jit(solution)/shard_map/ppermute | solution.py:193
  77.9 2.6 %shard_map.58 = bf16[1024,128]{1,0:T(8,128)(2,1)S(1)} custom-call(s32[8,128]{1,0:T(8,128)S(1)} %get-tuple-element.14.offsets_ref, bf16[16,128,128]{2,1,0:T(8,128)(2,1)S(1)} %collective-permute-done.ops_ref, bf16[1024,128]{1,0:T(8,128)(2,1)S(1)} %bitcast.20, bf16[768,128]{1,0:T(8,128)(2,1)S(1)} %collective-permute-done.1.low_ref, ...), custom_call_target="tpu_custom_call" | custom-call | tf_op jit(solution)/shard_map/pallas_call | solution.py:194
  80.4 10.9 %all_to_all.31.parts_ref = bf16[8,128,128]{2,1,0:T(8,128)(2,1)S(1)} all-to-all(bf16[8,128,128]{2,1,0:T(8,128)(2,1)S(1)} %bitcast.29), channel_id=1, replica_groups=mesh['x'=4,'zh'=2,'y'=4,'c'=2,'zl'=8] {'y','c'}, dimensions={0} | all-to-all | bytes 524288 | tf_op jit(solution)/shard_map/all_to_all | solution.py:170
  91.4 0.3 shard_map.59
  91.7 14.4 %all_to_all.32 = bf16[512,2,128]{2,1,0:T(2,128)(2,1)S(1)} all-to-all(bf16[512,2,128]{2,1,0:T(2,128)(2,1)S(1)} %bitcast.26), channel_id=1, replica_groups=mesh['x'=4,'zh'=2,'y'=4,'c'=2,'zl'=8] {'x','y','c'}, dimensions={0} | all-to-all | bytes 524288 | tf_op jit(solution)/shard_map/all_to_all | solution.py:170
  106.0 0.2 shard_map.60
  106.2 26.1 %all_to_all.33 = bf16[512,2,128]{2,1,0:T(2,128)(2,1)S(1)} all-to-all(bf16[512,2,128]{2,1,0:T(2,128)(2,1)S(1)} %bitcast.28), channel_id=1, replica_groups=mesh['x'=4,'zh'=2,'y'=4,'c'=2,'zl'=8] {'zh','zl'}, dimensions={0} | all-to-all | bytes 524288 | tf_op jit(solution)/shard_map/all_to_all | solution.py:170
  132.3 1.6 %shard_map.61 = f32[8,128]{1,0:T(8,128)} custom-call(bf16[2048,128]{1,0:T(8,128)(2,1)S(1)} %bitcast.22, bf16[1024,128]{1,0:T(8,128)(2,1)S(1)} %bitcast.25), custom_call_target="tpu_custom_call" | custom-call | tf_op jit(solution)/shard_map/pallas_call | solution.py:205
  (13 shorter events, 0.1 us)
Async XLA Ops:
  0.0 0.7 copy-start.2
  0.7 1.0 copy-start
  1.7 0.7 copy-start.3
  4.0 33.2 %all-to-all-start = ((bf16[528,2,128]{2,1,0:T(2,128)(2,1)}), bf16[528,2,128]{2,1,0:T(2,128)(2,1)S(1)}, u32[]{:S(2)}, u32[]{:S(2)}) async-start(bf16[528,2,128]{2,1,0:T(2,128)(2,1)} %bitcast.7), calls=%async_computation | async-start | bytes 540672 | tf_op jit(solution)/shard_map/all_to_all | solution.py:170
  19.2 0.7 copy-start.5
  37.2 9.0 %copy-start.4 = (bf16[16,128,128]{2,1,0:T(8,128)(2,1)S(1)}, bf16[16,128,128]{2,1,0:T(8,128)(2,1)}, u32[]{:S(2)}) copy-start(bf16[16,128,128]{2,1,0:T(8,128)(2,1)} %param.7) | copy-start | bytes 1572868
  38.9 17.3 %all-to-all-start.1 = ((bf16[768,2,128]{2,1,0:T(2,128)(2,1)}), bf16[768,2,128]{2,1,0:T(2,128)(2,1)S(1)}, u32[]{:S(2)}, u32[]{:S(2)}) async-start(bf16[768,2,128]{2,1,0:T(2,128)(2,1)} %bitcast.9), calls=%async_computation.1 | async-start | bytes 786432 | tf_op jit(solution)/shard_map/all_to_all | solution.py:170
  46.2 28.4 %collective-permute-start = (bf16[16,128,128]{2,1,0:T(8,128)(2,1)S(1)}, bf16[16,128,128]{2,1,0:T(8,128)(2,1)S(1)}, u32[]{:S(2)}, u32[]{:S(2)}) collective-permute-start(bf16[16,128,128]{2,1,0:T(8,128)(2,1)S(1)} %copy-done.4), channel_id=1, source_target_pairs={{0,0},{12,8},{17,16},{95,24},{34,32},{110,40},{51,48},{125,56},{1,... | collective-permute-start | bytes 1572872 | tf_op jit(solution)/shard_map/ppermute | solution.py:189
  66.7 11.2 %collective-permute-start.1 = (bf16[768,128]{1,0:T(8,128)(2,1)S(1)}, bf16[768,128]{1,0:T(8,128)(2,1)S(1)}, u32[]{:S(2)}, u32[]{:S(2)}) collective-permute-start(bf16[768,128]{1,0:T(8,128)(2,1)S(1)} %bitcast.32), channel_id=1, source_target_pairs={{0,128},{128,256},{256,384},{384,1},{1,129},{129,257},{257,385},{3... | collective-permute-start | bytes 589832 | tf_op jit(solution)/shard_map/ppermute | solution.py:192
  69.2 8.7 %collective-permute-start.2 = (bf16[512,128]{1,0:T(8,128)(2,1)S(1)}, bf16[512,128]{1,0:T(8,128)(2,1)S(1)}, u32[]{:S(2)}, u32[]{:S(2)}) collective-permute-start(bf16[512,128]{1,0:T(8,128)(2,1)S(1)} %bitcast.33), channel_id=1, source_target_pairs={{128,0},{256,128},{384,256},{1,384},{129,1},{257,129},{385,257},{2... | collective-permute-start | bytes 393224 | tf_op jit(solution)/shard_map/ppermute | solution.py:193
  106.0 26.3 %copy-start.1 = (bf16[1024,2,128]{2,1,0:T(2,128)(2,1)S(1)}, bf16[1024,2,128]{2,1,0:T(2,128)(2,1)}, u32[]{:S(2)}) copy-start(bf16[1024,2,128]{2,1,0:T(2,128)(2,1)} %param.5) | copy-start | bytes 1572868

commit v5 on v4

--- a/solution.py
+++ b/solution.py
@@ -52,8 +52,13 @@
     moments_ref[:, 32] = jnp.concatenate(rows, axis=0).astype(BF).reshape(16, 2, 128)
 
 
-def regroup_kernel(place_ref, got_ref, out_ref, offsets_ref):
-    quarter, half, shard = place_ref[0], place_ref[1], place_ref[2]
+def regroup_kernel(got_ref, out_ref, offsets_ref):
+    peer, layer = lax.axis_index("y") * 2 + lax.axis_index("c"), lax.axis_index("zl")
+    quarter, half = lax.rem(peer, 4), lax.rem(layer, 2)
+    reach = jnp.int32(0)
+    for a in range(8):
+        reach = jnp.where(peer == a, REACH[a] % 8, reach)
+    shard = lax.rem(layer + reach, 8)
     for z in range(16):
         out_ref[:, z] = got_ref[z, 0:32]
     extra = got_ref[:, 32].reshape(32, 128)
@@ -63,8 +68,8 @@
     for i in range(2):
         put = mask((row % 2 == 0) & (lane - 32 * quarter == row + i))
         take = mask((take_row % 2 == 0) & (take_lane == 64 * half + take_row + i))
-        moved = dot(extra, put.astype(BF), ((0,), (0,)))
-        ids = ids + dot(take.astype(BF), moved.astype(BF))
+        taken = dot(take.astype(BF), extra, ((1,), (1,)))
+        ids = ids + dot(taken.astype(BF), put.astype(BF))
     out_ref[:, 16] = ids.astype(BF).reshape(32, 2, 128)
     out_ref[:, 17:24] = jnp.zeros((32, 7, 2, 128), BF)
     own = jnp.sum(mask(row == 2 * shard + 1) * extra.astype(F32), axis=0, keepdims=True)
@@ -117,22 +122,14 @@
         out_ref[128 * four : 128 * four + 128, :] = dot(hot, local, ((0,), (0,))).astype(BF)
 
 
-def return_kernel(got_ref, out_ref):
-    for z in range(16):
-        out_ref[z] = got_ref[:, z]
-
-
 def field_kernel(rows_ref, picked_ref, out_ref):
     to, at = iota((128, 256), 0), iota((128, 256), 1)
     part = mask(at == 2 * to + 1).astype(BF)
-    ones = jnp.ones((8, 128), BF)
     for k in range(8):
         basis = dot(part, rows_ref[256 * k : 256 * k + 256, :])
-        product = basis * picked_ref[128 * k : 128 * k + 128, :].astype(F32)
-        high = product.astype(BF)
-        low = (product - high.astype(F32)).astype(BF)
-        field = dot(ones, high, ((1,), (1,))) + dot(ones, low, ((1,), (1,)))
-        out_ref[k : k + 1, :] = field[0:1] * (128 ** -0.5)
+        picked = [picked_ref[:, 2 * k + j].reshape(64, 128) for j in range(2)]
+        product = basis * jnp.concatenate(picked, axis=0).astype(F32)
+        out_ref[k : k + 1, :] = jnp.sum(product, axis=1)[None] * (128 ** -0.5)
 
 
 REACH = (0, 4, 1, -1, 2, -2, 3, -3)
@@ -171,11 +168,6 @@
 
 
 def body(bead_data, bead_cell, m2l_ops, offsets):
-    peer = lax.axis_index("y") * 2 + lax.axis_index("c")
-    layer = lax.axis_index("zl")
-    shard = (layer + 8 + jnp.array(REACH, jnp.int32)[peer]) % 8
-    place = jnp.stack([peer % 4, layer % 2, shard])
-
     rows = bead_data.reshape(2048, 128)
     moments = call(pack_kernel, shape(16, 33, 2, 128), [SMEM, VMEM, VMEM])(
         offsets.T, rows, bead_cell.reshape(8, 128)
@@ -183,8 +175,8 @@
     moments = exchange(moments.reshape(528, 2, 128), COLUMN)
     m2l_ops, moments = lax.optimization_barrier((m2l_ops, moments))
     moments, shifts = call(
-        regroup_kernel, [shape(32, 24, 2, 128), shape(8, 128, kind=jnp.int32)], [SMEM, VMEM]
-    )(place, moments.reshape(16, 33, 2, 128))
+        regroup_kernel, [shape(32, 24, 2, 128), shape(8, 128, kind=jnp.int32)], [VMEM]
+    )(moments.reshape(16, 33, 2, 128))
     moments = exchange(moments.reshape(768, 2, 128), LAYER).reshape(32, 48, 128)
     ops = lax.ppermute(m2l_ops, ("zh", "y", "c", "zl"), ops_moves())
     cells, ids = call(sum_kernel, [shape(8, 128, 128), shape(8, 128, kind=F32)], [VMEM])(moments)
@@ -199,9 +191,7 @@
     )(shifts, ops, slab, low, high)
     parts = exchange(parts.reshape(8, 128, 128), GROUP)
     picked = call(pick_kernel, shape(1024, 128), [VMEM, VMEM])(ids, parts)
-    picked = exchange(picked.reshape(512, 2, 128), LAYER)
-    picked = call(return_kernel, shape(16, 32, 2, 128), [VMEM])(picked.reshape(32, 16, 2, 128))
-    picked = exchange(picked.reshape(512, 2, 128), COLUMN).reshape(1024, 128)
+    picked = exchange(picked.reshape(512, 2, 128), LAYER + COLUMN).reshape(32, 16, 2, 128)
     return call(field_kernel, shape(8, 128, kind=F32), [VMEM, VMEM])(rows, picked).reshape(1024)
 
 

time: 134 us -> 131 us (0.978)
  the two profiles are of different devices: /device:TPU:32 before, /device:TPU:1 now
where the time goes in v5:
time: 131 us
  blocking collectives  88.8 us (68%)
  starting transfers between devices  22.4 us (17%)
  waiting for transfers between devices  11 us (8%)
  Pallas kernels  5.97 us (5%)
  local copies, waits for them, and re-layouts  2.44 us (2%)
    all_to_all x4, blocking collectives, exchange(): return lax.all_to_all(array, axes, split_axis=0, concat_axis=0, tiled=True)  88.8 us
    all_to_all x1, starting transfers between devices, exchange(): return lax.all_to_all(array, axes, split_axis=0, concat_axis=0, tiled=True)  13.3 us
    ppermute x1, waiting for transfers between devices, body(): ops = lax.ppermute(m2l_ops, ('zh', 'y', 'c', 'zl'), ops_moves())  6.3 us
    ppermute x1, starting transfers between devices, body(): ops = lax.ppermute(m2l_ops, ('zh', 'y', 'c', 'zl'), ops_moves())  5.55 us
    all_to_all x1, waiting for transfers between devices, exchange(): return lax.all_to_all(array, axes, split_axis=0, concat_axis=0, tiled=True)  4.74 us
  transfers between devices with their start and end apart: 4, of which 2 were waited for; matrix products, arithmetic and copies ran while one was open for 0% of the time, Pallas kernels for 0%

profile of v5, /device:TPU:1, one launch (start us, length us, event | category | flops | bytes accessed | tf_op | source)
XLA Modules:
  0.0 130.8 jit_solution(8221363631998540693)
XLA Ops:
  0.0 0.0 copy-start.2
  0.0 0.7 copy-done.2
  0.7 1.0 copy-done
  1.7 0.7 copy-done.3
  2.4 0.9 shard_map.46
  3.3 28.8 %all_to_all.25 = bf16[528,2,128]{2,1,0:T(2,128)(2,1)S(1)} all-to-all(bf16[528,2,128]{2,1,0:T(2,128)(2,1)S(1)} %bitcast.18), channel_id=1, replica_groups=mesh['x'=4,'zh'=2,'y'=4,'c'=2,'zl'=8] {'zh','zl'}, dimensions={0} | all-to-all | bytes 540672 | tf_op jit(solution)/shard_map/all_to_all | solution.py:167
  32.1 1.1 shard_map.47
  33.2 13.3 %all-to-all-start.1 = ((bf16[768,2,128]{2,1,0:T(2,128)(2,1)}), bf16[768,2,128]{2,1,0:T(2,128)(2,1)S(1)}, u32[]{:S(2)}, u32[]{:S(2)}) async-start(bf16[768,2,128]{2,1,0:T(2,128)(2,1)} %bitcast.5), calls=%async_computation.1 | async-start | bytes 786432 | tf_op jit(solution)/shard_map/all_to_all | solution.py:167
  46.5 0.0 copy-done.4
  46.5 5.6 %collective-permute-start = (bf16[16,128,128]{2,1,0:T(8,128)(2,1)S(1)}, bf16[16,128,128]{2,1,0:T(8,128)(2,1)S(1)}, u32[]{:S(2)}, u32[]{:S(2)}) collective-permute-start(bf16[16,128,128]{2,1,0:T(8,128)(2,1)S(1)} %copy-done.4), channel_id=1, source_target_pairs={{0,0},{12,8},{17,16},{95,24},{34,32},{110,40},{51,48},{125,56},{1,... | collective-permute-start | bytes 1572872 | tf_op jit(solution)/shard_map/ppermute | solution.py:181
  52.1 4.7 %all-to-all-done.1 = bf16[768,2,128]{2,1,0:T(2,128)(2,1)S(1)} async-done(((bf16[768,2,128]{2,1,0:T(2,128)(2,1)}), bf16[768,2,128]{2,1,0:T(2,128)(2,1)S(1)}, u32[]{:S(2)}, u32[]{:S(2)}) %all-to-all-start.1) | async-done | bytes 393248 | tf_op jit(solution)/shard_map/all_to_all | solution.py:167
  56.8 0.2 shard_map.48
  57.0 9.1 %all_to_all.26 = bf16[8,128,128]{2,1,0:T(8,128)(2,1)S(1)} all-to-all(bf16[8,128,128]{2,1,0:T(8,128)(2,1)S(1)} %get-tuple-element.16), channel_id=1, replica_groups=mesh['x'=4,'zh'=2,'y'=4,'c'=2,'zl'=8] {'y','c'}, dimensions={0} | all-to-all | bytes 524288 | tf_op jit(solution)/shard_map/all_to_all | solution.py:167
  66.2 2.3 %collective-permute-start.1 = (bf16[768,128]{1,0:T(8,128)(2,1)S(1)}, bf16[768,128]{1,0:T(8,128)(2,1)S(1)}, u32[]{:S(2)}, u32[]{:S(2)}) collective-permute-start(bf16[768,128]{1,0:T(8,128)(2,1)S(1)} %bitcast.25), channel_id=1, source_target_pairs={{0,128},{128,256},{256,384},{384,1},{1,129},{129,257},{257,385},{3... | collective-permute-start | bytes 589832 | tf_op jit(solution)/shard_map/ppermute | solution.py:184
  68.4 1.3 collective-permute-start.2
  69.7 6.3 %collective-permute-done.ops_ref = bf16[16,128,128]{2,1,0:T(8,128)(2,1)S(1)} collective-permute-done((bf16[16,128,128]{2,1,0:T(8,128)(2,1)S(1)}, bf16[16,128,128]{2,1,0:T(8,128)(2,1)S(1)}, u32[]{:S(2)}, u32[]{:S(2)}) %collective-permute-start) | collective-permute-done | bytes 524320 | tf_op jit(solution)/shard_map/ppermute | solution.py:181
  76.0 0.0 collective-permute-done.2.high_ref
  76.0 0.0 collective-permute-done.1.low_ref
  76.0 2.6 %shard_map.49 = bf16[1024,128]{1,0:T(8,128)(2,1)S(1)} custom-call(s32[8,128]{1,0:T(8,128)S(1)} %get-tuple-element.14.offsets_ref, bf16[16,128,128]{2,1,0:T(8,128)(2,1)S(1)} %collective-permute-done.ops_ref, bf16[1024,128]{1,0:T(8,128)(2,1)S(1)} %bitcast.14, bf16[768,128]{1,0:T(8,128)(2,1)S(1)} %collective-permute-done.1.low_ref, ...), custom_call_target="tpu_custom_call" | custom-call | tf_op jit(solution)/shard_map/pallas_call | solution.py:186
  78.6 9.5 %all_to_all.27.parts_ref = bf16[8,128,128]{2,1,0:T(8,128)(2,1)S(1)} all-to-all(bf16[8,128,128]{2,1,0:T(8,128)(2,1)S(1)} %bitcast.22), channel_id=1, replica_groups=mesh['x'=4,'zh'=2,'y'=4,'c'=2,'zl'=8] {'y','c'}, dimensions={0} | all-to-all | bytes 524288 | tf_op jit(solution)/shard_map/all_to_all | solution.py:167
  88.1 0.3 shard_map.50
  88.4 41.5 %all_to_all.28 = bf16[512,2,128]{2,1,0:T(2,128)(2,1)S(1)} all-to-all(bf16[512,2,128]{2,1,0:T(2,128)(2,1)S(1)} %bitcast.21), channel_id=1, replica_groups=mesh['x'=4,'zh'=2,'y'=4,'c'=2,'zl'=8] {'x','y','c','zh','zl'}, dimensions={0} | all-to-all | bytes 524288 | tf_op jit(solution)/shard_map/all_to_all | solution.py:167
  129.8 0.0 copy-done.1
  129.8 1.0 shard_map.51
  (6 shorter events, 0.0 us)
Async XLA Ops:
  0.0 0.7 copy-start.2
  0.7 1.0 copy-start
  1.7 0.7 copy-start.3
  32.1 14.4 %copy-start.4 = (bf16[16,128,128]{2,1,0:T(8,128)(2,1)S(1)}, bf16[16,128,128]{2,1,0:T(8,128)(2,1)}, u32[]{:S(2)}) copy-start(bf16[16,128,128]{2,1,0:T(8,128)(2,1)} %param.6) | copy-start | bytes 1572868
  33.2 23.7 %all-to-all-start.1 = ((bf16[768,2,128]{2,1,0:T(2,128)(2,1)}), bf16[768,2,128]{2,1,0:T(2,128)(2,1)S(1)}, u32[]{:S(2)}, u32[]{:S(2)}) async-start(bf16[768,2,128]{2,1,0:T(2,128)(2,1)} %bitcast.5), calls=%async_computation.1 | async-start | bytes 786432 | tf_op jit(solution)/shard_map/all_to_all | solution.py:167
  46.5 29.5 %collective-permute-start = (bf16[16,128,128]{2,1,0:T(8,128)(2,1)S(1)}, bf16[16,128,128]{2,1,0:T(8,128)(2,1)S(1)}, u32[]{:S(2)}, u32[]{:S(2)}) collective-permute-start(bf16[16,128,128]{2,1,0:T(8,128)(2,1)S(1)} %copy-done.4), channel_id=1, source_target_pairs={{0,0},{12,8},{17,16},{95,24},{34,32},{110,40},{51,48},{125,56},{1,... | collective-permute-start | bytes 1572872 | tf_op jit(solution)/shard_map/ppermute | solution.py:181
  66.2 9.9 %collective-permute-start.1 = (bf16[768,128]{1,0:T(8,128)(2,1)S(1)}, bf16[768,128]{1,0:T(8,128)(2,1)S(1)}, u32[]{:S(2)}, u32[]{:S(2)}) collective-permute-start(bf16[768,128]{1,0:T(8,128)(2,1)S(1)} %bitcast.25), channel_id=1, source_target_pairs={{0,128},{128,256},{256,384},{384,1},{1,129},{129,257},{257,385},{3... | collective-permute-start | bytes 589832 | tf_op jit(solution)/shard_map/ppermute | solution.py:184
  68.4 7.6 %collective-permute-start.2 = (bf16[512,128]{1,0:T(8,128)(2,1)S(1)}, bf16[512,128]{1,0:T(8,128)(2,1)S(1)}, u32[]{:S(2)}, u32[]{:S(2)}) collective-permute-start(bf16[512,128]{1,0:T(8,128)(2,1)S(1)} %bitcast.26), channel_id=1, source_target_pairs={{128,0},{256,128},{384,256},{1,384},{129,1},{257,129},{385,257},{2... | collective-permute-start | bytes 393224 | tf_op jit(solution)/shard_map/ppermute | solution.py:185
  88.1 41.7 %copy-start.1 = (bf16[1024,2,128]{2,1,0:T(2,128)(2,1)S(1)}, bf16[1024,2,128]{2,1,0:T(2,128)(2,1)}, u32[]{:S(2)}) copy-start(bf16[1024,2,128]{2,1,0:T(2,128)(2,1)} %param.4) | copy-start | bytes 1572868

commit v6 on v5

--- a/solution.py
+++ b/solution.py
@@ -136,7 +136,12 @@
 
 
 def ops_moves():
-    return [(spot((z + REACH[a]) % 16, a), spot(z, a)) for z in range(16) for a in range(8)]
+    moves = []
+    for z in range(16):
+        for a in range(8):
+            reach = -4 if REACH[a] == 4 and z % 2 else REACH[a]
+            moves.append((spot((z + reach) % 16, a), spot(z, a)))
+    return moves
 
 
 def spot(z, a):

time: 131 us -> 131 us (level)
  blocking collectives: 88.8 us -> 90.7 us
  waiting for transfers between devices: 11 us -> 9.14 us
    ppermute x1, waiting for transfers between devices: 6.3 us -> 0.01 us  [body(): ops = lax.ppermute(m2l_ops, ('zh', 'y', 'c', 'zl'), ops_moves())]
    ppermute x1, waiting for transfers between devices: 0.01 us -> 4.4 us  [body(): lax.ppermute(slab[:512], SLABS, [(slab_spot(i + 1), slab_spot(i)) for i i...]
    all_to_all x4, blocking collectives: 88.8 us -> 90.7 us  [exchange(): return lax.all_to_all(array, axes, split_axis=0, concat_axis=0, tiled=True)]
where the time goes in v6:
time: 131 us
  blocking collectives  90.7 us (69%)
  starting transfers between devices  22.4 us (17%)
  waiting for transfers between devices  9.14 us (7%)
  Pallas kernels  5.96 us (5%)
  local copies, waits for them, and re-layouts  2.44 us (2%)
    all_to_all x4, blocking collectives, exchange(): return lax.all_to_all(array, axes, split_axis=0, concat_axis=0, tiled=True)  90.7 us
    all_to_all x1, starting transfers between devices, exchange(): return lax.all_to_all(array, axes, split_axis=0, concat_axis=0, tiled=True)  13.3 us
    ppermute x1, starting transfers between devices, body(): ops = lax.ppermute(m2l_ops, ('zh', 'y', 'c', 'zl'), ops_moves())  5.55 us
    all_to_all x1, waiting for transfers between devices, exchange(): return lax.all_to_all(array, axes, split_axis=0, concat_axis=0, tiled=True)  4.74 us
    ppermute x1, waiting for transfers between devices, body(): lax.ppermute(slab[:512], SLABS, [(slab_spot(i + 1), slab_spot(i)) for i i...  4.4 us
  transfers between devices with their start and end apart: 4, of which 2 were waited for; matrix products, arithmetic and copies ran while one was open for 0% of the time, Pallas kernels for 0%

profile of v6, /device:TPU:1, one launch (start us, length us, event | category | flops | bytes accessed | tf_op | source)
XLA Modules:
  0.0 130.8 jit_solution(10685049880339574085)
XLA Ops:
  0.0 0.0 copy-start.2
  0.0 0.7 copy-done.2
  0.7 1.0 copy-done
  1.7 0.7 copy-done.3
  2.4 0.9 shard_map.46
  3.3 28.8 %all_to_all.25 = bf16[528,2,128]{2,1,0:T(2,128)(2,1)S(1)} all-to-all(bf16[528,2,128]{2,1,0:T(2,128)(2,1)S(1)} %bitcast.18), channel_id=1, replica_groups=mesh['x'=4,'zh'=2,'y'=4,'c'=2,'zl'=8] {'zh','zl'}, dimensions={0} | all-to-all | bytes 540672 | tf_op jit(solution)/shard_map/all_to_all | solution.py:172
  32.1 1.1 shard_map.47
  33.2 13.3 %all-to-all-start.1 = ((bf16[768,2,128]{2,1,0:T(2,128)(2,1)}), bf16[768,2,128]{2,1,0:T(2,128)(2,1)S(1)}, u32[]{:S(2)}, u32[]{:S(2)}) async-start(bf16[768,2,128]{2,1,0:T(2,128)(2,1)} %bitcast.5), calls=%async_computation.1 | async-start | bytes 786432 | tf_op jit(solution)/shard_map/all_to_all | solution.py:172
  46.5 0.0 copy-done.4
  46.5 5.6 %collective-permute-start = (bf16[16,128,128]{2,1,0:T(8,128)(2,1)S(1)}, bf16[16,128,128]{2,1,0:T(8,128)(2,1)S(1)}, u32[]{:S(2)}, u32[]{:S(2)}) collective-permute-start(bf16[16,128,128]{2,1,0:T(8,128)(2,1)S(1)} %copy-done.4), channel_id=1, source_target_pairs={{0,0},{12,8},{17,16},{95,24},{34,32},{110,40},{51,48},{125,56},{1,... | collective-permute-start | bytes 1572872 | tf_op jit(solution)/shard_map/ppermute | solution.py:186
  52.1 4.7 %all-to-all-done.1 = bf16[768,2,128]{2,1,0:T(2,128)(2,1)S(1)} async-done(((bf16[768,2,128]{2,1,0:T(2,128)(2,1)}), bf16[768,2,128]{2,1,0:T(2,128)(2,1)S(1)}, u32[]{:S(2)}, u32[]{:S(2)}) %all-to-all-start.1) | async-done | bytes 393248 | tf_op jit(solution)/shard_map/all_to_all | solution.py:172
  56.8 0.2 shard_map.48
  57.0 9.1 %all_to_all.26 = bf16[8,128,128]{2,1,0:T(8,128)(2,1)S(1)} all-to-all(bf16[8,128,128]{2,1,0:T(8,128)(2,1)S(1)} %get-tuple-element.16), channel_id=1, replica_groups=mesh['x'=4,'zh'=2,'y'=4,'c'=2,'zl'=8] {'y','c'}, dimensions={0} | all-to-all | bytes 524288 | tf_op jit(solution)/shard_map/all_to_all | solution.py:172
  66.2 2.3 %collective-permute-start.1 = (bf16[768,128]{1,0:T(8,128)(2,1)S(1)}, bf16[768,128]{1,0:T(8,128)(2,1)S(1)}, u32[]{:S(2)}, u32[]{:S(2)}) collective-permute-start(bf16[768,128]{1,0:T(8,128)(2,1)S(1)} %bitcast.25), channel_id=1, source_target_pairs={{0,128},{128,256},{256,384},{384,1},{1,129},{129,257},{257,385},{3... | collective-permute-start | bytes 589832 | tf_op jit(solution)/shard_map/ppermute | solution.py:189
  68.4 1.3 collective-permute-start.2
  69.7 0.0 collective-permute-done.ops_ref
  69.7 4.4 %collective-permute-done.2.high_ref = bf16[512,128]{1,0:T(8,128)(2,1)S(1)} collective-permute-done((bf16[512,128]{1,0:T(8,128)(2,1)S(1)}, bf16[512,128]{1,0:T(8,128)(2,1)S(1)}, u32[]{:S(2)}, u32[]{:S(2)}) %collective-permute-start.2) | collective-permute-done | bytes 131104 | tf_op jit(solution)/shard_map/ppermute | solution.py:190
  74.1 0.0 collective-permute-done.1.low_ref
  74.1 2.5 %shard_map.49 = bf16[1024,128]{1,0:T(8,128)(2,1)S(1)} custom-call(s32[8,128]{1,0:T(8,128)S(1)} %get-tuple-element.14.offsets_ref, bf16[16,128,128]{2,1,0:T(8,128)(2,1)S(1)} %collective-permute-done.ops_ref, bf16[1024,128]{1,0:T(8,128)(2,1)S(1)} %bitcast.14, bf16[768,128]{1,0:T(8,128)(2,1)S(1)} %collective-permute-done.1.low_ref, ...), custom_call_target="tpu_custom_call" | custom-call | tf_op jit(solution)/shard_map/pallas_call | solution.py:191
  76.7 11.4 %all_to_all.27.parts_ref = bf16[8,128,128]{2,1,0:T(8,128)(2,1)S(1)} all-to-all(bf16[8,128,128]{2,1,0:T(8,128)(2,1)S(1)} %bitcast.22), channel_id=1, replica_groups=mesh['x'=4,'zh'=2,'y'=4,'c'=2,'zl'=8] {'y','c'}, dimensions={0} | all-to-all | bytes 524288 | tf_op jit(solution)/shard_map/all_to_all | solution.py:172
  88.1 0.3 shard_map.50
  88.4 41.5 %all_to_all.28 = bf16[512,2,128]{2,1,0:T(2,128)(2,1)S(1)} all-to-all(bf16[512,2,128]{2,1,0:T(2,128)(2,1)S(1)} %bitcast.21), channel_id=1, replica_groups=mesh['x'=4,'zh'=2,'y'=4,'c'=2,'zl'=8] {'x','y','c','zh','zl'}, dimensions={0} | all-to-all | bytes 524288 | tf_op jit(solution)/shard_map/all_to_all | solution.py:172
  129.8 0.0 copy-done.1
  129.8 1.0 shard_map.51
  (6 shorter events, 0.0 us)
Async XLA Ops:
  0.0 0.7 copy-start.2
  0.7 1.0 copy-start
  1.7 0.7 copy-start.3
  32.1 14.4 %copy-start.4 = (bf16[16,128,128]{2,1,0:T(8,128)(2,1)S(1)}, bf16[16,128,128]{2,1,0:T(8,128)(2,1)}, u32[]{:S(2)}) copy-start(bf16[16,128,128]{2,1,0:T(8,128)(2,1)} %param.6) | copy-start | bytes 1572868
  33.2 23.7 %all-to-all-start.1 = ((bf16[768,2,128]{2,1,0:T(2,128)(2,1)}), bf16[768,2,128]{2,1,0:T(2,128)(2,1)S(1)}, u32[]{:S(2)}, u32[]{:S(2)}) async-start(bf16[768,2,128]{2,1,0:T(2,128)(2,1)} %bitcast.5), calls=%async_computation.1 | async-start | bytes 786432 | tf_op jit(solution)/shard_map/all_to_all | solution.py:172
  46.5 23.2 %collective-permute-start = (bf16[16,128,128]{2,1,0:T(8,128)(2,1)S(1)}, bf16[16,128,128]{2,1,0:T(8,128)(2,1)S(1)}, u32[]{:S(2)}, u32[]{:S(2)}) collective-permute-start(bf16[16,128,128]{2,1,0:T(8,128)(2,1)S(1)} %copy-done.4), channel_id=1, source_target_pairs={{0,0},{12,8},{17,16},{95,24},{34,32},{110,40},{51,48},{125,56},{1,... | collective-permute-start | bytes 1572872 | tf_op jit(solution)/shard_map/ppermute | solution.py:186
  66.2 8.0 %collective-permute-start.1 = (bf16[768,128]{1,0:T(8,128)(2,1)S(1)}, bf16[768,128]{1,0:T(8,128)(2,1)S(1)}, u32[]{:S(2)}, u32[]{:S(2)}) collective-permute-start(bf16[768,128]{1,0:T(8,128)(2,1)S(1)} %bitcast.25), channel_id=1, source_target_pairs={{0,128},{128,256},{256,384},{384,1},{1,129},{129,257},{257,385},{3... | collective-permute-start | bytes 589832 | tf_op jit(solution)/shard_map/ppermute | solution.py:189
  68.4 5.7 %collective-permute-start.2 = (bf16[512,128]{1,0:T(8,128)(2,1)S(1)}, bf16[512,128]{1,0:T(8,128)(2,1)S(1)}, u32[]{:S(2)}, u32[]{:S(2)}) collective-permute-start(bf16[512,128]{1,0:T(8,128)(2,1)S(1)} %bitcast.26), channel_id=1, source_target_pairs={{128,0},{256,128},{384,256},{1,384},{129,1},{257,129},{385,257},{2... | collective-permute-start | bytes 393224 | tf_op jit(solution)/shard_map/ppermute | solution.py:190
  88.1 41.7 %copy-start.1 = (bf16[1024,2,128]{2,1,0:T(2,128)(2,1)S(1)}, bf16[1024,2,128]{2,1,0:T(2,128)(2,1)}, u32[]{:S(2)}) copy-start(bf16[1024,2,128]{2,1,0:T(2,128)(2,1)} %param.4) | copy-start | bytes 1572868

commit v7 on v6

--- a/solution.py
+++ b/solution.py
@@ -16,9 +16,10 @@
 F32 = jnp.float32
 
 COLUMN = ("zh", "zl")
-LAYER = ("x", "y", "c")
-SLABS = ("x", "zh", "zl")
+LAYER = ("xh", "xl", "y", "c")
+SLABS = ("xh", "xl", "zh", "zl")
 GROUP = ("y", "c")
+PAIR = ("xl", "y", "c")
 VMEM = pl.BlockSpec(memory_space=pltpu.VMEM)
 SMEM = pl.BlockSpec(memory_space=pltpu.SMEM)
 
@@ -90,14 +91,20 @@
         cells_ref[peer] = cells
 
 
-def m2l_kernel(offsets_ref, ops_ref, own_ref, low_ref, high_ref, out_ref, rows, shifted):
+def m2l_kernel(offsets_ref, ops_ref, pair_ref, edge_ref, out_ref, rows, shifted):
+    second = lax.axis_index("xl")
     shifted[:, :, 0:3] = jnp.zeros((6, 9, 3, GY, 128), BF)
     shifted[:, :, 11:13] = jnp.zeros((6, 9, 2, GY, 128), BF)
     rows[:, 0:8, :] = jnp.zeros((GX, 8, 128), F32)
     rows[:, 40:48, :] = jnp.zeros((GX, 8, 128), F32)
     for plane in range(9):
-        ref, at = (low_ref, plane) if plane < 3 else (own_ref, plane - 3) if plane < 7 else (high_ref, plane - 7)
-        rows[:, 8:40, :] = ref[at * 256 : (at + 1) * 256, :].astype(F32).reshape(GX, GY, 128)
+        if plane < 3:
+            values = jnp.where(second == 1, pair_ref[plane + 1], edge_ref[plane])
+        elif plane < 7:
+            values = pair_ref[plane - 3 + 4 * second]
+        else:
+            values = jnp.where(second == 1, edge_ref[plane - 7], pair_ref[plane - 3])
+        rows[:, 8:40, :] = values.astype(F32).reshape(GX, GY, 128)
         for dy in range(6):
             shifted[dy, plane, 3:11] = rows[:, 5 + dy : 37 + dy, :].astype(BF)
     ops = ops_ref[...].reshape(16 * 128, 128)
@@ -135,11 +142,14 @@
 REACH = (0, 4, 1, -1, 2, -2, 3, -3)
 
 
-def ops_moves():
+STEPS = ((0, 2, 1, -1, 1, -1, 1, -1), (0, 2, 0, 0, 1, -1, 2, -2))
+
+
+def ops_moves(step):
     moves = []
     for z in range(16):
         for a in range(8):
-            reach = -4 if REACH[a] == 4 and z % 2 else REACH[a]
+            reach = -step[a] if REACH[a] == 4 and z % 2 else step[a]
             moves.append((spot((z + reach) % 16, a), spot(z, a)))
     return moves
 
@@ -183,17 +193,21 @@
         regroup_kernel, [shape(32, 24, 2, 128), shape(8, 128, kind=jnp.int32)], [VMEM]
     )(moments.reshape(16, 33, 2, 128))
     moments = exchange(moments.reshape(768, 2, 128), LAYER).reshape(32, 48, 128)
-    ops = lax.ppermute(m2l_ops, ("zh", "y", "c", "zl"), ops_moves())
-    cells, ids = call(sum_kernel, [shape(8, 128, 128), shape(8, 128, kind=F32)], [VMEM])(moments)
-    slab = exchange(cells, GROUP).reshape(1024, 128)
-    low = lax.ppermute(slab[256:], SLABS, [(slab_spot(i), slab_spot(i + 1)) for i in range(63)])
-    high = lax.ppermute(slab[:512], SLABS, [(slab_spot(i + 1), slab_spot(i)) for i in range(63)])
+    ops = m2l_ops
+    for step in STEPS:
+        ops = lax.ppermute(ops, ("zh", "y", "c", "zl"), ops_moves(step))
+    cells, ids = call(sum_kernel, [shape(16, 128, 128), shape(8, 128, kind=F32)], [VMEM])(moments)
+    pair = exchange(cells, PAIR).reshape(8, 256, 128)
+    edge = lax.dynamic_slice_in_dim(pair, 5 * lax.axis_index("xl"), 3, axis=0)
+    swaps = [(i, i + 1) for i in range(1, 63, 2)]
+    swaps = [(slab_spot(i), slab_spot(j)) for i, j in swaps + [(j, i) for i, j in swaps]]
+    edge = lax.ppermute(edge, SLABS, swaps)
     parts = call(
         m2l_kernel,
         shape(1024, 128),
-        [SMEM, VMEM, VMEM, VMEM, VMEM],
+        [SMEM, VMEM, VMEM, VMEM],
         [pltpu.VMEM((GX, 48, 128), F32), pltpu.VMEM((6, 9, 13, GY, 128), BF)],
-    )(shifts, ops, slab, low, high)
+    )(shifts, ops, pair, edge)
     parts = exchange(parts.reshape(8, 128, 128), GROUP)
     picked = call(pick_kernel, shape(1024, 128), [VMEM, VMEM])(ids, parts)
     picked = exchange(picked.reshape(512, 2, 128), LAYER + COLUMN).reshape(32, 16, 2, 128)
@@ -201,7 +215,7 @@
 
 
 def solution(mesh):
-    fine = Mesh(mesh.devices.reshape(4, 2, 4, 2, 8), ("x", "zh", "y", "c", "zl"))
-    every = ("x", "zh", "y", "c", "zl")
+    fine = Mesh(mesh.devices.reshape(2, 2, 2, 4, 2, 8), ("xh", "xl", "zh", "y", "c", "zl"))
+    every = ("xh", "xl", "zh", "y", "c", "zl")
     in_specs = (P(every, None, None), P(every), P("zl", None, None), P("zl", None))
     return jax.shard_map(body, mesh=fine, in_specs=in_specs, out_specs=P(every), check_vma=False)

time: 131 us -> 136 us (1.038)
  starting transfers between devices: 22.4 us -> 26 us
  waiting for transfers between devices: 9.14 us -> 12 us
  blocking collectives: 90.7 us -> 88.1 us
    all_to_all x1 -> x2, waiting for transfers between devices: 4.74 us -> 11.4 us  [exchange(): return lax.all_to_all(array, axes, split_axis=0, concat_axis=0, tiled=True)]
    ppermute x3, waiting for transfers between devices: 4.41 us -> 0.62 us  [the longest x2 0.62 us: body(): ops = lax.ppermute(ops, ('zh', 'y', 'c', 'zl'), ops_moves(step))]
    all_to_all x1 -> x2, starting transfers between devices: 13.3 us -> 16.8 us  [exchange(): return lax.all_to_all(array, axes, split_axis=0, concat_axis=0, tiled=True)]
    all_to_all x4 -> x3, blocking collectives: 90.7 us -> 88.1 us  [exchange(): return lax.all_to_all(array, axes, split_axis=0, concat_axis=0, tiled=True)]
  transfers between devices with their start and end apart: 4 -> 5, of which waited for: 2 -> 3; matrix products, arithmetic and copies ran while one was open for 0% -> 0% of each run, Pallas kernels for 0% -> 1%
where the time goes in v7:
time: 136 us; the launch traced here: 135 us
  blocking collectives  88.1 us (65%)
  starting transfers between devices  26 us (19%)
  waiting for transfers between devices  12 us (9%)
  Pallas kernels  6.81 us (5%)
  local copies, waits for them, and re-layouts  2.43 us (2%)
    all_to_all x3, blocking collectives, exchange(): return lax.all_to_all(array, axes, split_axis=0, concat_axis=0, tiled=True)  88.1 us
    all_to_all x2, starting transfers between devices, exchange(): return lax.all_to_all(array, axes, split_axis=0, concat_axis=0, tiled=True)  16.8 us
    all_to_all x2, waiting for transfers between devices, exchange(): return lax.all_to_all(array, axes, split_axis=0, concat_axis=0, tiled=True)  11.4 us
    ppermute x2, starting transfers between devices, body(): ops = lax.ppermute(ops, ('zh', 'y', 'c', 'zl'), ops_moves(step))  8.52 us
  transfers between devices with their start and end apart: 5, of which 3 were waited for; matrix products, arithmetic and copies ran while one was open for 0% of the time, Pallas kernels for 1%

profile of v7, /device:TPU:1, one launch (start us, length us, event | category | flops | bytes accessed | tf_op | source)
XLA Modules:
  0.0 135.4 jit_solution(17161543051023394237)
XLA Ops:
  0.0 0.7 copy-done.2
  0.7 1.0 copy-done
  1.7 0.7 copy-done.3
  2.4 0.9 shard_map.46
  3.3 28.8 %all_to_all.25 = bf16[528,2,128]{2,1,0:T(2,128)(2,1)S(1)} all-to-all(bf16[528,2,128]{2,1,0:T(2,128)(2,1)S(1)} %bitcast.17), channel_id=1, replica_groups=mesh['xh'=2,'xl'=2,'zh'=2,'y'=4,'c'=2,'zl'=8] {'zh','zl'}, dimensions={0} | all-to-all | bytes 540672 | tf_op jit(solution)/shard_map/all_to_all | solution.py:182
  32.1 1.1 shard_map.47
  33.2 13.3 %all-to-all-start.1 = ((bf16[768,2,128]{2,1,0:T(2,128)(2,1)}), bf16[768,2,128]{2,1,0:T(2,128)(2,1)S(1)}, u32[]{:S(2)}, u32[]{:S(2)}) async-start(bf16[768,2,128]{2,1,0:T(2,128)(2,1)} %bitcast.5), calls=%async_computation.1 | async-start | bytes 786432 | tf_op jit(solution)/shard_map/all_to_all | solution.py:182
  46.5 0.0 copy-done.4
  46.5 4.3 %collective-permute-start = (bf16[16,128,128]{2,1,0:T(8,128)(2,1)S(1)}, bf16[16,128,128]{2,1,0:T(8,128)(2,1)S(1)}, u32[]{:S(2)}, u32[]{:S(2)}) collective-permute-start(bf16[16,128,128]{2,1,0:T(8,128)(2,1)S(1)} %copy-done.4), channel_id=1, source_target_pairs={{0,0},{10,8},{17,16},{95,24},{33,32},{111,40},{49,48},{127,56},{1,... | collective-permute-start | bytes 1572872 | tf_op jit(solution)/shard_map/ppermute | solution.py:198
  50.8 6.0 %all-to-all-done.1 = bf16[768,2,128]{2,1,0:T(2,128)(2,1)S(1)} async-done(((bf16[768,2,128]{2,1,0:T(2,128)(2,1)}), bf16[768,2,128]{2,1,0:T(2,128)(2,1)S(1)}, u32[]{:S(2)}, u32[]{:S(2)}) %all-to-all-start.1) | async-done | bytes 393248 | tf_op jit(solution)/shard_map/all_to_all | solution.py:182
  56.8 1.1 shard_map.48
  57.9 3.5 %all-to-all-start.2 = ((bf16[16,128,128]{2,1,0:T(8,128)(2,1)}), bf16[16,128,128]{2,1,0:T(8,128)(2,1)S(1)}, u32[]{:S(2)}, u32[]{:S(2)}) async-start(bf16[16,128,128]{2,1,0:T(8,128)(2,1)} %get-tuple-element.16), calls=%async_computation.2 | async-start | bytes 1048576 | tf_op jit(solution)/shard_map/all_to_all | solution.py:182
  61.3 0.0 collective-permute-done
  61.4 4.3 %collective-permute-start.1 = (bf16[16,128,128]{2,1,0:T(8,128)(2,1)S(1)}, bf16[16,128,128]{2,1,0:T(8,128)(2,1)S(1)}, u32[]{:S(2)}, u32[]{:S(2)}) collective-permute-start(bf16[16,128,128]{2,1,0:T(8,128)(2,1)S(1)} %collective-permute-done), channel_id=1, source_target_pairs={{0,0},{10,8},{16,16},{24,24},{33,32},{111,40},{50,48},{126,56},{1,... | collective-permute-start | bytes 1572872 | tf_op jit(solution)/shard_map/ppermute | solution.py:198
  65.6 5.4 %all-to-all-done.2 = bf16[16,128,128]{2,1,0:T(8,128)(2,1)S(1)} async-done(((bf16[16,128,128]{2,1,0:T(8,128)(2,1)}), bf16[16,128,128]{2,1,0:T(8,128)(2,1)S(1)}, u32[]{:S(2)}, u32[]{:S(2)}) %all-to-all-start.2) | async-done | bytes 524320 | tf_op jit(solution)/shard_map/all_to_all | solution.py:182
  71.0 0.7 collective-permute-start.2
  71.7 0.6 collective-permute-done.1.ops_ref
  72.3 0.0 collective-permute-done.2.edge_ref
  72.3 2.6 %shard_map.49 = bf16[1024,128]{1,0:T(8,128)(2,1)S(1)} custom-call(s32[8,128]{1,0:T(8,128)S(1)} %get-tuple-element.14.offsets_ref, bf16[16,128,128]{2,1,0:T(8,128)(2,1)S(1)} %collective-permute-done.1.ops_ref, bf16[8,256,128]{2,1,0:T(8,128)(2,1)S(1)} %bitcast.13, bf16[3,256,128]{2,1,0:T(8,128)(2,1)S(1)} %collective-permute-done.2.edge_ref), custom_call_target="tpu_custom_call" | custom-call | tf_op jit(solution)/shard_map/pallas_call | solution.py:205
  74.9 19.4 %all_to_all.26.parts_ref = bf16[8,128,128]{2,1,0:T(8,128)(2,1)S(1)} all-to-all(bf16[8,128,128]{2,1,0:T(8,128)(2,1)S(1)} %bitcast.21), channel_id=1, replica_groups=mesh['xh'=2,'xl'=2,'zh'=2,'y'=4,'c'=2,'zl'=8] {'y','c'}, dimensions={0} | all-to-all | bytes 524288 | tf_op jit(solution)/shard_map/all_to_all | solution.py:182
  94.3 0.3 shard_map.50
  94.6 39.8 %all_to_all.27 = bf16[512,2,128]{2,1,0:T(2,128)(2,1)S(1)} all-to-all(bf16[512,2,128]{2,1,0:T(2,128)(2,1)S(1)} %bitcast.20), channel_id=1, replica_groups=mesh['xh'=2,'xl'=2,'zh'=2,'y'=4,'c'=2,'zl'=8] {'xh','xl','y','c','zh','zl'}, dimensions={0} | all-to-all | bytes 524288 | tf_op jit(solution)/shard_map/all_to_all | solution.py:182
  134.4 0.0 copy-done.1
  134.4 1.0 shard_map.51
  (6 shorter events, 0.0 us)
Async XLA Ops:
  0.0 0.7 copy-start.2
  0.7 1.0 copy-start
  1.7 0.7 copy-start.3
  32.1 14.4 %copy-start.4 = (bf16[16,128,128]{2,1,0:T(8,128)(2,1)S(1)}, bf16[16,128,128]{2,1,0:T(8,128)(2,1)}, u32[]{:S(2)}) copy-start(bf16[16,128,128]{2,1,0:T(8,128)(2,1)} %param.6) | copy-start | bytes 1572868
  33.2 23.7 %all-to-all-start.1 = ((bf16[768,2,128]{2,1,0:T(2,128)(2,1)}), bf16[768,2,128]{2,1,0:T(2,128)(2,1)S(1)}, u32[]{:S(2)}, u32[]{:S(2)}) async-start(bf16[768,2,128]{2,1,0:T(2,128)(2,1)} %bitcast.5), calls=%async_computation.1 | async-start | bytes 786432 | tf_op jit(solution)/shard_map/all_to_all | solution.py:182
  46.5 14.8 %collective-permute-start = (bf16[16,128,128]{2,1,0:T(8,128)(2,1)S(1)}, bf16[16,128,128]{2,1,0:T(8,128)(2,1)S(1)}, u32[]{:S(2)}, u32[]{:S(2)}) collective-permute-start(bf16[16,128,128]{2,1,0:T(8,128)(2,1)S(1)} %copy-done.4), channel_id=1, source_target_pairs={{0,0},{10,8},{17,16},{95,24},{33,32},{111,40},{49,48},{127,56},{1,... | collective-permute-start | bytes 1572872 | tf_op jit(solution)/shard_map/ppermute | solution.py:198
  57.9 13.1 %all-to-all-start.2 = ((bf16[16,128,128]{2,1,0:T(8,128)(2,1)}), bf16[16,128,128]{2,1,0:T(8,128)(2,1)S(1)}, u32[]{:S(2)}, u32[]{:S(2)}) async-start(bf16[16,128,128]{2,1,0:T(8,128)(2,1)} %get-tuple-element.16), calls=%async_computation.2 | async-start | bytes 1048576 | tf_op jit(solution)/shard_map/all_to_all | solution.py:182
  61.4 10.9 %collective-permute-start.1 = (bf16[16,128,128]{2,1,0:T(8,128)(2,1)S(1)}, bf16[16,128,128]{2,1,0:T(8,128)(2,1)S(1)}, u32[]{:S(2)}, u32[]{:S(2)}) collective-permute-start(bf16[16,128,128]{2,1,0:T(8,128)(2,1)S(1)} %collective-permute-done), channel_id=1, source_target_pairs={{0,0},{10,8},{16,16},{24,24},{33,32},{111,40},{50,48},{126,56},{1,... | collective-permute-start | bytes 1572872 | tf_op jit(solution)/shard_map/ppermute | solution.py:198
  71.0 1.3 collective-permute-start.2
  94.3 40.1 %copy-start.1 = (bf16[1024,2,128]{2,1,0:T(2,128)(2,1)S(1)}, bf16[1024,2,128]{2,1,0:T(2,128)(2,1)}, u32[]{:S(2)}) copy-start(bf16[1024,2,128]{2,1,0:T(2,128)(2,1)} %param.4) | copy-start | bytes 1572868

commit v8 on v6

--- a/solution.py
+++ b/solution.py
@@ -17,7 +17,6 @@
 
 COLUMN = ("zh", "zl")
 LAYER = ("x", "y", "c")
-SLABS = ("x", "zh", "zl")
 GROUP = ("y", "c")
 VMEM = pl.BlockSpec(memory_space=pltpu.VMEM)
 SMEM = pl.BlockSpec(memory_space=pltpu.SMEM)
@@ -90,14 +89,26 @@
         cells_ref[peer] = cells
 
 
-def m2l_kernel(offsets_ref, ops_ref, own_ref, low_ref, high_ref, out_ref, rows, shifted):
+def edge_kernel(slab_ref, out_ref):
+    first = 1 - lax.axis_index("c")
+    for plane in range(3):
+        out_ref[plane] = slab_ref[first + plane]
+
+
+def m2l_kernel(offsets_ref, ops_ref, slab_ref, near_ref, far_ref, out_ref, rows, shifted):
+    core = lax.axis_index("c")
     shifted[:, :, 0:3] = jnp.zeros((6, 9, 3, GY, 128), BF)
     shifted[:, :, 11:13] = jnp.zeros((6, 9, 2, GY, 128), BF)
     rows[:, 0:8, :] = jnp.zeros((GX, 8, 128), F32)
     rows[:, 40:48, :] = jnp.zeros((GX, 8, 128), F32)
     for plane in range(9):
-        ref, at = (low_ref, plane) if plane < 3 else (own_ref, plane - 3) if plane < 7 else (high_ref, plane - 7)
-        rows[:, 8:40, :] = ref[at * 256 : (at + 1) * 256, :].astype(F32).reshape(GX, GY, 128)
+        if plane < 3:
+            values = jnp.where(core == 0, near_ref[plane], far_ref[plane])
+        elif plane < 7:
+            values = slab_ref[plane - 3]
+        else:
+            values = jnp.where(core == 0, far_ref[plane - 7], near_ref[plane - 7])
+        rows[:, 8:40, :] = values.astype(F32).reshape(GX, GY, 128)
         for dy in range(6):
             shifted[dy, plane, 3:11] = rows[:, 5 + dy : 37 + dy, :].astype(BF)
     ops = ops_ref[...].reshape(16 * 128, 128)
@@ -148,8 +159,12 @@
     return (z // 8 * 8 + a) * 8 + z % 8
 
 
-def slab_spot(s):
-    return s % 4 * 16 + s // 4
+def halo_moves():
+    def at(s, core):
+        x, z = s % 4, s // 4
+        return ((x * 2 + z // 8) * 2 + core) * 8 + z % 8
+
+    return [(at(i + core, core), at(i + 1 - core, core)) for i in range(63) for core in range(2)]
 
 
 def call(kernel, out_shape, in_specs, scratch=()):
@@ -185,15 +200,17 @@
     moments = exchange(moments.reshape(768, 2, 128), LAYER).reshape(32, 48, 128)
     ops = lax.ppermute(m2l_ops, ("zh", "y", "c", "zl"), ops_moves())
     cells, ids = call(sum_kernel, [shape(8, 128, 128), shape(8, 128, kind=F32)], [VMEM])(moments)
-    slab = exchange(cells, GROUP).reshape(1024, 128)
-    low = lax.ppermute(slab[256:], SLABS, [(slab_spot(i), slab_spot(i + 1)) for i in range(63)])
-    high = lax.ppermute(slab[:512], SLABS, [(slab_spot(i + 1), slab_spot(i)) for i in range(63)])
+    slab = exchange(cells, GROUP).reshape(4, 256, 128)
+    near = call(edge_kernel, shape(3, 256, 128), [VMEM])(slab)
+    near, ops = lax.optimization_barrier((near, ops))
+    near = lax.ppermute(near, ("x", "zh", "c", "zl"), halo_moves())
+    far = lax.ppermute(near, "c", [(0, 1), (1, 0)])
     parts = call(
         m2l_kernel,
         shape(1024, 128),
         [SMEM, VMEM, VMEM, VMEM, VMEM],
         [pltpu.VMEM((GX, 48, 128), F32), pltpu.VMEM((6, 9, 13, GY, 128), BF)],
-    )(shifts, ops, slab, low, high)
+    )(shifts, ops, slab, near, far)
     parts = exchange(parts.reshape(8, 128, 128), GROUP)
     picked = call(pick_kernel, shape(1024, 128), [VMEM, VMEM])(ids, parts)
     picked = exchange(picked.reshape(512, 2, 128), LAYER + COLUMN).reshape(32, 16, 2, 128)

time: 131 us -> 135 us (1.031)
  blocking collectives: 90.7 us -> 92.7 us
  waiting for transfers between devices: 9.14 us -> 10.9 us
    all_to_all x4, blocking collectives: 90.7 us -> 92.7 us  [exchange(): return lax.all_to_all(array, axes, split_axis=0, concat_axis=0, tiled=True)]
    ppermute x2, waiting for transfers between devices: 4.4 us -> 6.21 us  [the longest x1 5.11 us: body(): near = lax.ppermute(near, ('x', 'zh', 'c', 'zl'), halo_moves())]
  transfers between devices with their start and end apart: 4 -> 4, of which waited for: 2 -> 3; matrix products, arithmetic and copies ran while one was open for 0% -> 0% of each run, Pallas kernels for 0% -> 0%
where the time goes in v8:
time: 135 us
  blocking collectives  92.7 us (69%)
  starting transfers between devices  22.4 us (17%)
  waiting for transfers between devices  10.9 us (8%)
  Pallas kernels  5.99 us (4%)
  local copies, waits for them, and re-layouts  2.42 us (2%)
    all_to_all x4, blocking collectives, exchange(): return lax.all_to_all(array, axes, split_axis=0, concat_axis=0, tiled=True)  92.7 us
    all_to_all x1, starting transfers between devices, exchange(): return lax.all_to_all(array, axes, split_axis=0, concat_axis=0, tiled=True)  13.3 us
    ppermute x1, starting transfers between devices, body(): ops = lax.ppermute(m2l_ops, ('zh', 'y', 'c', 'zl'), ops_moves())  5.55 us
    ppermute x1, waiting for transfers between devices, body(): near = lax.ppermute(near, ('x', 'zh', 'c', 'zl'), halo_moves())  5.11 us
    all_to_all x1, waiting for transfers between devices, exchange(): return lax.all_to_all(array, axes, split_axis=0, concat_axis=0, tiled=True)  4.74 us
  transfers between devices with their start and end apart: 4, of which 3 were waited for; matrix products, arithmetic and copies ran while one was open for 0% of the time, Pallas kernels for 0%

profile of v8, /device:TPU:1, one launch (start us, length us, event | category | flops | bytes accessed | tf_op | source)
XLA Modules:
  0.0 134.6 jit_solution(10196078055967705161)
XLA Ops:
  0.0 0.0 copy-start.2
  0.0 0.7 copy-done.2
  0.7 1.0 copy-done
  1.7 0.7 copy-done.3
  2.4 0.9 shard_map.46
  3.3 28.8 %all_to_all.25 = bf16[528,2,128]{2,1,0:T(2,128)(2,1)S(1)} all-to-all(bf16[528,2,128]{2,1,0:T(2,128)(2,1)S(1)} %bitcast.17), channel_id=1, replica_groups=mesh['x'=4,'zh'=2,'y'=4,'c'=2,'zl'=8] {'zh','zl'}, dimensions={0} | all-to-all | bytes 540672 | tf_op jit(solution)/shard_map/all_to_all | solution.py:187
  32.1 1.1 shard_map.47
  33.2 13.3 %all-to-all-start.1 = ((bf16[768,2,128]{2,1,0:T(2,128)(2,1)}), bf16[768,2,128]{2,1,0:T(2,128)(2,1)S(1)}, u32[]{:S(2)}, u32[]{:S(2)}) async-start(bf16[768,2,128]{2,1,0:T(2,128)(2,1)} %bitcast.5), calls=%async_computation.1 | async-start | bytes 786432 | tf_op jit(solution)/shard_map/all_to_all | solution.py:187
  46.5 0.0 copy-done.4
  46.5 5.6 %collective-permute-start = (bf16[16,128,128]{2,1,0:T(8,128)(2,1)S(1)}, bf16[16,128,128]{2,1,0:T(8,128)(2,1)S(1)}, u32[]{:S(2)}, u32[]{:S(2)}) collective-permute-start(bf16[16,128,128]{2,1,0:T(8,128)(2,1)S(1)} %copy-done.4), channel_id=1, source_target_pairs={{0,0},{12,8},{17,16},{95,24},{34,32},{110,40},{51,48},{125,56},{1,... | collective-permute-start | bytes 1572872 | tf_op jit(solution)/shard_map/ppermute | solution.py:201
  52.1 4.7 %all-to-all-done.1 = bf16[768,2,128]{2,1,0:T(2,128)(2,1)S(1)} async-done(((bf16[768,2,128]{2,1,0:T(2,128)(2,1)}), bf16[768,2,128]{2,1,0:T(2,128)(2,1)S(1)}, u32[]{:S(2)}, u32[]{:S(2)}) %all-to-all-start.1) | async-done | bytes 393248 | tf_op jit(solution)/shard_map/all_to_all | solution.py:187
  56.8 0.2 shard_map.48
  57.0 9.1 %all_to_all.26 = bf16[8,128,128]{2,1,0:T(8,128)(2,1)S(1)} all-to-all(bf16[8,128,128]{2,1,0:T(8,128)(2,1)S(1)} %get-tuple-element.17), channel_id=1, replica_groups=mesh['x'=4,'zh'=2,'y'=4,'c'=2,'zl'=8] {'y','c'}, dimensions={0} | all-to-all | bytes 524288 | tf_op jit(solution)/shard_map/all_to_all | solution.py:187
  66.2 0.0 collective-permute-done.ops_ref
  66.2 1.3 collective-permute-start.1
  67.5 5.1 %collective-permute-done.1.near_ref = bf16[3,256,128]{2,1,0:T(8,128)(2,1)S(1)} collective-permute-done((bf16[3,256,128]{2,1,0:T(8,128)(2,1)S(1)}, bf16[3,256,128]{2,1,0:T(8,128)(2,1)S(1)}, u32[]{:S(2)}, u32[]{:S(2)}) %collective-permute-start.1) | collective-permute-done | bytes 196640 | tf_op jit(solution)/shard_map/ppermute | solution.py:206
  72.6 2.2 %collective-permute-start.2 = (bf16[3,256,128]{2,1,0:T(8,128)(2,1)S(1)}, bf16[3,256,128]{2,1,0:T(8,128)(2,1)S(1)}, u32[]{:S(2)}, u32[]{:S(2)}) collective-permute-start(bf16[3,256,128]{2,1,0:T(8,128)(2,1)S(1)} %collective-permute-done.1.near_ref), channel_id=1, source_target_pairs={{0,8},{8,0},{1,9},{9,1},{2,10},{10,2},{3,11},{11,3},{4,12},{12,4},... | collective-permute-start | bytes 589832 | tf_op jit(solution)/shard_map/ppermute | solution.py:207
  74.8 1.1 collective-permute-done.2.far_ref
  75.9 2.6 %shard_map.50 = bf16[1024,128]{1,0:T(8,128)(2,1)S(1)} custom-call(s32[8,128]{1,0:T(8,128)S(1)} %get-tuple-element.16.offsets_ref, bf16[16,128,128]{2,1,0:T(8,128)(2,1)S(1)} %collective-permute-done.ops_ref, bf16[4,256,128]{2,1,0:T(8,128)(2,1)S(1)} %bitcast.13, bf16[3,256,128]{2,1,0:T(8,128)(2,1)S(1)} %collective-permute-done.1.near_ref, ...), custom_call_target="tpu_custom_call" | custom-call | tf_op jit(solution)/shard_map/pallas_call | solution.py:208
  78.5 15.4 %all_to_all.27.parts_ref = bf16[8,128,128]{2,1,0:T(8,128)(2,1)S(1)} all-to-all(bf16[8,128,128]{2,1,0:T(8,128)(2,1)S(1)} %bitcast.21), channel_id=1, replica_groups=mesh['x'=4,'zh'=2,'y'=4,'c'=2,'zl'=8] {'y','c'}, dimensions={0} | all-to-all | bytes 524288 | tf_op jit(solution)/shard_map/all_to_all | solution.py:187
  93.8 0.3 shard_map.51
  94.1 39.5 %all_to_all.28 = bf16[512,2,128]{2,1,0:T(2,128)(2,1)S(1)} all-to-all(bf16[512,2,128]{2,1,0:T(2,128)(2,1)S(1)} %bitcast.20), channel_id=1, replica_groups=mesh['x'=4,'zh'=2,'y'=4,'c'=2,'zl'=8] {'x','y','c','zh','zl'}, dimensions={0} | all-to-all | bytes 524288 | tf_op jit(solution)/shard_map/all_to_all | solution.py:187
  133.6 0.0 copy-done.1
  133.6 1.0 shard_map.52
  (5 shorter events, 0.0 us)
Async XLA Ops:
  0.0 0.7 copy-start.2
  0.7 1.0 copy-start
  1.7 0.7 copy-start.3
  32.1 14.4 %copy-start.4 = (bf16[16,128,128]{2,1,0:T(8,128)(2,1)S(1)}, bf16[16,128,128]{2,1,0:T(8,128)(2,1)}, u32[]{:S(2)}) copy-start(bf16[16,128,128]{2,1,0:T(8,128)(2,1)} %param.6) | copy-start | bytes 1572868
  33.2 23.7 %all-to-all-start.1 = ((bf16[768,2,128]{2,1,0:T(2,128)(2,1)}), bf16[768,2,128]{2,1,0:T(2,128)(2,1)S(1)}, u32[]{:S(2)}, u32[]{:S(2)}) async-start(bf16[768,2,128]{2,1,0:T(2,128)(2,1)} %bitcast.5), calls=%async_computation.1 | async-start | bytes 786432 | tf_op jit(solution)/shard_map/all_to_all | solution.py:187
  46.5 19.6 %collective-permute-start = (bf16[16,128,128]{2,1,0:T(8,128)(2,1)S(1)}, bf16[16,128,128]{2,1,0:T(8,128)(2,1)S(1)}, u32[]{:S(2)}, u32[]{:S(2)}) collective-permute-start(bf16[16,128,128]{2,1,0:T(8,128)(2,1)S(1)} %copy-done.4), channel_id=1, source_target_pairs={{0,0},{12,8},{17,16},{95,24},{34,32},{110,40},{51,48},{125,56},{1,... | collective-permute-start | bytes 1572872 | tf_op jit(solution)/shard_map/ppermute | solution.py:201
  66.2 6.4 %collective-permute-start.1 = (bf16[3,256,128]{2,1,0:T(8,128)(2,1)S(1)}, bf16[3,256,128]{2,1,0:T(8,128)(2,1)S(1)}, u32[]{:S(2)}, u32[]{:S(2)}) collective-permute-start(bf16[3,256,128]{2,1,0:T(8,128)(2,1)S(1)} %shard_map.49), channel_id=1, source_target_pairs={{0,128},{136,8},{128,256},{264,136},{256,384},{392,264},{384,1},{9... | collective-permute-start | bytes 589832 | tf_op jit(solution)/shard_map/ppermute | solution.py:206
  72.6 3.3 %collective-permute-start.2 = (bf16[3,256,128]{2,1,0:T(8,128)(2,1)S(1)}, bf16[3,256,128]{2,1,0:T(8,128)(2,1)S(1)}, u32[]{:S(2)}, u32[]{:S(2)}) collective-permute-start(bf16[3,256,128]{2,1,0:T(8,128)(2,1)S(1)} %collective-permute-done.1.near_ref), channel_id=1, source_target_pairs={{0,8},{8,0},{1,9},{9,1},{2,10},{10,2},{3,11},{11,3},{4,12},{12,4},... | collective-permute-start | bytes 589832 | tf_op jit(solution)/shard_map/ppermute | solution.py:207
  93.8 39.8 %copy-start.1 = (bf16[1024,2,128]{2,1,0:T(2,128)(2,1)S(1)}, bf16[1024,2,128]{2,1,0:T(2,128)(2,1)}, u32[]{:S(2)}) copy-start(bf16[1024,2,128]{2,1,0:T(2,128)(2,1)} %param.4) | copy-start | bytes 1572868

commit v9 on v6

--- a/solution.py
+++ b/solution.py
@@ -71,7 +71,6 @@
         taken = dot(take.astype(BF), extra, ((1,), (1,)))
         ids = ids + dot(taken.astype(BF), put.astype(BF))
     out_ref[:, 16] = ids.astype(BF).reshape(32, 2, 128)
-    out_ref[:, 17:24] = jnp.zeros((32, 7, 2, 128), BF)
     own = jnp.sum(mask(row == 2 * shard + 1) * extra.astype(F32), axis=0, keepdims=True)
     offsets_ref[...] = jnp.broadcast_to(own, (8, 128)).astype(jnp.int32)
 
@@ -79,12 +78,12 @@
 def sum_kernel(got_ref, cells_ref, ids_ref):
     cell = iota((128, 128), 0)
     total = jnp.zeros((128, 128), F32)
+    every = got_ref[:, 16].reshape(64, 128).astype(F32)
     for four in range(8):
-        blocks = [got_ref[4 * four + j] for j in range(4)]
-        ids = sum(block[32:48].astype(F32) for block in blocks)[0:1]
+        ids = jnp.sum(every[8 * four : 8 * four + 8], axis=0, keepdims=True)
         ids_ref[four : four + 1, :] = ids
         hot = mask(ids.astype(jnp.int32) == cell).astype(BF)
-        total = total + dot(hot, jnp.concatenate([block[0:32] for block in blocks], axis=0))
+        total = total + dot(hot, got_ref[4 * four : 4 * four + 4, 0:16].reshape(128, 128))
     cells = total.astype(BF)
     for peer in range(cells_ref.shape[0]):
         cells_ref[peer] = cells
@@ -122,12 +121,17 @@
         out_ref[128 * four : 128 * four + 128, :] = dot(hot, local, ((0,), (0,))).astype(BF)
 
 
-def field_kernel(rows_ref, picked_ref, out_ref):
+def basis_kernel(rows_ref, out_ref):
     to, at = iota((128, 256), 0), iota((128, 256), 1)
     part = mask(at == 2 * to + 1).astype(BF)
     for k in range(8):
-        basis = dot(part, rows_ref[256 * k : 256 * k + 256, :])
+        out_ref[128 * k : 128 * k + 128, :] = dot(part, rows_ref[256 * k : 256 * k + 256, :]).astype(BF)
+
+
+def field_kernel(basis_ref, picked_ref, out_ref):
+    for k in range(8):
         picked = [picked_ref[:, 2 * k + j].reshape(64, 128) for j in range(2)]
+        basis = basis_ref[128 * k : 128 * k + 128, :].astype(F32)
         product = basis * jnp.concatenate(picked, axis=0).astype(F32)
         out_ref[k : k + 1, :] = jnp.sum(product, axis=1)[None] * (128 ** -0.5)
 
@@ -152,7 +156,7 @@
     return s % 4 * 16 + s // 4
 
 
-def call(kernel, out_shape, in_specs, scratch=()):
+def call(kernel, out_shape, in_specs, scratch=(), cost=None):
     many = isinstance(out_shape, list)
     return pl.pallas_call(
         kernel,
@@ -161,6 +165,7 @@
         out_specs=[VMEM] * len(out_shape) if many else VMEM,
         scratch_shapes=list(scratch),
         compiler_params=pltpu.CompilerParams(vmem_limit_bytes=40 * 1024 * 1024),
+        cost_estimate=cost and pl.CostEstimate(flops=cost, bytes_accessed=786432, transcendentals=0),
     )
 
 
@@ -180,14 +185,16 @@
     moments = exchange(moments.reshape(528, 2, 128), COLUMN)
     m2l_ops, moments = lax.optimization_barrier((m2l_ops, moments))
     moments, shifts = call(
-        regroup_kernel, [shape(32, 24, 2, 128), shape(8, 128, kind=jnp.int32)], [VMEM]
+        regroup_kernel, [shape(32, 17, 2, 128), shape(8, 128, kind=jnp.int32)], [VMEM]
     )(moments.reshape(16, 33, 2, 128))
-    moments = exchange(moments.reshape(768, 2, 128), LAYER).reshape(32, 48, 128)
+    moments = exchange(moments.reshape(544, 2, 128), LAYER).reshape(32, 17, 2, 128)
     ops = lax.ppermute(m2l_ops, ("zh", "y", "c", "zl"), ops_moves())
     cells, ids = call(sum_kernel, [shape(8, 128, 128), shape(8, 128, kind=F32)], [VMEM])(moments)
     slab = exchange(cells, GROUP).reshape(1024, 128)
     low = lax.ppermute(slab[256:], SLABS, [(slab_spot(i), slab_spot(i + 1)) for i in range(63)])
     high = lax.ppermute(slab[:512], SLABS, [(slab_spot(i + 1), slab_spot(i)) for i in range(63)])
+    basis = call(basis_kernel, shape(1024, 128), [VMEM], cost=67_000_000)(rows)
+    ops, basis = lax.optimization_barrier((ops, basis))
     parts = call(
         m2l_kernel,
         shape(1024, 128),
@@ -197,7 +204,7 @@
     parts = exchange(parts.reshape(8, 128, 128), GROUP)
     picked = call(pick_kernel, shape(1024, 128), [VMEM, VMEM])(ids, parts)
     picked = exchange(picked.reshape(512, 2, 128), LAYER + COLUMN).reshape(32, 16, 2, 128)
-    return call(field_kernel, shape(8, 128, kind=F32), [VMEM, VMEM])(rows, picked).reshape(1024)
+    return call(field_kernel, shape(8, 128, kind=F32), [VMEM, VMEM])(basis, picked).reshape(1024)
 
 
 def solution(mesh):

time: 131 us -> 130 us (level)
  waiting for transfers between devices: 9.14 us -> 7.69 us
where the time goes in v9:
time: 130 us
  blocking collectives  90.9 us (70%)
  starting transfers between devices  22.4 us (17%)
  waiting for transfers between devices  7.69 us (6%)
  Pallas kernels  6.17 us (5%)
  local copies, waits for them, and re-layouts  2.44 us (2%)
    all_to_all x4, blocking collectives, exchange(): return lax.all_to_all(array, axes, split_axis=0, concat_axis=0, tiled=True)  90.9 us
    all_to_all x1, starting transfers between devices, exchange(): return lax.all_to_all(array, axes, split_axis=0, concat_axis=0, tiled=True)  13.3 us
    ppermute x1, starting transfers between devices, body(): ops = lax.ppermute(m2l_ops, ('zh', 'y', 'c', 'zl'), ops_moves())  5.55 us
    ppermute x1, waiting for transfers between devices, body(): lax.ppermute(slab[:512], SLABS, [(slab_spot(i + 1), slab_spot(i)) for i i...  4.1 us
    all_to_all x1, waiting for transfers between devices, exchange(): return lax.all_to_all(array, axes, split_axis=0, concat_axis=0, tiled=True)  3.58 us
  transfers between devices with their start and end apart: 4, of which 2 were waited for; matrix products, arithmetic and copies ran while one was open for 0% of the time, Pallas kernels for 0%

profile of v9, /device:TPU:1, one launch (start us, length us, event | category | flops | bytes accessed | tf_op | source)
XLA Modules:
  0.0 129.7 jit_solution(8580890015812160618)
XLA Ops:
  0.0 0.7 copy-done.2
  0.7 1.0 copy-done
  1.7 0.7 copy-done.3
  2.4 0.9 shard_map.46
  3.3 28.8 %all_to_all.25 = bf16[528,2,128]{2,1,0:T(2,128)(2,1)S(1)} all-to-all(bf16[528,2,128]{2,1,0:T(2,128)(2,1)S(1)} %bitcast.18), channel_id=1, replica_groups=mesh['x'=4,'zh'=2,'y'=4,'c'=2,'zl'=8] {'zh','zl'}, dimensions={0} | all-to-all | bytes 540672 | tf_op jit(solution)/shard_map/all_to_all | solution.py:177
  32.1 1.0 shard_map.48
  33.1 13.3 %all-to-all-start.1 = ((bf16[544,2,128]{2,1,0:T(2,128)(2,1)}), bf16[544,2,128]{2,1,0:T(2,128)(2,1)S(1)}, u32[]{:S(2)}, u32[]{:S(2)}) async-start(bf16[544,2,128]{2,1,0:T(2,128)(2,1)} %bitcast.5), calls=%async_computation.1 | async-start | bytes 557056 | tf_op jit(solution)/shard_map/all_to_all | solution.py:177
  46.5 0.0 copy-done.4
  46.5 5.6 %collective-permute-start = (bf16[16,128,128]{2,1,0:T(8,128)(2,1)S(1)}, bf16[16,128,128]{2,1,0:T(8,128)(2,1)S(1)}, u32[]{:S(2)}, u32[]{:S(2)}) collective-permute-start(bf16[16,128,128]{2,1,0:T(8,128)(2,1)S(1)} %copy-done.4), channel_id=1, source_target_pairs={{0,0},{12,8},{17,16},{95,24},{34,32},{110,40},{51,48},{125,56},{1,... | collective-permute-start | bytes 1572872 | tf_op jit(solution)/shard_map/ppermute | solution.py:191
  52.0 3.6 %all-to-all-done.1 = bf16[544,2,128]{2,1,0:T(2,128)(2,1)S(1)} async-done(((bf16[544,2,128]{2,1,0:T(2,128)(2,1)}), bf16[544,2,128]{2,1,0:T(2,128)(2,1)S(1)}, u32[]{:S(2)}, u32[]{:S(2)}) %all-to-all-start.1) | async-done | bytes 278560 | tf_op jit(solution)/shard_map/all_to_all | solution.py:177
  55.6 0.3 shard_map.49
  55.9 0.0 copy-start.1
  56.0 9.2 %all_to_all.26 = bf16[8,128,128]{2,1,0:T(8,128)(2,1)S(1)} all-to-all(bf16[8,128,128]{2,1,0:T(8,128)(2,1)S(1)} %get-tuple-element.20), channel_id=1, replica_groups=mesh['x'=4,'zh'=2,'y'=4,'c'=2,'zl'=8] {'y','c'}, dimensions={0} | all-to-all | bytes 524288 | tf_op jit(solution)/shard_map/all_to_all | solution.py:177
  65.2 2.2 %collective-permute-start.1 = (bf16[768,128]{1,0:T(8,128)(2,1)S(1)}, bf16[768,128]{1,0:T(8,128)(2,1)S(1)}, u32[]{:S(2)}, u32[]{:S(2)}) collective-permute-start(bf16[768,128]{1,0:T(8,128)(2,1)S(1)} %bitcast.25), channel_id=1, source_target_pairs={{0,128},{128,256},{256,384},{384,1},{1,129},{129,257},{257,385},{3... | collective-permute-start | bytes 589832 | tf_op jit(solution)/shard_map/ppermute | solution.py:194
  67.4 1.3 collective-permute-start.2
  68.7 0.3 shard_map.47.basis_ref
  69.0 0.0 collective-permute-done.ops_ref
  69.0 4.1 %collective-permute-done.2.high_ref = bf16[512,128]{1,0:T(8,128)(2,1)S(1)} collective-permute-done((bf16[512,128]{1,0:T(8,128)(2,1)S(1)}, bf16[512,128]{1,0:T(8,128)(2,1)S(1)}, u32[]{:S(2)}, u32[]{:S(2)}) %collective-permute-start.2) | collective-permute-done | bytes 131104 | tf_op jit(solution)/shard_map/ppermute | solution.py:195
  73.1 0.0 collective-permute-done.1.low_ref
  73.1 2.5 %shard_map.50 = bf16[1024,128]{1,0:T(8,128)(2,1)S(1)} custom-call(s32[8,128]{1,0:T(8,128)S(1)} %get-tuple-element.18.offsets_ref, bf16[16,128,128]{2,1,0:T(8,128)(2,1)S(1)} %collective-permute-done.ops_ref, bf16[1024,128]{1,0:T(8,128)(2,1)S(1)} %bitcast.14, bf16[768,128]{1,0:T(8,128)(2,1)S(1)} %collective-permute-done.1.low_ref, ...), custom_call_target="tpu_custom_call" | custom-call | tf_op jit(solution)/shard_map/pallas_call | solution.py:198
  75.7 11.4 %all_to_all.27.parts_ref = bf16[8,128,128]{2,1,0:T(8,128)(2,1)S(1)} all-to-all(bf16[8,128,128]{2,1,0:T(8,128)(2,1)S(1)} %bitcast.22), channel_id=1, replica_groups=mesh['x'=4,'zh'=2,'y'=4,'c'=2,'zl'=8] {'y','c'}, dimensions={0} | all-to-all | bytes 524288 | tf_op jit(solution)/shard_map/all_to_all | solution.py:177
  87.1 0.3 shard_map.51
  87.4 41.5 %all_to_all.28 = bf16[512,2,128]{2,1,0:T(2,128)(2,1)S(1)} all-to-all(bf16[512,2,128]{2,1,0:T(2,128)(2,1)S(1)} %bitcast.20), channel_id=1, replica_groups=mesh['x'=4,'zh'=2,'y'=4,'c'=2,'zl'=8] {'x','y','c','zh','zl'}, dimensions={0} | all-to-all | bytes 524288 | tf_op jit(solution)/shard_map/all_to_all | solution.py:177
  128.8 0.9 shard_map.52
  (7 shorter events, 0.0 us)
Async XLA Ops:
  0.0 0.7 copy-start.2
  0.7 1.0 copy-start
  1.7 0.7 copy-start.3
  32.1 14.4 %copy-start.4 = (bf16[16,128,128]{2,1,0:T(8,128)(2,1)S(1)}, bf16[16,128,128]{2,1,0:T(8,128)(2,1)}, u32[]{:S(2)}) copy-start(bf16[16,128,128]{2,1,0:T(8,128)(2,1)} %param.6) | copy-start | bytes 1572868
  33.1 22.5 %all-to-all-start.1 = ((bf16[544,2,128]{2,1,0:T(2,128)(2,1)}), bf16[544,2,128]{2,1,0:T(2,128)(2,1)S(1)}, u32[]{:S(2)}, u32[]{:S(2)}) async-start(bf16[544,2,128]{2,1,0:T(2,128)(2,1)} %bitcast.5), calls=%async_computation.1 | async-start | bytes 557056 | tf_op jit(solution)/shard_map/all_to_all | solution.py:177
  46.5 22.5 %collective-permute-start = (bf16[16,128,128]{2,1,0:T(8,128)(2,1)S(1)}, bf16[16,128,128]{2,1,0:T(8,128)(2,1)S(1)}, u32[]{:S(2)}, u32[]{:S(2)}) collective-permute-start(bf16[16,128,128]{2,1,0:T(8,128)(2,1)S(1)} %copy-done.4), channel_id=1, source_target_pairs={{0,0},{12,8},{17,16},{95,24},{34,32},{110,40},{51,48},{125,56},{1,... | collective-permute-start | bytes 1572872 | tf_op jit(solution)/shard_map/ppermute | solution.py:191
  55.9 12.8 %copy-start.1 = (bf16[1024,2,128]{2,1,0:T(2,128)(2,1)S(1)}, bf16[1024,2,128]{2,1,0:T(2,128)(2,1)}, u32[]{:S(2)}) copy-start(bf16[1024,2,128]{2,1,0:T(2,128)(2,1)} %param.4) | copy-start | bytes 1572868
  65.2 8.0 %collective-permute-start.1 = (bf16[768,128]{1,0:T(8,128)(2,1)S(1)}, bf16[768,128]{1,0:T(8,128)(2,1)S(1)}, u32[]{:S(2)}, u32[]{:S(2)}) collective-permute-start(bf16[768,128]{1,0:T(8,128)(2,1)S(1)} %bitcast.25), channel_id=1, source_target_pairs={{0,128},{128,256},{256,384},{384,1},{1,129},{129,257},{257,385},{3... | collective-permute-start | bytes 589832 | tf_op jit(solution)/shard_map/ppermute | solution.py:194
  67.4 5.7 %collective-permute-start.2 = (bf16[512,128]{1,0:T(8,128)(2,1)S(1)}, bf16[512,128]{1,0:T(8,128)(2,1)S(1)}, u32[]{:S(2)}, u32[]{:S(2)}) collective-permute-start(bf16[512,128]{1,0:T(8,128)(2,1)S(1)} %bitcast.26), channel_id=1, source_target_pairs={{128,0},{256,128},{384,256},{1,384},{129,1},{257,129},{385,257},{2... | collective-permute-start | bytes 393224 | tf_op jit(solution)/shard_map/ppermute | solution.py:195

commit v10 on v9

--- a/solution.py
+++ b/solution.py
@@ -89,16 +89,28 @@
         cells_ref[peer] = cells
 
 
-def m2l_kernel(offsets_ref, ops_ref, own_ref, low_ref, high_ref, out_ref, rows, shifted):
+def fill(rows, shifted, plane, values):
+    rows[:, 8:40, :] = values.astype(F32).reshape(GX, GY, 128)
+    for dy in range(6):
+        shifted[dy, plane, 3:11] = rows[:, 5 + dy : 37 + dy, :].astype(BF)
+
+
+def shift_kernel(own_ref, shifted, rows):
     shifted[:, :, 0:3] = jnp.zeros((6, 9, 3, GY, 128), BF)
     shifted[:, :, 11:13] = jnp.zeros((6, 9, 2, GY, 128), BF)
     rows[:, 0:8, :] = jnp.zeros((GX, 8, 128), F32)
     rows[:, 40:48, :] = jnp.zeros((GX, 8, 128), F32)
-    for plane in range(9):
-        ref, at = (low_ref, plane) if plane < 3 else (own_ref, plane - 3) if plane < 7 else (high_ref, plane - 7)
-        rows[:, 8:40, :] = ref[at * 256 : (at + 1) * 256, :].astype(F32).reshape(GX, GY, 128)
-        for dy in range(6):
-            shifted[dy, plane, 3:11] = rows[:, 5 + dy : 37 + dy, :].astype(BF)
+    for plane in range(CZS):
+        fill(rows, shifted, plane + 3, own_ref[plane * 256 : (plane + 1) * 256, :])
+
+
+def m2l_kernel(offsets_ref, ops_ref, low_ref, high_ref, given_ref, out_ref, shifted, rows):
+    rows[:, 0:8, :] = jnp.zeros((GX, 8, 128), F32)
+    rows[:, 40:48, :] = jnp.zeros((GX, 8, 128), F32)
+    for plane in range(3):
+        fill(rows, shifted, plane, low_ref[plane * 256 : (plane + 1) * 256, :])
+    for plane in range(2):
+        fill(rows, shifted, plane + 7, high_ref[plane * 256 : (plane + 1) * 256, :])
     ops = ops_ref[...].reshape(16 * 128, 128)
     for z in range(CZS):
         windows = []
@@ -156,7 +168,7 @@
     return s % 4 * 16 + s // 4
 
 
-def call(kernel, out_shape, in_specs, scratch=(), cost=None):
+def call(kernel, out_shape, in_specs, scratch=(), cost=None, aliases={}):
     many = isinstance(out_shape, list)
     return pl.pallas_call(
         kernel,
@@ -164,6 +176,7 @@
         in_specs=in_specs,
         out_specs=[VMEM] * len(out_shape) if many else VMEM,
         scratch_shapes=list(scratch),
+        input_output_aliases=aliases,
         compiler_params=pltpu.CompilerParams(vmem_limit_bytes=40 * 1024 * 1024),
         cost_estimate=cost and pl.CostEstimate(flops=cost, bytes_accessed=786432, transcendentals=0),
     )
@@ -195,12 +208,12 @@
     high = lax.ppermute(slab[:512], SLABS, [(slab_spot(i + 1), slab_spot(i)) for i in range(63)])
     basis = call(basis_kernel, shape(1024, 128), [VMEM], cost=67_000_000)(rows)
     ops, basis = lax.optimization_barrier((ops, basis))
-    parts = call(
-        m2l_kernel,
-        shape(1024, 128),
-        [SMEM, VMEM, VMEM, VMEM, VMEM],
-        [pltpu.VMEM((GX, 48, 128), F32), pltpu.VMEM((6, 9, 13, GY, 128), BF)],
-    )(shifts, ops, slab, low, high)
+    buffer = shape(6, 9, 13, GY, 128)
+    rows = [pltpu.VMEM((GX, 48, 128), F32)]
+    shifted = call(shift_kernel, buffer, [VMEM], rows, cost=100_000_000)(slab)
+    parts, _ = call(
+        m2l_kernel, [shape(1024, 128), buffer], [SMEM, VMEM, VMEM, VMEM, VMEM], rows, aliases={4: 1}
+    )(shifts, ops, low, high, shifted)
     parts = exchange(parts.reshape(8, 128, 128), GROUP)
     picked = call(pick_kernel, shape(1024, 128), [VMEM, VMEM])(ids, parts)
     picked = exchange(picked.reshape(512, 2, 128), LAYER + COLUMN).reshape(32, 16, 2, 128)

time: 130 us -> 130 us (level)
  waiting for transfers between devices: 7.69 us -> 6.18 us
    ppermute x1, waiting for transfers between devices: 4.1 us -> 2.58 us  [body(): lax.ppermute(slab[:512], SLABS, [(slab_spot(i + 1), slab_spot(i)) for i i...]
    unnamed x10 -> x8, local copies, waits for them, and re-layouts: 2.42 us -> 3.45 us
  transfers between devices with their start and end apart: 4 -> 4, of which waited for: 2 -> 2; matrix products, arithmetic and copies ran while one was open for 0% -> 0% of each run, Pallas kernels for 0% -> 1%
where the time goes in v10:
time: 130 us; the launch traced here: 129 us
  blocking collectives  90.7 us (70%)
  starting transfers between devices  22.4 us (17%)
  Pallas kernels  6.18 us (5%)
  waiting for transfers between devices  6.18 us (5%)
  local copies, waits for them, and re-layouts  3.47 us (3%)
    all_to_all x4, blocking collectives, exchange(): return lax.all_to_all(array, axes, split_axis=0, concat_axis=0, tiled=True)  90.7 us
    all_to_all x1, starting transfers between devices, exchange(): return lax.all_to_all(array, axes, split_axis=0, concat_axis=0, tiled=True)  13.3 us
    ppermute x1, starting transfers between devices, body(): ops = lax.ppermute(m2l_ops, ('zh', 'y', 'c', 'zl'), ops_moves())  5.55 us
    all_to_all x1, waiting for transfers between devices, exchange(): return lax.all_to_all(array, axes, split_axis=0, concat_axis=0, tiled=True)  3.59 us
    unnamed x8, local copies, waits for them, and re-layouts  3.45 us
  transfers between devices with their start and end apart: 4, of which 2 were waited for; matrix products, arithmetic and copies ran while one was open for 0% of the time, Pallas kernels for 1%

profile of v10, /device:TPU:1, one launch (start us, length us, event | category | flops | bytes accessed | tf_op | source)
XLA Modules:
  0.0 129.1 jit_solution(12312571283096681674)
XLA Ops:
  0.0 1.0 copy-done
  1.0 0.7 copy-done.2
  1.7 0.7 copy-done.3
  2.4 0.9 shard_map.46
  3.3 28.8 %all_to_all.25 = bf16[528,2,128]{2,1,0:T(2,128)(2,1)S(1)} all-to-all(bf16[528,2,128]{2,1,0:T(2,128)(2,1)S(1)} %bitcast.18), channel_id=1, replica_groups=mesh['x'=4,'zh'=2,'y'=4,'c'=2,'zl'=8] {'zh','zl'}, dimensions={0} | all-to-all | bytes 540672 | tf_op jit(solution)/shard_map/all_to_all | solution.py:190
  32.1 1.0 shard_map.48
  33.1 13.3 %all-to-all-start.1 = ((bf16[544,2,128]{2,1,0:T(2,128)(2,1)}), bf16[544,2,128]{2,1,0:T(2,128)(2,1)S(1)}, u32[]{:S(2)}, u32[]{:S(2)}) async-start(bf16[544,2,128]{2,1,0:T(2,128)(2,1)} %bitcast.5), calls=%async_computation.1 | async-start | bytes 557056 | tf_op jit(solution)/shard_map/all_to_all | solution.py:190
  46.5 5.6 %collective-permute-start = (bf16[16,128,128]{2,1,0:T(8,128)(2,1)}, bf16[16,128,128]{2,1,0:T(8,128)(2,1)S(1)}, u32[]{:S(2)}, u32[]{:S(2)}) collective-permute-start(bf16[16,128,128]{2,1,0:T(8,128)(2,1)} %param.6), channel_id=1, source_target_pairs={{0,0},{12,8},{17,16},{95,24},{34,32},{110,40},{51,48},{125,56},{1,... | collective-permute-start | bytes 1572872 | tf_op jit(solution)/shard_map/ppermute | solution.py:204
  52.0 3.6 %all-to-all-done.1 = bf16[544,2,128]{2,1,0:T(2,128)(2,1)S(1)} async-done(((bf16[544,2,128]{2,1,0:T(2,128)(2,1)}), bf16[544,2,128]{2,1,0:T(2,128)(2,1)S(1)}, u32[]{:S(2)}, u32[]{:S(2)}) %all-to-all-start.1) | async-done | bytes 278560 | tf_op jit(solution)/shard_map/all_to_all | solution.py:190
  55.6 0.3 shard_map.49
  55.9 9.1 %all_to_all.26 = bf16[8,128,128]{2,1,0:T(8,128)(2,1)S(1)} all-to-all(bf16[8,128,128]{2,1,0:T(8,128)(2,1)S(1)} %get-tuple-element.21), channel_id=1, replica_groups=mesh['x'=4,'zh'=2,'y'=4,'c'=2,'zl'=8] {'y','c'}, dimensions={0} | all-to-all | bytes 524288 | tf_op jit(solution)/shard_map/all_to_all | solution.py:190
  65.0 2.2 %collective-permute-start.1 = (bf16[768,128]{1,0:T(8,128)(2,1)S(1)}, bf16[768,128]{1,0:T(8,128)(2,1)S(1)}, u32[]{:S(2)}, u32[]{:S(2)}) collective-permute-start(bf16[768,128]{1,0:T(8,128)(2,1)S(1)} %bitcast.25), channel_id=1, source_target_pairs={{0,128},{128,256},{256,384},{384,1},{1,129},{129,257},{257,385},{3... | collective-permute-start | bytes 589832 | tf_op jit(solution)/shard_map/ppermute | solution.py:207
  67.3 1.3 %collective-permute-start.2 = (bf16[512,128]{1,0:T(8,128)(2,1)S(1)}, bf16[512,128]{1,0:T(8,128)(2,1)S(1)}, u32[]{:S(2)}, u32[]{:S(2)}) collective-permute-start(bf16[512,128]{1,0:T(8,128)(2,1)S(1)} %bitcast.26), channel_id=1, source_target_pairs={{128,0},{256,128},{384,256},{1,384},{129,1},{257,129},{385,257},{2... | collective-permute-start | bytes 393224 | tf_op jit(solution)/shard_map/ppermute | solution.py:208
  68.6 0.0 copy-start.1
  68.6 1.0 copy-done.1
  69.6 0.3 shard_map.47.basis_ref
  69.9 0.5 shard_map.50.given_ref
  70.4 0.0 collective-permute-done.ops_ref
  70.4 2.6 %collective-permute-done.2.high_ref = bf16[512,128]{1,0:T(8,128)(2,1)S(1)} collective-permute-done((bf16[512,128]{1,0:T(8,128)(2,1)S(1)}, bf16[512,128]{1,0:T(8,128)(2,1)S(1)}, u32[]{:S(2)}, u32[]{:S(2)}) %collective-permute-start.2) | collective-permute-done | bytes 131104 | tf_op jit(solution)/shard_map/ppermute | solution.py:208
  73.0 2.1 %shard_map.51 = (bf16[1024,128]{1,0:T(8,128)(2,1)S(1)}, bf16[6,9,13,32,128]{4,3,2,1,0:T(8,128)(2,1)S(1)}) custom-call(s32[8,128]{1,0:T(8,128)S(1)} %get-tuple-element.19.offsets_ref, bf16[16,128,128]{2,1,0:T(8,128)(2,1)S(1)} %collective-permute-done.ops_ref, bf16[768,128]{1,0:T(8,128)(2,1)S(1)} %collective-permute-done.1.low_ref, ...), custom_call_target="tpu_custom_call", output_to_operand_aliasing={{1}: (4, {})} | custom-call | tf_op jit(solution)/shard_map/pallas_call | solution.py:214
  75.1 11.4 %all_to_all.27.parts_ref = bf16[8,128,128]{2,1,0:T(8,128)(2,1)S(1)} all-to-all(bf16[8,128,128]{2,1,0:T(8,128)(2,1)S(1)} %bitcast.22), channel_id=1, replica_groups=mesh['x'=4,'zh'=2,'y'=4,'c'=2,'zl'=8] {'y','c'}, dimensions={0} | all-to-all | bytes 524288 | tf_op jit(solution)/shard_map/all_to_all | solution.py:190
  86.5 0.3 shard_map.52
  86.7 41.5 %all_to_all.28 = bf16[512,2,128]{2,1,0:T(2,128)(2,1)S(1)} all-to-all(bf16[512,2,128]{2,1,0:T(2,128)(2,1)S(1)} %bitcast.20), channel_id=1, replica_groups=mesh['x'=4,'zh'=2,'y'=4,'c'=2,'zl'=8] {'x','y','c','zh','zl'}, dimensions={0} | all-to-all | bytes 524288 | tf_op jit(solution)/shard_map/all_to_all | solution.py:190
  128.2 0.8 shard_map.53
  (6 shorter events, 0.0 us)
Async XLA Ops:
  0.0 1.0 copy-start
  1.0 0.7 copy-start.2
  1.7 0.7 copy-start.3
  33.1 22.5 %all-to-all-start.1 = ((bf16[544,2,128]{2,1,0:T(2,128)(2,1)}), bf16[544,2,128]{2,1,0:T(2,128)(2,1)S(1)}, u32[]{:S(2)}, u32[]{:S(2)}) async-start(bf16[544,2,128]{2,1,0:T(2,128)(2,1)} %bitcast.5), calls=%async_computation.1 | async-start | bytes 557056 | tf_op jit(solution)/shard_map/all_to_all | solution.py:190
  46.5 23.9 %collective-permute-start = (bf16[16,128,128]{2,1,0:T(8,128)(2,1)}, bf16[16,128,128]{2,1,0:T(8,128)(2,1)S(1)}, u32[]{:S(2)}, u32[]{:S(2)}) collective-permute-start(bf16[16,128,128]{2,1,0:T(8,128)(2,1)} %param.6), channel_id=1, source_target_pairs={{0,0},{12,8},{17,16},{95,24},{34,32},{110,40},{51,48},{125,56},{1,... | collective-permute-start | bytes 1572872 | tf_op jit(solution)/shard_map/ppermute | solution.py:204
  65.0 8.0 %collective-permute-start.1 = (bf16[768,128]{1,0:T(8,128)(2,1)S(1)}, bf16[768,128]{1,0:T(8,128)(2,1)S(1)}, u32[]{:S(2)}, u32[]{:S(2)}) collective-permute-start(bf16[768,128]{1,0:T(8,128)(2,1)S(1)} %bitcast.25), channel_id=1, source_target_pairs={{0,128},{128,256},{256,384},{384,1},{1,129},{129,257},{257,385},{3... | collective-permute-start | bytes 589832 | tf_op jit(solution)/shard_map/ppermute | solution.py:207
  67.3 5.7 %collective-permute-start.2 = (bf16[512,128]{1,0:T(8,128)(2,1)S(1)}, bf16[512,128]{1,0:T(8,128)(2,1)S(1)}, u32[]{:S(2)}, u32[]{:S(2)}) collective-permute-start(bf16[512,128]{1,0:T(8,128)(2,1)S(1)} %bitcast.26), channel_id=1, source_target_pairs={{128,0},{256,128},{384,256},{1,384},{129,1},{257,129},{385,257},{2... | collective-permute-start | bytes 393224 | tf_op jit(solution)/shard_map/ppermute | solution.py:208
  68.6 1.0 copy-start.1

commit v11 on v10

--- a/solution.py
+++ b/solution.py
@@ -15,8 +15,7 @@
 BF = jnp.bfloat16
 F32 = jnp.float32
 
-COLUMN = ("zh", "zl")
-LAYER = ("x", "y", "c")
+WIDE = ("zh", "zl", "x")
 SLABS = ("x", "zh", "zl")
 GROUP = ("y", "c")
 VMEM = pl.BlockSpec(memory_space=pltpu.VMEM)
@@ -39,51 +38,53 @@
     to, at = iota((64, 128), 0), iota((64, 128), 1)
     part = mask(at == 2 * to).astype(BF)
     for z in range(16):
-        moments_ref[z, 0:32] = dot(part, rows_ref[128 * z : 128 * z + 128, :]).astype(BF).reshape(32, 2, 128)
+        moments = dot(part, rows_ref[128 * z : 128 * z + 128, :]).astype(BF)
+        moments_ref[4 * z : 4 * z + 4, 0:8] = moments.reshape(4, 8, 2, 128)
     inside = jnp.bitwise_and(cells_ref[...], RUN - 1).astype(F32)
     lane = iota((1, 128), 1)
     shifts = jnp.zeros((1, 128), F32)
     for k in range(16):
         for j in range(3):
             shifts = jnp.where(lane == 3 * k + j, offsets_ref[j, k].astype(F32), shifts)
-    rows = []
-    for z in range(16):
-        rows += [inside[z // 2 : z // 2 + 1], shifts]
-    moments_ref[:, 32] = jnp.concatenate(rows, axis=0).astype(BF).reshape(16, 2, 128)
+    row = iota((16, 128), 0)
+    for k in range(8):
+        pairs = jnp.where(row % 2 == 0, inside[k : k + 1], shifts).astype(BF)
+        moments_ref[8 * k : 8 * k + 8, 8] = pairs.reshape(8, 2, 128)
 
 
 def regroup_kernel(got_ref, out_ref, offsets_ref):
-    peer, layer = lax.axis_index("y") * 2 + lax.axis_index("c"), lax.axis_index("zl")
-    quarter, half = lax.rem(peer, 4), lax.rem(layer, 2)
+    layer = lax.axis_index("zl")
+    peer = lax.axis_index("y") * 2 + lax.axis_index("c")
+    seat = lax.rem(layer, 2) * 4 + lax.axis_index("x")
     reach = jnp.int32(0)
     for a in range(8):
         reach = jnp.where(peer == a, REACH[a] % 8, reach)
     shard = lax.rem(layer + reach, 8)
-    for z in range(16):
-        out_ref[:, z] = got_ref[z, 0:32]
-    extra = got_ref[:, 32].reshape(32, 128)
-    row, lane = iota((32, 128), 0), iota((32, 128), 1)
-    take_row, take_lane = iota((64, 128), 0), iota((64, 128), 1)
-    ids = jnp.zeros((64, 128), F32)
+    for owner in range(8):
+        out_ref[owner, 0:64] = got_ref[:, owner]
+    extra = got_ref[:, 8].reshape(128, 128)
+    row, lane = iota((128, 128), 0), iota((128, 128), 1)
+    take_row, take_lane = iota((16, 128), 0), iota((16, 128), 1)
+    ids = jnp.zeros((16, 128), F32)
     for i in range(2):
-        put = mask((row % 2 == 0) & (lane - 32 * quarter == row + i))
-        take = mask((take_row % 2 == 0) & (take_lane == 64 * half + take_row + i))
+        put = mask((row % 2 == 0) & (lane == row + i))
+        take = mask((take_row % 2 == 0) & (take_lane == 16 * seat + take_row + i))
         taken = dot(take.astype(BF), extra, ((1,), (1,)))
         ids = ids + dot(taken.astype(BF), put.astype(BF))
-    out_ref[:, 16] = ids.astype(BF).reshape(32, 2, 128)
-    own = jnp.sum(mask(row == 2 * shard + 1) * extra.astype(F32), axis=0, keepdims=True)
+    out_ref[:, 64] = ids.astype(BF).reshape(8, 2, 128)
+    own = jnp.sum(mask(row == 8 * shard + 1) * extra.astype(F32), axis=0, keepdims=True)
     offsets_ref[...] = jnp.broadcast_to(own, (8, 128)).astype(jnp.int32)
 
 
 def sum_kernel(got_ref, cells_ref, ids_ref):
     cell = iota((128, 128), 0)
     total = jnp.zeros((128, 128), F32)
-    every = got_ref[:, 16].reshape(64, 128).astype(F32)
-    for four in range(8):
-        ids = jnp.sum(every[8 * four : 8 * four + 8], axis=0, keepdims=True)
-        ids_ref[four : four + 1, :] = ids
+    every = got_ref[:, 64].reshape(16, 128).astype(F32)
+    for peer in range(8):
+        ids = jnp.sum(every[2 * peer : 2 * peer + 2], axis=0, keepdims=True)
+        ids_ref[peer : peer + 1, :] = ids
         hot = mask(ids.astype(jnp.int32) == cell).astype(BF)
-        total = total + dot(hot, got_ref[4 * four : 4 * four + 4, 0:16].reshape(128, 128))
+        total = total + dot(hot, got_ref[peer, 0:64].reshape(128, 128))
     cells = total.astype(BF)
     for peer in range(cells_ref.shape[0]):
         cells_ref[peer] = cells
@@ -142,7 +143,7 @@
 
 def field_kernel(basis_ref, picked_ref, out_ref):
     for k in range(8):
-        picked = [picked_ref[:, 2 * k + j].reshape(64, 128) for j in range(2)]
+        picked = [picked_ref[:, 8 * k + j].reshape(16, 128) for j in range(8)]
         basis = basis_ref[128 * k : 128 * k + 128, :].astype(F32)
         product = basis * jnp.concatenate(picked, axis=0).astype(F32)
         out_ref[k : k + 1, :] = jnp.sum(product, axis=1)[None] * (128 ** -0.5)
@@ -192,15 +193,15 @@
 
 def body(bead_data, bead_cell, m2l_ops, offsets):
     rows = bead_data.reshape(2048, 128)
-    moments = call(pack_kernel, shape(16, 33, 2, 128), [SMEM, VMEM, VMEM])(
+    moments = call(pack_kernel, shape(64, 9, 2, 128), [SMEM, VMEM, VMEM])(
         offsets.T, rows, bead_cell.reshape(8, 128)
     )
-    moments = exchange(moments.reshape(528, 2, 128), COLUMN)
+    moments = exchange(moments.reshape(576, 2, 128), WIDE)
     m2l_ops, moments = lax.optimization_barrier((m2l_ops, moments))
     moments, shifts = call(
-        regroup_kernel, [shape(32, 17, 2, 128), shape(8, 128, kind=jnp.int32)], [VMEM]
-    )(moments.reshape(16, 33, 2, 128))
-    moments = exchange(moments.reshape(544, 2, 128), LAYER).reshape(32, 17, 2, 128)
+        regroup_kernel, [shape(8, 65, 2, 128), shape(8, 128, kind=jnp.int32)], [VMEM]
+    )(moments.reshape(64, 9, 2, 128))
+    moments = exchange(moments.reshape(520, 2, 128), GROUP).reshape(8, 65, 2, 128)
     ops = lax.ppermute(m2l_ops, ("zh", "y", "c", "zl"), ops_moves())
     cells, ids = call(sum_kernel, [shape(8, 128, 128), shape(8, 128, kind=F32)], [VMEM])(moments)
     slab = exchange(cells, GROUP).reshape(1024, 128)
@@ -216,7 +217,7 @@
     )(shifts, ops, low, high, shifted)
     parts = exchange(parts.reshape(8, 128, 128), GROUP)
     picked = call(pick_kernel, shape(1024, 128), [VMEM, VMEM])(ids, parts)
-    picked = exchange(picked.reshape(512, 2, 128), LAYER + COLUMN).reshape(32, 16, 2, 128)
+    picked = exchange(picked.reshape(512, 2, 128), GROUP + WIDE).reshape(8, 64, 2, 128)
     return call(field_kernel, shape(8, 128, kind=F32), [VMEM, VMEM])(basis, picked).reshape(1024)
 
 

time: 130 us -> 131 us (level)
  blocking collectives: 90.7 us -> 99 us
  starting transfers between devices: 22.4 us -> 15.9 us
    all_to_all x4, blocking collectives: 90.7 us -> 99 us  [exchange(): return lax.all_to_all(array, axes, split_axis=0, concat_axis=0, tiled=True)]
    all_to_all x1, starting transfers between devices: 13.3 us -> 8.42 us  [exchange(): return lax.all_to_all(array, axes, split_axis=0, concat_axis=0, tiled=True)]
    ppermute x1, starting transfers between devices: 5.55 us -> 3.53 us  [body(): ops = lax.ppermute(m2l_ops, ('zh', 'y', 'c', 'zl'), ops_moves())]
where the time goes in v11:
time: 131 us; the launch traced here: 130 us
  blocking collectives  99 us (76%)
  starting transfers between devices  15.9 us (12%)
  Pallas kernels  6.14 us (5%)
  waiting for transfers between devices  5.6 us (4%)
  local copies, waits for them, and re-layouts  3.47 us (3%)
    all_to_all x4, blocking collectives, exchange(): return lax.all_to_all(array, axes, split_axis=0, concat_axis=0, tiled=True)  99 us
    all_to_all x1, starting transfers between devices, exchange(): return lax.all_to_all(array, axes, split_axis=0, concat_axis=0, tiled=True)  8.42 us
    ppermute x1, starting transfers between devices, body(): ops = lax.ppermute(m2l_ops, ('zh', 'y', 'c', 'zl'), ops_moves())  3.53 us
    unnamed x8, local copies, waits for them, and re-layouts  3.45 us
    all_to_all x1, waiting for transfers between devices, exchange(): return lax.all_to_all(array, axes, split_axis=0, concat_axis=0, tiled=True)  3.01 us
    ppermute x1, starting transfers between devices, body(): lax.ppermute(slab[256:], SLABS, [(slab_spot(i), slab_spot(i + 1)) for i i...  2.63 us
  transfers between devices with their start and end apart: 4, of which 2 were waited for; matrix products, arithmetic and copies ran while one was open for 0% of the time, Pallas kernels for 1%

profile of v11, /device:TPU:1, one launch (start us, length us, event | category | flops | bytes accessed | tf_op | source)
XLA Modules:
  0.0 130.2 jit_solution(9231158908184205472)
XLA Ops:
  0.0 1.0 copy-done
  1.0 0.7 copy-done.2
  1.7 0.7 copy-done.3
  2.4 0.9 shard_map.46
  3.3 39.4 %all_to_all.25 = bf16[576,2,128]{2,1,0:T(2,128)(2,1)S(1)} all-to-all(bf16[576,2,128]{2,1,0:T(2,128)(2,1)S(1)} %bitcast.17), channel_id=1, replica_groups=mesh['x'=4,'zh'=2,'y'=4,'c'=2,'zl'=8] {'zh','zl','x'}, dimensions={0} | all-to-all | bytes 589824 | tf_op jit(solution)/shard_map/all_to_all | solution.py:191
  42.7 1.0 shard_map.48
  43.7 8.4 %all-to-all-start.1 = ((bf16[520,2,128]{2,1,0:T(2,128)(2,1)}), bf16[520,2,128]{2,1,0:T(2,128)(2,1)S(1)}, u32[]{:S(2)}, u32[]{:S(2)}) async-start(bf16[520,2,128]{2,1,0:T(2,128)(2,1)} %bitcast.5), calls=%async_computation.1 | async-start | bytes 532480 | tf_op jit(solution)/shard_map/all_to_all | solution.py:191
  52.1 3.5 %collective-permute-start = (bf16[16,128,128]{2,1,0:T(8,128)(2,1)}, bf16[16,128,128]{2,1,0:T(8,128)(2,1)S(1)}, u32[]{:S(2)}, u32[]{:S(2)}) collective-permute-start(bf16[16,128,128]{2,1,0:T(8,128)(2,1)} %param.6), channel_id=1, source_target_pairs={{0,0},{12,8},{17,16},{95,24},{34,32},{110,40},{51,48},{125,56},{1,... | collective-permute-start | bytes 1572872 | tf_op jit(solution)/shard_map/ppermute | solution.py:205
  55.6 3.0 %all-to-all-done.1 = bf16[520,2,128]{2,1,0:T(2,128)(2,1)S(1)} async-done(((bf16[520,2,128]{2,1,0:T(2,128)(2,1)}), bf16[520,2,128]{2,1,0:T(2,128)(2,1)S(1)}, u32[]{:S(2)}, u32[]{:S(2)}) %all-to-all-start.1) | async-done | bytes 266272 | tf_op jit(solution)/shard_map/all_to_all | solution.py:191
  58.6 0.3 shard_map.49
  58.9 10.0 %all_to_all.26 = bf16[8,128,128]{2,1,0:T(8,128)(2,1)S(1)} all-to-all(bf16[8,128,128]{2,1,0:T(8,128)(2,1)S(1)} %get-tuple-element.21), channel_id=1, replica_groups=mesh['x'=4,'zh'=2,'y'=4,'c'=2,'zl'=8] {'y','c'}, dimensions={0} | all-to-all | bytes 524288 | tf_op jit(solution)/shard_map/all_to_all | solution.py:191
  68.9 2.6 %collective-permute-start.1 = (bf16[768,128]{1,0:T(8,128)(2,1)S(1)}, bf16[768,128]{1,0:T(8,128)(2,1)S(1)}, u32[]{:S(2)}, u32[]{:S(2)}) collective-permute-start(bf16[768,128]{1,0:T(8,128)(2,1)S(1)} %bitcast.25), channel_id=1, source_target_pairs={{0,128},{128,256},{256,384},{384,1},{1,129},{129,257},{257,385},{3... | collective-permute-start | bytes 589832 | tf_op jit(solution)/shard_map/ppermute | solution.py:208
  71.6 1.3 collective-permute-start.2
  72.9 0.0 copy-start.1
  72.9 1.0 copy-done.1
  73.9 0.3 shard_map.47.basis_ref
  74.2 0.5 shard_map.50.given_ref
  74.7 0.0 collective-permute-done.ops_ref
  74.7 2.6 %collective-permute-done.2.high_ref = bf16[512,128]{1,0:T(8,128)(2,1)S(1)} collective-permute-done((bf16[512,128]{1,0:T(8,128)(2,1)S(1)}, bf16[512,128]{1,0:T(8,128)(2,1)S(1)}, u32[]{:S(2)}, u32[]{:S(2)}) %collective-permute-start.2) | collective-permute-done | bytes 131104 | tf_op jit(solution)/shard_map/ppermute | solution.py:209
  77.3 2.1 %shard_map.51 = (bf16[1024,128]{1,0:T(8,128)(2,1)S(1)}, bf16[6,9,13,32,128]{4,3,2,1,0:T(8,128)(2,1)S(1)}) custom-call(s32[8,128]{1,0:T(8,128)S(1)} %get-tuple-element.19.offsets_ref, bf16[16,128,128]{2,1,0:T(8,128)(2,1)S(1)} %collective-permute-done.ops_ref, bf16[768,128]{1,0:T(8,128)(2,1)S(1)} %collective-permute-done.1.low_ref, ...), custom_call_target="tpu_custom_call", output_to_operand_aliasing={{1}: (4, {})} | custom-call | tf_op jit(solution)/shard_map/pallas_call | solution.py:215
  79.4 11.4 %all_to_all.27.parts_ref = bf16[8,128,128]{2,1,0:T(8,128)(2,1)S(1)} all-to-all(bf16[8,128,128]{2,1,0:T(8,128)(2,1)S(1)} %bitcast.22), channel_id=1, replica_groups=mesh['x'=4,'zh'=2,'y'=4,'c'=2,'zl'=8] {'y','c'}, dimensions={0} | all-to-all | bytes 524288 | tf_op jit(solution)/shard_map/all_to_all | solution.py:191
  90.7 0.3 shard_map.52
  91.0 38.3 %all_to_all.28 = bf16[512,2,128]{2,1,0:T(2,128)(2,1)S(1)} all-to-all(bf16[512,2,128]{2,1,0:T(2,128)(2,1)S(1)} %bitcast.20), channel_id=1, replica_groups=mesh['x'=4,'zh'=2,'y'=4,'c'=2,'zl'=8] {'y','c','zh','zl','x'}, dimensions={0} | all-to-all | bytes 524288 | tf_op jit(solution)/shard_map/all_to_all | solution.py:191
  129.4 0.9 shard_map.53
  (6 shorter events, 0.0 us)
Async XLA Ops:
  0.0 1.0 copy-start
  1.0 0.7 copy-start.2
  1.7 0.7 copy-start.3
  43.7 15.0 %all-to-all-start.1 = ((bf16[520,2,128]{2,1,0:T(2,128)(2,1)}), bf16[520,2,128]{2,1,0:T(2,128)(2,1)S(1)}, u32[]{:S(2)}, u32[]{:S(2)}) async-start(bf16[520,2,128]{2,1,0:T(2,128)(2,1)} %bitcast.5), calls=%async_computation.1 | async-start | bytes 532480 | tf_op jit(solution)/shard_map/all_to_all | solution.py:191
  52.1 22.6 %collective-permute-start = (bf16[16,128,128]{2,1,0:T(8,128)(2,1)}, bf16[16,128,128]{2,1,0:T(8,128)(2,1)S(1)}, u32[]{:S(2)}, u32[]{:S(2)}) collective-permute-start(bf16[16,128,128]{2,1,0:T(8,128)(2,1)} %param.6), channel_id=1, source_target_pairs={{0,0},{12,8},{17,16},{95,24},{34,32},{110,40},{51,48},{125,56},{1,... | collective-permute-start | bytes 1572872 | tf_op jit(solution)/shard_map/ppermute | solution.py:205
  68.9 8.4 %collective-permute-start.1 = (bf16[768,128]{1,0:T(8,128)(2,1)S(1)}, bf16[768,128]{1,0:T(8,128)(2,1)S(1)}, u32[]{:S(2)}, u32[]{:S(2)}) collective-permute-start(bf16[768,128]{1,0:T(8,128)(2,1)S(1)} %bitcast.25), channel_id=1, source_target_pairs={{0,128},{128,256},{256,384},{384,1},{1,129},{129,257},{257,385},{3... | collective-permute-start | bytes 589832 | tf_op jit(solution)/shard_map/ppermute | solution.py:208
  71.6 5.7 %collective-permute-start.2 = (bf16[512,128]{1,0:T(8,128)(2,1)S(1)}, bf16[512,128]{1,0:T(8,128)(2,1)S(1)}, u32[]{:S(2)}, u32[]{:S(2)}) collective-permute-start(bf16[512,128]{1,0:T(8,128)(2,1)S(1)} %bitcast.26), channel_id=1, source_target_pairs={{128,0},{256,128},{384,256},{1,384},{129,1},{257,129},{385,257},{2... | collective-permute-start | bytes 393224 | tf_op jit(solution)/shard_map/ppermute | solution.py:209
  72.9 1.0 copy-start.1

commit v12 on v10

--- a/solution.py
+++ b/solution.py
@@ -20,6 +20,7 @@
 SLABS = ("x", "zh", "zl")
 GROUP = ("y", "c")
 VMEM = pl.BlockSpec(memory_space=pltpu.VMEM)
+ANY = pl.BlockSpec(memory_space=pl.ANY)
 SMEM = pl.BlockSpec(memory_space=pltpu.SMEM)
 
 
@@ -35,11 +36,15 @@
     return lax.dot_general(a, b, (dims, ((), ())), precision=precision, preferred_element_type=F32)
 
 
-def pack_kernel(offsets_ref, rows_ref, cells_ref, moments_ref):
-    to, at = iota((64, 128), 0), iota((64, 128), 1)
-    part = mask(at == 2 * to).astype(BF)
-    for z in range(16):
-        moments_ref[z, 0:32] = dot(part, rows_ref[128 * z : 128 * z + 128, :]).astype(BF).reshape(32, 2, 128)
+def pack_kernel(offsets_hbm, rows_hbm, cells_hbm, out_hbm, offsets_ref, rows_ref, cells_ref, moments_ref, sems):
+    halves = [pl.ds(0, 1024), pl.ds(1024, 1024)]
+    copies = [pltpu.make_async_copy(rows_hbm.at[half], rows_ref.at[half], sems.at[i]) for i, half in enumerate(halves)]
+    copies.append(pltpu.make_async_copy(cells_hbm, cells_ref, sems.at[2]))
+    copies.append(pltpu.make_async_copy(offsets_hbm, offsets_ref, sems.at[3]))
+    for copy in copies:
+        copy.start()
+    copies[2].wait()
+    copies[3].wait()
     inside = jnp.bitwise_and(cells_ref[...], RUN - 1).astype(F32)
     lane = iota((1, 128), 1)
     shifts = jnp.zeros((1, 128), F32)
@@ -50,6 +55,17 @@
     for z in range(16):
         rows += [inside[z // 2 : z // 2 + 1], shifts]
     moments_ref[:, 32] = jnp.concatenate(rows, axis=0).astype(BF).reshape(16, 2, 128)
+    to, at = iota((64, 128), 0), iota((64, 128), 1)
+    part = mask(at == 2 * to).astype(BF)
+    outs = [pl.ds(0, 8), pl.ds(8, 8)]
+    outs = [pltpu.make_async_copy(moments_ref.at[half], out_hbm.at[half], sems.at[4 + i]) for i, half in enumerate(outs)]
+    for half in range(2):
+        copies[half].wait()
+        for z in range(8 * half, 8 * half + 8):
+            moments_ref[z, 0:32] = dot(part, rows_ref[128 * z : 128 * z + 128, :]).astype(BF).reshape(32, 2, 128)
+        outs[half].start()
+    for copy in outs:
+        copy.wait()
 
 
 def regroup_kernel(got_ref, out_ref, offsets_ref):
@@ -168,16 +184,16 @@
     return s % 4 * 16 + s // 4
 
 
-def call(kernel, out_shape, in_specs, scratch=(), cost=None, aliases={}):
+def call(kernel, out_shape, in_specs, scratch=(), cost=None, aliases={}, vmem=40, out=VMEM):
     many = isinstance(out_shape, list)
     return pl.pallas_call(
         kernel,
         out_shape=out_shape,
         in_specs=in_specs,
-        out_specs=[VMEM] * len(out_shape) if many else VMEM,
+        out_specs=[VMEM] * len(out_shape) if many else out,
         scratch_shapes=list(scratch),
         input_output_aliases=aliases,
-        compiler_params=pltpu.CompilerParams(vmem_limit_bytes=40 * 1024 * 1024),
+        compiler_params=pltpu.CompilerParams(vmem_limit_bytes=vmem * 1024 * 1024),
         cost_estimate=cost and pl.CostEstimate(flops=cost, bytes_accessed=786432, transcendentals=0),
     )
 
@@ -192,7 +208,9 @@
 
 def body(bead_data, bead_cell, m2l_ops, offsets):
     rows = bead_data.reshape(2048, 128)
-    moments = call(pack_kernel, shape(16, 33, 2, 128), [SMEM, VMEM, VMEM])(
+    scratch = [pltpu.SMEM((3, 16), jnp.int32), pltpu.VMEM((2048, 128), BF), pltpu.VMEM((8, 128), jnp.int32)]
+    scratch += [pltpu.VMEM((16, 33, 2, 128), BF), pltpu.SemaphoreType.DMA((6,))]
+    moments = call(pack_kernel, shape(16, 33, 2, 128), [ANY, ANY, ANY], scratch, vmem=60, out=ANY)(
         offsets.T, rows, bead_cell.reshape(8, 128)
     )
     moments = exchange(moments.reshape(528, 2, 128), COLUMN)

time: 130 us -> 129 us (level)
  local copies, waits for them, and re-layouts: 3.47 us -> 1.06 us
    unnamed x8 -> x2, local copies, waits for them, and re-layouts: 3.45 us -> 1.04 us
where the time goes in v12:
time: 129 us; the launch traced here: 128 us
  blocking collectives  90.9 us (70%)
  starting transfers between devices  22.4 us (17%)
  Pallas kernels  7.42 us (6%)
  waiting for transfers between devices  6.18 us (5%)
    all_to_all x4, blocking collectives, exchange(): return lax.all_to_all(array, axes, split_axis=0, concat_axis=0, tiled=True)  90.9 us
    all_to_all x1, starting transfers between devices, exchange(): return lax.all_to_all(array, axes, split_axis=0, concat_axis=0, tiled=True)  13.3 us
    ppermute x1, starting transfers between devices, body(): ops = lax.ppermute(m2l_ops, ('zh', 'y', 'c', 'zl'), ops_moves())  5.55 us
    all_to_all x1, waiting for transfers between devices, exchange(): return lax.all_to_all(array, axes, split_axis=0, concat_axis=0, tiled=True)  3.59 us
    ppermute x1, waiting for transfers between devices, body(): lax.ppermute(slab[:512], SLABS, [(slab_spot(i + 1), slab_spot(i)) for i i...  2.58 us
  transfers between devices with their start and end apart: 4, of which 2 were waited for; matrix products, arithmetic and copies ran while one was open for 0% of the time, Pallas kernels for 1%

profile of v12, /device:TPU:1, one launch (start us, length us, event | category | flops | bytes accessed | tf_op | source)
XLA Modules:
  0.0 128.1 jit_solution(8760837156693413641)
XLA Ops:
  0.0 2.1 %shard_map.46 = bf16[16,33,2,128]{3,2,1,0:T(2,128)(2,1)} custom-call(s32[3,16]{1,0:T(4,128)} %bitcast.26, bf16[2048,128]{1,0:T(8,128)(2,1)} %bitcast.15, s32[8,128]{1,0:T(8,128)} %bitcast.25), custom_call_target="tpu_custom_call" | custom-call | tf_op jit(solution)/shard_map/pallas_call | solution.py:213
  2.1 29.0 %all_to_all.25 = bf16[528,2,128]{2,1,0:T(2,128)(2,1)S(1)} all-to-all(bf16[528,2,128]{2,1,0:T(2,128)(2,1)} %bitcast.22), channel_id=1, replica_groups=mesh['x'=4,'zh'=2,'y'=4,'c'=2,'zl'=8] {'zh','zl'}, dimensions={0} | all-to-all | bytes 540672 | tf_op jit(solution)/shard_map/all_to_all | solution.py:206
  31.1 1.0 shard_map.48
  32.2 13.3 %all-to-all-start.1 = ((bf16[544,2,128]{2,1,0:T(2,128)(2,1)}), bf16[544,2,128]{2,1,0:T(2,128)(2,1)S(1)}, u32[]{:S(2)}, u32[]{:S(2)}) async-start(bf16[544,2,128]{2,1,0:T(2,128)(2,1)} %bitcast.5), calls=%async_computation.1 | async-start | bytes 557056 | tf_op jit(solution)/shard_map/all_to_all | solution.py:206
  45.5 5.6 %collective-permute-start = (bf16[16,128,128]{2,1,0:T(8,128)(2,1)}, bf16[16,128,128]{2,1,0:T(8,128)(2,1)S(1)}, u32[]{:S(2)}, u32[]{:S(2)}) collective-permute-start(bf16[16,128,128]{2,1,0:T(8,128)(2,1)} %param.6), channel_id=1, source_target_pairs={{0,0},{12,8},{17,16},{95,24},{34,32},{110,40},{51,48},{125,56},{1,... | collective-permute-start | bytes 1572872 | tf_op jit(solution)/shard_map/ppermute | solution.py:222
  51.1 3.6 %all-to-all-done.1 = bf16[544,2,128]{2,1,0:T(2,128)(2,1)S(1)} async-done(((bf16[544,2,128]{2,1,0:T(2,128)(2,1)}), bf16[544,2,128]{2,1,0:T(2,128)(2,1)S(1)}, u32[]{:S(2)}, u32[]{:S(2)}) %all-to-all-start.1) | async-done | bytes 278560 | tf_op jit(solution)/shard_map/all_to_all | solution.py:206
  54.7 0.3 shard_map.49
  55.0 9.1 %all_to_all.26 = bf16[8,128,128]{2,1,0:T(8,128)(2,1)S(1)} all-to-all(bf16[8,128,128]{2,1,0:T(8,128)(2,1)S(1)} %get-tuple-element.21), channel_id=1, replica_groups=mesh['x'=4,'zh'=2,'y'=4,'c'=2,'zl'=8] {'y','c'}, dimensions={0} | all-to-all | bytes 524288 | tf_op jit(solution)/shard_map/all_to_all | solution.py:206
  64.1 2.2 %collective-permute-start.1 = (bf16[768,128]{1,0:T(8,128)(2,1)S(1)}, bf16[768,128]{1,0:T(8,128)(2,1)S(1)}, u32[]{:S(2)}, u32[]{:S(2)}) collective-permute-start(bf16[768,128]{1,0:T(8,128)(2,1)S(1)} %bitcast.23), channel_id=1, source_target_pairs={{0,128},{128,256},{256,384},{384,1},{1,129},{129,257},{257,385},{3... | collective-permute-start | bytes 589832 | tf_op jit(solution)/shard_map/ppermute | solution.py:225
  66.3 1.3 %collective-permute-start.2 = (bf16[512,128]{1,0:T(8,128)(2,1)S(1)}, bf16[512,128]{1,0:T(8,128)(2,1)S(1)}, u32[]{:S(2)}, u32[]{:S(2)}) collective-permute-start(bf16[512,128]{1,0:T(8,128)(2,1)S(1)} %bitcast.24), channel_id=1, source_target_pairs={{128,0},{256,128},{384,256},{1,384},{129,1},{257,129},{385,257},{2... | collective-permute-start | bytes 393224 | tf_op jit(solution)/shard_map/ppermute | solution.py:226
  67.6 0.0 copy-start
  67.6 1.0 copy-done
  68.7 0.3 shard_map.47.basis_ref
  68.9 0.5 shard_map.50.given_ref
  69.4 0.0 collective-permute-done.ops_ref
  69.4 2.6 %collective-permute-done.2.high_ref = bf16[512,128]{1,0:T(8,128)(2,1)S(1)} collective-permute-done((bf16[512,128]{1,0:T(8,128)(2,1)S(1)}, bf16[512,128]{1,0:T(8,128)(2,1)S(1)}, u32[]{:S(2)}, u32[]{:S(2)}) %collective-permute-start.2) | collective-permute-done | bytes 131104 | tf_op jit(solution)/shard_map/ppermute | solution.py:226
  72.0 0.0 collective-permute-done.1.low_ref
  72.0 2.1 %shard_map.51 = (bf16[1024,128]{1,0:T(8,128)(2,1)S(1)}, bf16[6,9,13,32,128]{4,3,2,1,0:T(8,128)(2,1)S(1)}) custom-call(s32[8,128]{1,0:T(8,128)S(1)} %get-tuple-element.19.offsets_ref, bf16[16,128,128]{2,1,0:T(8,128)(2,1)S(1)} %collective-permute-done.ops_ref, bf16[768,128]{1,0:T(8,128)(2,1)S(1)} %collective-permute-done.1.low_ref, ...), custom_call_target="tpu_custom_call", output_to_operand_aliasing={{1}: (4, {})} | custom-call | tf_op jit(solution)/shard_map/pallas_call | solution.py:232
  74.1 11.4 %all_to_all.27.parts_ref = bf16[8,128,128]{2,1,0:T(8,128)(2,1)S(1)} all-to-all(bf16[8,128,128]{2,1,0:T(8,128)(2,1)S(1)} %bitcast.21), channel_id=1, replica_groups=mesh['x'=4,'zh'=2,'y'=4,'c'=2,'zl'=8] {'y','c'}, dimensions={0} | all-to-all | bytes 524288 | tf_op jit(solution)/shard_map/all_to_all | solution.py:206
  85.5 0.3 shard_map.52
  85.8 41.5 %all_to_all.28 = bf16[512,2,128]{2,1,0:T(2,128)(2,1)S(1)} all-to-all(bf16[512,2,128]{2,1,0:T(2,128)(2,1)S(1)} %bitcast.19), channel_id=1, replica_groups=mesh['x'=4,'zh'=2,'y'=4,'c'=2,'zl'=8] {'x','y','c','zh','zl'}, dimensions={0} | all-to-all | bytes 524288 | tf_op jit(solution)/shard_map/all_to_all | solution.py:206
  127.3 0.8 shard_map.53
  (2 shorter events, 0.0 us)
Async XLA Ops:
  32.2 22.5 %all-to-all-start.1 = ((bf16[544,2,128]{2,1,0:T(2,128)(2,1)}), bf16[544,2,128]{2,1,0:T(2,128)(2,1)S(1)}, u32[]{:S(2)}, u32[]{:S(2)}) async-start(bf16[544,2,128]{2,1,0:T(2,128)(2,1)} %bitcast.5), calls=%async_computation.1 | async-start | bytes 557056 | tf_op jit(solution)/shard_map/all_to_all | solution.py:206
  45.5 23.9 %collective-permute-start = (bf16[16,128,128]{2,1,0:T(8,128)(2,1)}, bf16[16,128,128]{2,1,0:T(8,128)(2,1)S(1)}, u32[]{:S(2)}, u32[]{:S(2)}) collective-permute-start(bf16[16,128,128]{2,1,0:T(8,128)(2,1)} %param.6), channel_id=1, source_target_pairs={{0,0},{12,8},{17,16},{95,24},{34,32},{110,40},{51,48},{125,56},{1,... | collective-permute-start | bytes 1572872 | tf_op jit(solution)/shard_map/ppermute | solution.py:222
  64.1 8.0 %collective-permute-start.1 = (bf16[768,128]{1,0:T(8,128)(2,1)S(1)}, bf16[768,128]{1,0:T(8,128)(2,1)S(1)}, u32[]{:S(2)}, u32[]{:S(2)}) collective-permute-start(bf16[768,128]{1,0:T(8,128)(2,1)S(1)} %bitcast.23), channel_id=1, source_target_pairs={{0,128},{128,256},{256,384},{384,1},{1,129},{129,257},{257,385},{3... | collective-permute-start | bytes 589832 | tf_op jit(solution)/shard_map/ppermute | solution.py:225
  66.3 5.7 %collective-permute-start.2 = (bf16[512,128]{1,0:T(8,128)(2,1)S(1)}, bf16[512,128]{1,0:T(8,128)(2,1)S(1)}, u32[]{:S(2)}, u32[]{:S(2)}) collective-permute-start(bf16[512,128]{1,0:T(8,128)(2,1)S(1)} %bitcast.24), channel_id=1, source_target_pairs={{128,0},{256,128},{384,256},{1,384},{129,1},{257,129},{385,257},{2... | collective-permute-start | bytes 393224 | tf_op jit(solution)/shard_map/ppermute | solution.py:226
  67.6 1.0 copy-start

commit v13 on v12

--- a/solution.py
+++ b/solution.py
@@ -68,7 +68,7 @@
         copy.wait()
 
 
-def regroup_kernel(got_ref, out_ref, offsets_ref):
+def regroup_kernel(got_ref, out_hbm, offsets_ref, out_ref, sems):
     peer, layer = lax.axis_index("y") * 2 + lax.axis_index("c"), lax.axis_index("zl")
     quarter, half = lax.rem(peer, 4), lax.rem(layer, 2)
     reach = jnp.int32(0)
@@ -77,6 +77,9 @@
     shard = lax.rem(layer + reach, 8)
     for z in range(16):
         out_ref[:, z] = got_ref[z, 0:32]
+    parts = [pl.ds(0, 16), pl.ds(16, 1)]
+    copies = [pltpu.make_async_copy(out_ref.at[:, part], out_hbm.at[:, part], sems.at[i]) for i, part in enumerate(parts)]
+    copies[0].start()
     extra = got_ref[:, 32].reshape(32, 128)
     row, lane = iota((32, 128), 0), iota((32, 128), 1)
     take_row, take_lane = iota((64, 128), 0), iota((64, 128), 1)
@@ -87,8 +90,11 @@
         taken = dot(take.astype(BF), extra, ((1,), (1,)))
         ids = ids + dot(taken.astype(BF), put.astype(BF))
     out_ref[:, 16] = ids.astype(BF).reshape(32, 2, 128)
+    copies[1].start()
     own = jnp.sum(mask(row == 2 * shard + 1) * extra.astype(F32), axis=0, keepdims=True)
     offsets_ref[...] = jnp.broadcast_to(own, (8, 128)).astype(jnp.int32)
+    for copy in copies:
+        copy.wait()
 
 
 def sum_kernel(got_ref, cells_ref, ids_ref):
@@ -190,7 +196,7 @@
         kernel,
         out_shape=out_shape,
         in_specs=in_specs,
-        out_specs=[VMEM] * len(out_shape) if many else out,
+        out_specs=[VMEM] * len(out_shape) if many and out is VMEM else out,
         scratch_shapes=list(scratch),
         input_output_aliases=aliases,
         compiler_params=pltpu.CompilerParams(vmem_limit_bytes=vmem * 1024 * 1024),
@@ -216,7 +222,11 @@
     moments = exchange(moments.reshape(528, 2, 128), COLUMN)
     m2l_ops, moments = lax.optimization_barrier((m2l_ops, moments))
     moments, shifts = call(
-        regroup_kernel, [shape(32, 17, 2, 128), shape(8, 128, kind=jnp.int32)], [VMEM]
+        regroup_kernel,
+        [shape(32, 17, 2, 128), shape(8, 128, kind=jnp.int32)],
+        [VMEM],
+        [pltpu.VMEM((32, 17, 2, 128), BF), pltpu.SemaphoreType.DMA((2,))],
+        out=[ANY, VMEM],
     )(moments.reshape(16, 33, 2, 128))
     moments = exchange(moments.reshape(544, 2, 128), LAYER).reshape(32, 17, 2, 128)
     ops = lax.ppermute(m2l_ops, ("zh", "y", "c", "zl"), ops_moves())

time: 129 us -> 129 us (level)
  no operation moved by 1% of the time
where the time goes in v13:
time: 129 us; the launch traced here: 128 us
  blocking collectives  90.9 us (70%)
  starting transfers between devices  22.4 us (17%)
  Pallas kernels  7.39 us (6%)
  waiting for transfers between devices  6.18 us (5%)
    all_to_all x4, blocking collectives, exchange(): return lax.all_to_all(array, axes, split_axis=0, concat_axis=0, tiled=True)  90.9 us
    all_to_all x1, starting transfers between devices, exchange(): return lax.all_to_all(array, axes, split_axis=0, concat_axis=0, tiled=True)  13.4 us
    ppermute x1, starting transfers between devices, body(): ops = lax.ppermute(m2l_ops, ('zh', 'y', 'c', 'zl'), ops_moves())  5.55 us
    all_to_all x1, waiting for transfers between devices, exchange(): return lax.all_to_all(array, axes, split_axis=0, concat_axis=0, tiled=True)  3.59 us
    ppermute x1, waiting for transfers between devices, body(): lax.ppermute(slab[:512], SLABS, [(slab_spot(i + 1), slab_spot(i)) for i i...  2.58 us
  transfers between devices with their start and end apart: 4, of which 2 were waited for; matrix products, arithmetic and copies ran while one was open for 0% of the time, Pallas kernels for 1%

profile of v13, /device:TPU:1, one launch (start us, length us, event | category | flops | bytes accessed | tf_op | source)
XLA Modules:
  0.0 128.1 jit_solution(5491596393181940682)
XLA Ops:
  0.0 2.1 %shard_map.46 = bf16[16,33,2,128]{3,2,1,0:T(2,128)(2,1)} custom-call(s32[3,16]{1,0:T(4,128)} %bitcast.26, bf16[2048,128]{1,0:T(8,128)(2,1)} %bitcast.15, s32[8,128]{1,0:T(8,128)} %bitcast.25), custom_call_target="tpu_custom_call" | custom-call | tf_op jit(solution)/shard_map/pallas_call | solution.py:219
  2.1 29.0 %all_to_all.25 = bf16[528,2,128]{2,1,0:T(2,128)(2,1)S(1)} all-to-all(bf16[528,2,128]{2,1,0:T(2,128)(2,1)} %bitcast.22), channel_id=1, replica_groups=mesh['x'=4,'zh'=2,'y'=4,'c'=2,'zl'=8] {'zh','zl'}, dimensions={0} | all-to-all | bytes 540672 | tf_op jit(solution)/shard_map/all_to_all | solution.py:212
  31.1 1.0 shard_map.48
  32.1 13.4 %all-to-all-start.1 = ((bf16[544,2,128]{2,1,0:T(2,128)(2,1)}), bf16[544,2,128]{2,1,0:T(2,128)(2,1)S(1)}, u32[]{:S(2)}, u32[]{:S(2)}) async-start(bf16[544,2,128]{2,1,0:T(2,128)(2,1)} %bitcast.5), calls=%async_computation.1 | async-start | bytes 557056 | tf_op jit(solution)/shard_map/all_to_all | solution.py:212
  45.5 5.6 %collective-permute-start = (bf16[16,128,128]{2,1,0:T(8,128)(2,1)}, bf16[16,128,128]{2,1,0:T(8,128)(2,1)S(1)}, u32[]{:S(2)}, u32[]{:S(2)}) collective-permute-start(bf16[16,128,128]{2,1,0:T(8,128)(2,1)} %param.6), channel_id=1, source_target_pairs={{0,0},{12,8},{17,16},{95,24},{34,32},{110,40},{51,48},{125,56},{1,... | collective-permute-start | bytes 1572872 | tf_op jit(solution)/shard_map/ppermute | solution.py:232
  51.1 3.6 %all-to-all-done.1 = bf16[544,2,128]{2,1,0:T(2,128)(2,1)S(1)} async-done(((bf16[544,2,128]{2,1,0:T(2,128)(2,1)}), bf16[544,2,128]{2,1,0:T(2,128)(2,1)S(1)}, u32[]{:S(2)}, u32[]{:S(2)}) %all-to-all-start.1) | async-done | bytes 278560 | tf_op jit(solution)/shard_map/all_to_all | solution.py:212
  54.6 0.3 shard_map.49
  55.0 9.1 %all_to_all.26 = bf16[8,128,128]{2,1,0:T(8,128)(2,1)S(1)} all-to-all(bf16[8,128,128]{2,1,0:T(8,128)(2,1)S(1)} %get-tuple-element.21), channel_id=1, replica_groups=mesh['x'=4,'zh'=2,'y'=4,'c'=2,'zl'=8] {'y','c'}, dimensions={0} | all-to-all | bytes 524288 | tf_op jit(solution)/shard_map/all_to_all | solution.py:212
  64.0 2.2 %collective-permute-start.1 = (bf16[768,128]{1,0:T(8,128)(2,1)S(1)}, bf16[768,128]{1,0:T(8,128)(2,1)S(1)}, u32[]{:S(2)}, u32[]{:S(2)}) collective-permute-start(bf16[768,128]{1,0:T(8,128)(2,1)S(1)} %bitcast.23), channel_id=1, source_target_pairs={{0,128},{128,256},{256,384},{384,1},{1,129},{129,257},{257,385},{3... | collective-permute-start | bytes 589832 | tf_op jit(solution)/shard_map/ppermute | solution.py:235
  66.3 1.3 %collective-permute-start.2 = (bf16[512,128]{1,0:T(8,128)(2,1)S(1)}, bf16[512,128]{1,0:T(8,128)(2,1)S(1)}, u32[]{:S(2)}, u32[]{:S(2)}) collective-permute-start(bf16[512,128]{1,0:T(8,128)(2,1)S(1)} %bitcast.24), channel_id=1, source_target_pairs={{128,0},{256,128},{384,256},{1,384},{129,1},{257,129},{385,257},{2... | collective-permute-start | bytes 393224 | tf_op jit(solution)/shard_map/ppermute | solution.py:236
  67.6 0.0 copy-start
  67.6 1.0 copy-done
  68.6 0.3 shard_map.47.basis_ref
  68.9 0.5 shard_map.50.given_ref
  69.4 0.0 collective-permute-done.ops_ref
  69.4 2.6 %collective-permute-done.2.high_ref = bf16[512,128]{1,0:T(8,128)(2,1)S(1)} collective-permute-done((bf16[512,128]{1,0:T(8,128)(2,1)S(1)}, bf16[512,128]{1,0:T(8,128)(2,1)S(1)}, u32[]{:S(2)}, u32[]{:S(2)}) %collective-permute-start.2) | collective-permute-done | bytes 131104 | tf_op jit(solution)/shard_map/ppermute | solution.py:236
  72.0 0.0 collective-permute-done.1.low_ref
  72.0 2.1 %shard_map.51 = (bf16[1024,128]{1,0:T(8,128)(2,1)S(1)}, bf16[6,9,13,32,128]{4,3,2,1,0:T(8,128)(2,1)S(1)}) custom-call(s32[8,128]{1,0:T(8,128)S(1)} %get-tuple-element.19.offsets_ref, bf16[16,128,128]{2,1,0:T(8,128)(2,1)S(1)} %collective-permute-done.ops_ref, bf16[768,128]{1,0:T(8,128)(2,1)S(1)} %collective-permute-done.1.low_ref, ...), custom_call_target="tpu_custom_call", output_to_operand_aliasing={{1}: (4, {})} | custom-call | tf_op jit(solution)/shard_map/pallas_call | solution.py:242
  74.1 11.4 %all_to_all.27.parts_ref = bf16[8,128,128]{2,1,0:T(8,128)(2,1)S(1)} all-to-all(bf16[8,128,128]{2,1,0:T(8,128)(2,1)S(1)} %bitcast.21), channel_id=1, replica_groups=mesh['x'=4,'zh'=2,'y'=4,'c'=2,'zl'=8] {'y','c'}, dimensions={0} | all-to-all | bytes 524288 | tf_op jit(solution)/shard_map/all_to_all | solution.py:212
  85.5 0.3 shard_map.52
  85.8 41.5 %all_to_all.28 = bf16[512,2,128]{2,1,0:T(2,128)(2,1)S(1)} all-to-all(bf16[512,2,128]{2,1,0:T(2,128)(2,1)S(1)} %bitcast.19), channel_id=1, replica_groups=mesh['x'=4,'zh'=2,'y'=4,'c'=2,'zl'=8] {'x','y','c','zh','zl'}, dimensions={0} | all-to-all | bytes 524288 | tf_op jit(solution)/shard_map/all_to_all | solution.py:212
  127.3 0.8 shard_map.53
  (2 shorter events, 0.0 us)
Async XLA Ops:
  32.1 22.5 %all-to-all-start.1 = ((bf16[544,2,128]{2,1,0:T(2,128)(2,1)}), bf16[544,2,128]{2,1,0:T(2,128)(2,1)S(1)}, u32[]{:S(2)}, u32[]{:S(2)}) async-start(bf16[544,2,128]{2,1,0:T(2,128)(2,1)} %bitcast.5), calls=%async_computation.1 | async-start | bytes 557056 | tf_op jit(solution)/shard_map/all_to_all | solution.py:212
  45.5 23.9 %collective-permute-start = (bf16[16,128,128]{2,1,0:T(8,128)(2,1)}, bf16[16,128,128]{2,1,0:T(8,128)(2,1)S(1)}, u32[]{:S(2)}, u32[]{:S(2)}) collective-permute-start(bf16[16,128,128]{2,1,0:T(8,128)(2,1)} %param.6), channel_id=1, source_target_pairs={{0,0},{12,8},{17,16},{95,24},{34,32},{110,40},{51,48},{125,56},{1,... | collective-permute-start | bytes 1572872 | tf_op jit(solution)/shard_map/ppermute | solution.py:232
  64.0 8.0 %collective-permute-start.1 = (bf16[768,128]{1,0:T(8,128)(2,1)S(1)}, bf16[768,128]{1,0:T(8,128)(2,1)S(1)}, u32[]{:S(2)}, u32[]{:S(2)}) collective-permute-start(bf16[768,128]{1,0:T(8,128)(2,1)S(1)} %bitcast.23), channel_id=1, source_target_pairs={{0,128},{128,256},{256,384},{384,1},{1,129},{129,257},{257,385},{3... | collective-permute-start | bytes 589832 | tf_op jit(solution)/shard_map/ppermute | solution.py:235
  66.3 5.7 %collective-permute-start.2 = (bf16[512,128]{1,0:T(8,128)(2,1)S(1)}, bf16[512,128]{1,0:T(8,128)(2,1)S(1)}, u32[]{:S(2)}, u32[]{:S(2)}) collective-permute-start(bf16[512,128]{1,0:T(8,128)(2,1)S(1)} %bitcast.24), channel_id=1, source_target_pairs={{128,0},{256,128},{384,256},{1,384},{129,1},{257,129},{385,257},{2... | collective-permute-start | bytes 393224 | tf_op jit(solution)/shard_map/ppermute | solution.py:236
  67.6 1.0 copy-start

commit v14 on v12

--- a/solution.py
+++ b/solution.py
@@ -120,13 +120,16 @@
         fill(rows, shifted, plane + 3, own_ref[plane * 256 : (plane + 1) * 256, :])
 
 
-def m2l_kernel(offsets_ref, ops_ref, low_ref, high_ref, given_ref, out_ref, shifted, rows):
+def m2l_kernel(shifts_ref, ops_ref, low_ref, high_ref, given_ref, out_ref, shifted, rows, offsets_ref, sem):
+    copy = pltpu.make_async_copy(shifts_ref, offsets_ref, sem)
+    copy.start()
     rows[:, 0:8, :] = jnp.zeros((GX, 8, 128), F32)
     rows[:, 40:48, :] = jnp.zeros((GX, 8, 128), F32)
     for plane in range(3):
         fill(rows, shifted, plane, low_ref[plane * 256 : (plane + 1) * 256, :])
     for plane in range(2):
         fill(rows, shifted, plane + 7, high_ref[plane * 256 : (plane + 1) * 256, :])
+    copy.wait()
     ops = ops_ref[...].reshape(16 * 128, 128)
     for z in range(CZS):
         windows = []
@@ -230,7 +233,11 @@
     rows = [pltpu.VMEM((GX, 48, 128), F32)]
     shifted = call(shift_kernel, buffer, [VMEM], rows, cost=100_000_000)(slab)
     parts, _ = call(
-        m2l_kernel, [shape(1024, 128), buffer], [SMEM, VMEM, VMEM, VMEM, VMEM], rows, aliases={4: 1}
+        m2l_kernel,
+        [shape(1024, 128), buffer],
+        [VMEM] * 5,
+        rows + [pltpu.SMEM((8, 128), jnp.int32), pltpu.SemaphoreType.DMA],
+        aliases={4: 1},
     )(shifts, ops, low, high, shifted)
     parts = exchange(parts.reshape(8, 128, 128), GROUP)
     picked = call(pick_kernel, shape(1024, 128), [VMEM, VMEM])(ids, parts)

time: 129 us -> 128 us (level)
  no operation moved by 1% of the time
where the time goes in v14:
time: 128 us
  blocking collectives  90.9 us (71%)
  starting transfers between devices  22.4 us (18%)
  Pallas kernels  7.22 us (6%)
  waiting for transfers between devices  6.18 us (5%)
    all_to_all x4, blocking collectives, exchange(): return lax.all_to_all(array, axes, split_axis=0, concat_axis=0, tiled=True)  90.9 us
    all_to_all x1, starting transfers between devices, exchange(): return lax.all_to_all(array, axes, split_axis=0, concat_axis=0, tiled=True)  13.3 us
    ppermute x1, starting transfers between devices, body(): ops = lax.ppermute(m2l_ops, ('zh', 'y', 'c', 'zl'), ops_moves())  5.55 us
    all_to_all x1, waiting for transfers between devices, exchange(): return lax.all_to_all(array, axes, split_axis=0, concat_axis=0, tiled=True)  3.59 us
    ppermute x1, waiting for transfers between devices, body(): lax.ppermute(slab[:512], SLABS, [(slab_spot(i + 1), slab_spot(i)) for i i...  2.58 us
  transfers between devices with their start and end apart: 4, of which 2 were waited for; matrix products, arithmetic and copies ran while one was open for 0% of the time, Pallas kernels for 1%

profile of v14, /device:TPU:1, one launch (start us, length us, event | category | flops | bytes accessed | tf_op | source)
XLA Modules:
  0.0 127.9 jit_solution(13509186235065173924)
XLA Ops:
  0.0 2.1 %shard_map.46 = bf16[16,33,2,128]{3,2,1,0:T(2,128)(2,1)} custom-call(s32[3,16]{1,0:T(4,128)} %bitcast.26, bf16[2048,128]{1,0:T(8,128)(2,1)} %bitcast.15, s32[8,128]{1,0:T(8,128)} %bitcast.25), custom_call_target="tpu_custom_call" | custom-call | tf_op jit(solution)/shard_map/pallas_call | solution.py:216
  2.1 29.0 %all_to_all.25 = bf16[528,2,128]{2,1,0:T(2,128)(2,1)S(1)} all-to-all(bf16[528,2,128]{2,1,0:T(2,128)(2,1)} %bitcast.22), channel_id=1, replica_groups=mesh['x'=4,'zh'=2,'y'=4,'c'=2,'zl'=8] {'zh','zl'}, dimensions={0} | all-to-all | bytes 540672 | tf_op jit(solution)/shard_map/all_to_all | solution.py:209
  31.1 1.0 shard_map.48
  32.2 13.3 %all-to-all-start.1 = ((bf16[544,2,128]{2,1,0:T(2,128)(2,1)}), bf16[544,2,128]{2,1,0:T(2,128)(2,1)S(1)}, u32[]{:S(2)}, u32[]{:S(2)}) async-start(bf16[544,2,128]{2,1,0:T(2,128)(2,1)} %bitcast.5), calls=%async_computation.1 | async-start | bytes 557056 | tf_op jit(solution)/shard_map/all_to_all | solution.py:209
  45.5 5.6 %collective-permute-start = (bf16[16,128,128]{2,1,0:T(8,128)(2,1)}, bf16[16,128,128]{2,1,0:T(8,128)(2,1)S(1)}, u32[]{:S(2)}, u32[]{:S(2)}) collective-permute-start(bf16[16,128,128]{2,1,0:T(8,128)(2,1)} %param.6), channel_id=1, source_target_pairs={{0,0},{12,8},{17,16},{95,24},{34,32},{110,40},{51,48},{125,56},{1,... | collective-permute-start | bytes 1572872 | tf_op jit(solution)/shard_map/ppermute | solution.py:225
  51.1 3.6 %all-to-all-done.1 = bf16[544,2,128]{2,1,0:T(2,128)(2,1)S(1)} async-done(((bf16[544,2,128]{2,1,0:T(2,128)(2,1)}), bf16[544,2,128]{2,1,0:T(2,128)(2,1)S(1)}, u32[]{:S(2)}, u32[]{:S(2)}) %all-to-all-start.1) | async-done | bytes 278560 | tf_op jit(solution)/shard_map/all_to_all | solution.py:209
  54.7 0.3 shard_map.49
  55.0 9.1 %all_to_all.26 = bf16[8,128,128]{2,1,0:T(8,128)(2,1)S(1)} all-to-all(bf16[8,128,128]{2,1,0:T(8,128)(2,1)S(1)} %get-tuple-element.21), channel_id=1, replica_groups=mesh['x'=4,'zh'=2,'y'=4,'c'=2,'zl'=8] {'y','c'}, dimensions={0} | all-to-all | bytes 524288 | tf_op jit(solution)/shard_map/all_to_all | solution.py:209
  64.1 2.2 %collective-permute-start.1 = (bf16[768,128]{1,0:T(8,128)(2,1)S(1)}, bf16[768,128]{1,0:T(8,128)(2,1)S(1)}, u32[]{:S(2)}, u32[]{:S(2)}) collective-permute-start(bf16[768,128]{1,0:T(8,128)(2,1)S(1)} %bitcast.23), channel_id=1, source_target_pairs={{0,128},{128,256},{256,384},{384,1},{1,129},{129,257},{257,385},{3... | collective-permute-start | bytes 589832 | tf_op jit(solution)/shard_map/ppermute | solution.py:228
  66.3 1.3 %collective-permute-start.2 = (bf16[512,128]{1,0:T(8,128)(2,1)S(1)}, bf16[512,128]{1,0:T(8,128)(2,1)S(1)}, u32[]{:S(2)}, u32[]{:S(2)}) collective-permute-start(bf16[512,128]{1,0:T(8,128)(2,1)S(1)} %bitcast.24), channel_id=1, source_target_pairs={{128,0},{256,128},{384,256},{1,384},{129,1},{257,129},{385,257},{2... | collective-permute-start | bytes 393224 | tf_op jit(solution)/shard_map/ppermute | solution.py:229
  67.6 0.0 copy-start
  67.6 1.0 copy-done
  68.7 0.3 shard_map.47.basis_ref
  68.9 0.5 shard_map.50.given_ref
  69.4 0.0 collective-permute-done.ops_ref
  69.4 2.6 %collective-permute-done.2.high_ref = bf16[512,128]{1,0:T(8,128)(2,1)S(1)} collective-permute-done((bf16[512,128]{1,0:T(8,128)(2,1)S(1)}, bf16[512,128]{1,0:T(8,128)(2,1)S(1)}, u32[]{:S(2)}, u32[]{:S(2)}) %collective-permute-start.2) | collective-permute-done | bytes 131104 | tf_op jit(solution)/shard_map/ppermute | solution.py:229
  72.0 0.0 collective-permute-done.1.low_ref
  72.0 1.9 %shard_map.51 = (bf16[1024,128]{1,0:T(8,128)(2,1)S(1)}, bf16[6,9,13,32,128]{4,3,2,1,0:T(8,128)(2,1)S(1)}) custom-call(s32[8,128]{1,0:T(8,128)S(1)} %get-tuple-element.19.shifts_ref, bf16[16,128,128]{2,1,0:T(8,128)(2,1)S(1)} %collective-permute-done.ops_ref, bf16[768,128]{1,0:T(8,128)(2,1)S(1)} %collective-permute-done.1.low_ref, ...), custom_call_target="tpu_custom_call", output_to_operand_aliasing={{1}: (4, {})} | custom-call | tf_op jit(solution)/shard_map/pallas_call | solution.py:235
  73.9 11.4 %all_to_all.27.parts_ref = bf16[8,128,128]{2,1,0:T(8,128)(2,1)S(1)} all-to-all(bf16[8,128,128]{2,1,0:T(8,128)(2,1)S(1)} %bitcast.21), channel_id=1, replica_groups=mesh['x'=4,'zh'=2,'y'=4,'c'=2,'zl'=8] {'y','c'}, dimensions={0} | all-to-all | bytes 524288 | tf_op jit(solution)/shard_map/all_to_all | solution.py:209
  85.3 0.3 shard_map.52
  85.6 41.5 %all_to_all.28 = bf16[512,2,128]{2,1,0:T(2,128)(2,1)S(1)} all-to-all(bf16[512,2,128]{2,1,0:T(2,128)(2,1)S(1)} %bitcast.19), channel_id=1, replica_groups=mesh['x'=4,'zh'=2,'y'=4,'c'=2,'zl'=8] {'x','y','c','zh','zl'}, dimensions={0} | all-to-all | bytes 524288 | tf_op jit(solution)/shard_map/all_to_all | solution.py:209
  127.1 0.8 shard_map.53
  (2 shorter events, 0.0 us)
Async XLA Ops:
  32.2 22.5 %all-to-all-start.1 = ((bf16[544,2,128]{2,1,0:T(2,128)(2,1)}), bf16[544,2,128]{2,1,0:T(2,128)(2,1)S(1)}, u32[]{:S(2)}, u32[]{:S(2)}) async-start(bf16[544,2,128]{2,1,0:T(2,128)(2,1)} %bitcast.5), calls=%async_computation.1 | async-start | bytes 557056 | tf_op jit(solution)/shard_map/all_to_all | solution.py:209
  45.5 23.9 %collective-permute-start = (bf16[16,128,128]{2,1,0:T(8,128)(2,1)}, bf16[16,128,128]{2,1,0:T(8,128)(2,1)S(1)}, u32[]{:S(2)}, u32[]{:S(2)}) collective-permute-start(bf16[16,128,128]{2,1,0:T(8,128)(2,1)} %param.6), channel_id=1, source_target_pairs={{0,0},{12,8},{17,16},{95,24},{34,32},{110,40},{51,48},{125,56},{1,... | collective-permute-start | bytes 1572872 | tf_op jit(solution)/shard_map/ppermute | solution.py:225
  64.1 8.0 %collective-permute-start.1 = (bf16[768,128]{1,0:T(8,128)(2,1)S(1)}, bf16[768,128]{1,0:T(8,128)(2,1)S(1)}, u32[]{:S(2)}, u32[]{:S(2)}) collective-permute-start(bf16[768,128]{1,0:T(8,128)(2,1)S(1)} %bitcast.23), channel_id=1, source_target_pairs={{0,128},{128,256},{256,384},{384,1},{1,129},{129,257},{257,385},{3... | collective-permute-start | bytes 589832 | tf_op jit(solution)/shard_map/ppermute | solution.py:228
  66.3 5.7 %collective-permute-start.2 = (bf16[512,128]{1,0:T(8,128)(2,1)S(1)}, bf16[512,128]{1,0:T(8,128)(2,1)S(1)}, u32[]{:S(2)}, u32[]{:S(2)}) collective-permute-start(bf16[512,128]{1,0:T(8,128)(2,1)S(1)} %bitcast.24), channel_id=1, source_target_pairs={{128,0},{256,128},{384,256},{1,384},{129,1},{257,129},{385,257},{2... | collective-permute-start | bytes 393224 | tf_op jit(solution)/shard_map/ppermute | solution.py:229
  67.6 1.0 copy-start

commit v15 on v14

--- a/solution.py
+++ b/solution.py
@@ -37,14 +37,13 @@
 
 
 def pack_kernel(offsets_hbm, rows_hbm, cells_hbm, out_hbm, offsets_ref, rows_ref, cells_ref, moments_ref, sems):
-    halves = [pl.ds(0, 1024), pl.ds(1024, 1024)]
-    copies = [pltpu.make_async_copy(rows_hbm.at[half], rows_ref.at[half], sems.at[i]) for i, half in enumerate(halves)]
-    copies.append(pltpu.make_async_copy(cells_hbm, cells_ref, sems.at[2]))
-    copies.append(pltpu.make_async_copy(offsets_hbm, offsets_ref, sems.at[3]))
+    copies = [pltpu.make_async_copy(rows_hbm, rows_ref, sems.at[0])]
+    copies.append(pltpu.make_async_copy(cells_hbm, cells_ref, sems.at[1]))
+    copies.append(pltpu.make_async_copy(offsets_hbm, offsets_ref, sems.at[2]))
     for copy in copies:
         copy.start()
+    copies[1].wait()
     copies[2].wait()
-    copies[3].wait()
     inside = jnp.bitwise_and(cells_ref[...], RUN - 1).astype(F32)
     lane = iota((1, 128), 1)
     shifts = jnp.zeros((1, 128), F32)
@@ -58,9 +57,9 @@
     to, at = iota((64, 128), 0), iota((64, 128), 1)
     part = mask(at == 2 * to).astype(BF)
     outs = [pl.ds(0, 8), pl.ds(8, 8)]
-    outs = [pltpu.make_async_copy(moments_ref.at[half], out_hbm.at[half], sems.at[4 + i]) for i, half in enumerate(outs)]
+    outs = [pltpu.make_async_copy(moments_ref.at[half], out_hbm.at[half], sems.at[3 + i]) for i, half in enumerate(outs)]
+    copies[0].wait()
     for half in range(2):
-        copies[half].wait()
         for z in range(8 * half, 8 * half + 8):
             moments_ref[z, 0:32] = dot(part, rows_ref[128 * z : 128 * z + 128, :]).astype(BF).reshape(32, 2, 128)
         outs[half].start()
@@ -212,7 +211,7 @@
 def body(bead_data, bead_cell, m2l_ops, offsets):
     rows = bead_data.reshape(2048, 128)
     scratch = [pltpu.SMEM((3, 16), jnp.int32), pltpu.VMEM((2048, 128), BF), pltpu.VMEM((8, 128), jnp.int32)]
-    scratch += [pltpu.VMEM((16, 33, 2, 128), BF), pltpu.SemaphoreType.DMA((6,))]
+    scratch += [pltpu.VMEM((16, 33, 2, 128), BF), pltpu.SemaphoreType.DMA((5,))]
     moments = call(pack_kernel, shape(16, 33, 2, 128), [ANY, ANY, ANY], scratch, vmem=60, out=ANY)(
         offsets.T, rows, bead_cell.reshape(8, 128)
     )

time: 128 us -> 128 us (level)
  no operation moved by 1% of the time
where the time goes in v15:
time: 128 us
  blocking collectives  90.9 us (71%)
  starting transfers between devices  22.4 us (18%)
  Pallas kernels  7.15 us (6%)
  waiting for transfers between devices  6.18 us (5%)
    all_to_all x4, blocking collectives, exchange(): return lax.all_to_all(array, axes, split_axis=0, concat_axis=0, tiled=True)  90.9 us
    all_to_all x1, starting transfers between devices, exchange(): return lax.all_to_all(array, axes, split_axis=0, concat_axis=0, tiled=True)  13.3 us
    ppermute x1, starting transfers between devices, body(): ops = lax.ppermute(m2l_ops, ('zh', 'y', 'c', 'zl'), ops_moves())  5.55 us
    all_to_all x1, waiting for transfers between devices, exchange(): return lax.all_to_all(array, axes, split_axis=0, concat_axis=0, tiled=True)  3.59 us
    ppermute x1, waiting for transfers between devices, body(): lax.ppermute(slab[:512], SLABS, [(slab_spot(i + 1), slab_spot(i)) for i i...  2.58 us
  transfers between devices with their start and end apart: 4, of which 2 were waited for; matrix products, arithmetic and copies ran while one was open for 0% of the time, Pallas kernels for 1%

profile of v15, /device:TPU:1, one launch (start us, length us, event | category | flops | bytes accessed | tf_op | source)
XLA Modules:
  0.0 127.9 jit_solution(6376369372241781960)
XLA Ops:
  0.0 2.0 %shard_map.46 = bf16[16,33,2,128]{3,2,1,0:T(2,128)(2,1)} custom-call(s32[3,16]{1,0:T(4,128)} %bitcast.26, bf16[2048,128]{1,0:T(8,128)(2,1)} %bitcast.15, s32[8,128]{1,0:T(8,128)} %bitcast.25), custom_call_target="tpu_custom_call" | custom-call | tf_op jit(solution)/shard_map/pallas_call | solution.py:215
  2.1 29.0 %all_to_all.25 = bf16[528,2,128]{2,1,0:T(2,128)(2,1)S(1)} all-to-all(bf16[528,2,128]{2,1,0:T(2,128)(2,1)} %bitcast.22), channel_id=1, replica_groups=mesh['x'=4,'zh'=2,'y'=4,'c'=2,'zl'=8] {'zh','zl'}, dimensions={0} | all-to-all | bytes 540672 | tf_op jit(solution)/shard_map/all_to_all | solution.py:208
  31.1 1.0 shard_map.48
  32.1 13.3 %all-to-all-start.1 = ((bf16[544,2,128]{2,1,0:T(2,128)(2,1)}), bf16[544,2,128]{2,1,0:T(2,128)(2,1)S(1)}, u32[]{:S(2)}, u32[]{:S(2)}) async-start(bf16[544,2,128]{2,1,0:T(2,128)(2,1)} %bitcast.5), calls=%async_computation.1 | async-start | bytes 557056 | tf_op jit(solution)/shard_map/all_to_all | solution.py:208
  45.4 5.6 %collective-permute-start = (bf16[16,128,128]{2,1,0:T(8,128)(2,1)}, bf16[16,128,128]{2,1,0:T(8,128)(2,1)S(1)}, u32[]{:S(2)}, u32[]{:S(2)}) collective-permute-start(bf16[16,128,128]{2,1,0:T(8,128)(2,1)} %param.6), channel_id=1, source_target_pairs={{0,0},{12,8},{17,16},{95,24},{34,32},{110,40},{51,48},{125,56},{1,... | collective-permute-start | bytes 1572872 | tf_op jit(solution)/shard_map/ppermute | solution.py:224
  51.0 3.6 %all-to-all-done.1 = bf16[544,2,128]{2,1,0:T(2,128)(2,1)S(1)} async-done(((bf16[544,2,128]{2,1,0:T(2,128)(2,1)}), bf16[544,2,128]{2,1,0:T(2,128)(2,1)S(1)}, u32[]{:S(2)}, u32[]{:S(2)}) %all-to-all-start.1) | async-done | bytes 278560 | tf_op jit(solution)/shard_map/all_to_all | solution.py:208
  54.6 0.3 shard_map.49
  54.9 9.1 %all_to_all.26 = bf16[8,128,128]{2,1,0:T(8,128)(2,1)S(1)} all-to-all(bf16[8,128,128]{2,1,0:T(8,128)(2,1)S(1)} %get-tuple-element.21), channel_id=1, replica_groups=mesh['x'=4,'zh'=2,'y'=4,'c'=2,'zl'=8] {'y','c'}, dimensions={0} | all-to-all | bytes 524288 | tf_op jit(solution)/shard_map/all_to_all | solution.py:208
  64.0 2.2 %collective-permute-start.1 = (bf16[768,128]{1,0:T(8,128)(2,1)S(1)}, bf16[768,128]{1,0:T(8,128)(2,1)S(1)}, u32[]{:S(2)}, u32[]{:S(2)}) collective-permute-start(bf16[768,128]{1,0:T(8,128)(2,1)S(1)} %bitcast.23), channel_id=1, source_target_pairs={{0,128},{128,256},{256,384},{384,1},{1,129},{129,257},{257,385},{3... | collective-permute-start | bytes 589832 | tf_op jit(solution)/shard_map/ppermute | solution.py:227
  66.2 1.3 %collective-permute-start.2 = (bf16[512,128]{1,0:T(8,128)(2,1)S(1)}, bf16[512,128]{1,0:T(8,128)(2,1)S(1)}, u32[]{:S(2)}, u32[]{:S(2)}) collective-permute-start(bf16[512,128]{1,0:T(8,128)(2,1)S(1)} %bitcast.24), channel_id=1, source_target_pairs={{128,0},{256,128},{384,256},{1,384},{129,1},{257,129},{385,257},{2... | collective-permute-start | bytes 393224 | tf_op jit(solution)/shard_map/ppermute | solution.py:228
  67.5 0.0 copy-start
  67.6 1.0 copy-done
  68.6 0.3 shard_map.47.basis_ref
  68.9 0.5 shard_map.50.given_ref
  69.4 0.0 collective-permute-done.ops_ref
  69.4 2.6 %collective-permute-done.2.high_ref = bf16[512,128]{1,0:T(8,128)(2,1)S(1)} collective-permute-done((bf16[512,128]{1,0:T(8,128)(2,1)S(1)}, bf16[512,128]{1,0:T(8,128)(2,1)S(1)}, u32[]{:S(2)}, u32[]{:S(2)}) %collective-permute-start.2) | collective-permute-done | bytes 131104 | tf_op jit(solution)/shard_map/ppermute | solution.py:228
  72.0 0.0 collective-permute-done.1.low_ref
  72.0 1.9 %shard_map.51 = (bf16[1024,128]{1,0:T(8,128)(2,1)S(1)}, bf16[6,9,13,32,128]{4,3,2,1,0:T(8,128)(2,1)S(1)}) custom-call(s32[8,128]{1,0:T(8,128)S(1)} %get-tuple-element.19.shifts_ref, bf16[16,128,128]{2,1,0:T(8,128)(2,1)S(1)} %collective-permute-done.ops_ref, bf16[768,128]{1,0:T(8,128)(2,1)S(1)} %collective-permute-done.1.low_ref, ...), custom_call_target="tpu_custom_call", output_to_operand_aliasing={{1}: (4, {})} | custom-call | tf_op jit(solution)/shard_map/pallas_call | solution.py:234
  73.9 11.4 %all_to_all.27.parts_ref = bf16[8,128,128]{2,1,0:T(8,128)(2,1)S(1)} all-to-all(bf16[8,128,128]{2,1,0:T(8,128)(2,1)S(1)} %bitcast.21), channel_id=1, replica_groups=mesh['x'=4,'zh'=2,'y'=4,'c'=2,'zl'=8] {'y','c'}, dimensions={0} | all-to-all | bytes 524288 | tf_op jit(solution)/shard_map/all_to_all | solution.py:208
  85.2 0.3 shard_map.52
  85.5 41.5 %all_to_all.28 = bf16[512,2,128]{2,1,0:T(2,128)(2,1)S(1)} all-to-all(bf16[512,2,128]{2,1,0:T(2,128)(2,1)S(1)} %bitcast.19), channel_id=1, replica_groups=mesh['x'=4,'zh'=2,'y'=4,'c'=2,'zl'=8] {'x','y','c','zh','zl'}, dimensions={0} | all-to-all | bytes 524288 | tf_op jit(solution)/shard_map/all_to_all | solution.py:208
  127.0 0.8 shard_map.53
  (2 shorter events, 0.0 us)
Async XLA Ops:
  32.1 22.5 %all-to-all-start.1 = ((bf16[544,2,128]{2,1,0:T(2,128)(2,1)}), bf16[544,2,128]{2,1,0:T(2,128)(2,1)S(1)}, u32[]{:S(2)}, u32[]{:S(2)}) async-start(bf16[544,2,128]{2,1,0:T(2,128)(2,1)} %bitcast.5), calls=%async_computation.1 | async-start | bytes 557056 | tf_op jit(solution)/shard_map/all_to_all | solution.py:208
  45.4 23.9 %collective-permute-start = (bf16[16,128,128]{2,1,0:T(8,128)(2,1)}, bf16[16,128,128]{2,1,0:T(8,128)(2,1)S(1)}, u32[]{:S(2)}, u32[]{:S(2)}) collective-permute-start(bf16[16,128,128]{2,1,0:T(8,128)(2,1)} %param.6), channel_id=1, source_target_pairs={{0,0},{12,8},{17,16},{95,24},{34,32},{110,40},{51,48},{125,56},{1,... | collective-permute-start | bytes 1572872 | tf_op jit(solution)/shard_map/ppermute | solution.py:224
  64.0 8.0 %collective-permute-start.1 = (bf16[768,128]{1,0:T(8,128)(2,1)S(1)}, bf16[768,128]{1,0:T(8,128)(2,1)S(1)}, u32[]{:S(2)}, u32[]{:S(2)}) collective-permute-start(bf16[768,128]{1,0:T(8,128)(2,1)S(1)} %bitcast.23), channel_id=1, source_target_pairs={{0,128},{128,256},{256,384},{384,1},{1,129},{129,257},{257,385},{3... | collective-permute-start | bytes 589832 | tf_op jit(solution)/shard_map/ppermute | solution.py:227
  66.2 5.7 %collective-permute-start.2 = (bf16[512,128]{1,0:T(8,128)(2,1)S(1)}, bf16[512,128]{1,0:T(8,128)(2,1)S(1)}, u32[]{:S(2)}, u32[]{:S(2)}) collective-permute-start(bf16[512,128]{1,0:T(8,128)(2,1)S(1)} %bitcast.24), channel_id=1, source_target_pairs={{128,0},{256,128},{384,256},{1,384},{129,1},{257,129},{385,257},{2... | collective-permute-start | bytes 393224 | tf_op jit(solution)/shard_map/ppermute | solution.py:228
  67.5 1.0 copy-start
